TPU v7x, 512 devices: a whole 4x4x16 slice. The times are simulated.
512 devices in a mesh: member: 32 (over z_lo, x), tile: 16 (over z_hi, y, core).
Axes of the slice: x: 4, y: 4, z: 16 (z_hi: 2, z_lo: 8; z = z_hi * 8 + z_lo), core: 2. Of those that a mesh axis runs over, the one named last changes fastest.
Arguments:
- increment: bfloat16 [32, 64, 32, 1280], P('member', None, 'tile'), may hold values from -6 to 6
- courant_x: bfloat16 [64, 32, 1280], P(None, 'tile'), may hold values from 0.049804688 to 0.34960938
- courant_y: bfloat16 [64, 32, 1280], P(None, 'tile'), may hold values from 0.049804688 to 0.34960938
- diffusivity: float32 [64], replicated, may hold values from 0.01 to 0.07
- column_inverse: float32 [64, 64, 64], P('tile')
- jacobian: float32 [256, 64], replicated, may hold values from -0.75 to 0.75
- obs_cells: int32 [4, 4096], P(None, 'tile'), may hold values from 0 to 40959, as said below
- owner: int32 [4], replicated, may hold values from 0 to 31
- channel_mask: int32 [4, 256], replicated, may hold values 0 or 1
- departures: bfloat16 [32, 4, 256, 4096], P('member', None, None, 'tile'), may hold values from -6 to 6
Outputs:
- final_state: bfloat16 [32, 64, 32, 1280], P('member', None, 'tile')
- innovations: float32 [32, 4, 256, 4096], P('member', None, None, 'tile')
- perturbed: bfloat16 [32, 4, 256, 4096], P('member', None, None, 'tile')
Inputs may be any that keep to these rules, and one draw needn't show every extreme that they name: `obs_cells`: entry o of each slot names a cell in latitude rows 2 * (o // 256) to 2 * (o // 256) + 1, cells numbered row-major over the 32 x 1280 grid.
All inputs are finite; a program needn't handle non-finite values.
Results may differ from a plain program's by a relative error of at most 0.009.
Values may be sent and summed in bfloat16 or wider, within the bound.
No kernel may reach another device: no remote copies, remote signals or barrier semaphores. Data moves between devices by JAX's collectives and lax.ppermute only.
A program may use at most 64 MiB of HBM per device.

v0:
```python
import jax
import jax.numpy as jnp
from jax import lax
from jax.sharding import PartitionSpec as P

SLOTS = 4


def padded_2(block, sides, width):
    for axis, dim in sides:
        count = lax.axis_size(axis)
        forward = [(i, i + 1) for i in range(count - 1)]
        backward = [(target, source) for source, target in forward]
        low = lax.ppermute(
            lax.slice_in_dim(block, block.shape[dim] - width, None, axis=dim), axis, forward
        )
        high = lax.ppermute(lax.slice_in_dim(block, 0, width, axis=dim), axis, backward)
        block = jnp.concatenate([low, block, high], axis=dim)
    return block


def broadcast(value, axis, source):
    kept = jnp.where(lax.axis_index(axis) == source, value, 0).astype(value.dtype)
    return lax.psum(kept, axis)


def advance(state_field, padded, courant_east, courant_north, diffusivity):
    southern = padded[:, :-2]
    northern = padded[:, 2:]
    western = jnp.roll(state_field, 1, axis=2)
    eastern = jnp.roll(state_field, -1, axis=2)
    spread = diffusivity[:, None, None] * (
        eastern + western + northern + southern - 4.0 * state_field
    )
    return (
        state_field
        - courant_east * (state_field - western)
        - courant_north * (state_field - southern)
        + spread
    )


def vertical(state_field, inverse):
    level_count, row_count, lon_count = state_field.shape
    block_count = inverse.shape[0]
    grouped = state_field.reshape(level_count, row_count, block_count, lon_count // block_count)
    mixed = jnp.einsum("bkl,lybw->kybw", inverse, grouped, precision=lax.Precision.HIGHEST)
    return mixed.reshape(level_count, row_count, lon_count)


def local(
    increment,
    courant_x,
    courant_y,
    diffusivity,
    column_inverse,
    jacobian,
    obs_cells,
    owner,
    channel_mask,
    departures,
):
    state_field = increment[0].astype(jnp.float32)
    courant_east = courant_x.astype(jnp.float32)
    courant_north = courant_y.astype(jnp.float32)
    level_count, row_count, lon_count = state_field.shape
    offset = lax.axis_index("tile") * (row_count * lon_count)
    member_count = lax.axis_size("member")
    inverses_all = lax.all_gather(column_inverse, "tile", axis=0, tiled=True)
    modeled_list = []
    innovation_list = []
    for slot_index in range(SLOTS):
        padded = padded_2(state_field.astype(jnp.bfloat16), (("tile", 1),), 1).astype(
            state_field.dtype
        )
        state_field = advance(state_field, padded, courant_east, courant_north, diffusivity)
        state_field = vertical(state_field, inverses_all)
        columns_all = state_field.reshape(level_count, row_count * lon_count)
        picked = jnp.take(columns_all, obs_cells[slot_index] - offset, axis=1)
        modeled = jnp.dot(jacobian, picked, precision=lax.Precision.HIGHEST)
        owned = broadcast(departures[0, slot_index], "member", owner[slot_index]).astype(
            jnp.float32
        )
        summed = lax.psum(modeled.astype(jnp.bfloat16), "member").astype(jnp.float32)
        ensemble_mean = summed / member_count
        innovation_list.append(
            jnp.where(channel_mask[slot_index][:, None] == 1, owned - modeled, jnp.float32(0.0))
        )
        modeled_list.append((modeled - ensemble_mean).astype(jnp.bfloat16))
    final_state = state_field.astype(jnp.bfloat16)[None]
    innovations = jnp.stack(innovation_list)[None]
    perturbed = jnp.stack(modeled_list)[None]
    return (final_state, innovations, perturbed)


def solution(mesh):
    placed = (
        P("member", None, "tile", None),
        P(None, "tile", None),
        P(None, "tile", None),
        P(),
        P("tile", None, None),
        P(),
        P(None, "tile"),
        P(),
        P(),
        P("member", None, None, "tile"),
    )
    return jax.shard_map(
        local,
        mesh=mesh,
        in_specs=placed,
        out_specs=(
            P("member", None, "tile", None),
            P("member", None, None, "tile"),
            P("member", None, None, "tile"),
        ),
        check_vma=False,
    )
```

profile of v0, /device:TPU:24, one launch (start us, length us, event | category | flops | bytes accessed | tf_op | source)
XLA Modules:
  0.0 692.8 jit_solution(7631357054191573354)
XLA Ops:
  9.1 1.9 collective-permute-start
  11.0 3.6 collective-permute-start.1
  21.4 5.9 collective-permute-done.1
  28.6 81.5 %all-gather.2.cloned.1.call-done = f32[64,64,64]{2,1,0:T(8,128)} async-done(((f32[4,64,64]{2,1,0:T(8,128)}), f32[64,64,64]{2,1,0:T(8,128)}) %all-gather.2.cloned.1.call-update) | async-done | bytes 1048592 | tf_op jit(solution)/shard_map/all_gather | solution.py:69
  110.2 5.0 fusion.12
  115.2 1.8 copy.88
  117.0 1.6 copy.92
  121.1 2.1 collective-permute-start.2
  123.3 3.6 collective-permute-start.3
  126.9 2.0 gather_fusion
  130.3 1.3 fusion.32
  131.7 1.6 copy.98
  133.3 3.4 fusion.17
  136.7 1.8 copy.100
  139.7 1.5 copy.104
  142.5 2.4 reshape_reshape.13
  145.6 12.7 %collective-permute-start.4 = (bf16[64,1,1280]{2,0,1:T(8,128)(2,1)}, bf16[64,1,1280]{2,0,1:T(8,128)(2,1)}, u32[]{:S(2)}, u32[]{:S(2)}) collective-permute-start(bf16[64,1,1280]{2,0,1:T(8,128)(2,1)} %get-tuple-element.50), channel_id=1, source_target_pairs={{0,1},{1,2},{2,3},{3,4},{4,5},{5,6},{6,7},{7,8},{8,9},{9,10},{10,1... | collective-permute-start | bytes 491528 | tf_op jit(solution)/shard_map/ppermute | solution.py:14
  158.4 1.9 collective-permute-start.5
  160.3 2.0 gather_fusion.1
  164.8 1.3 fusion.35
  166.1 1.6 copy.110
  167.7 3.4 fusion.22
  171.1 1.8 copy.112
  174.1 1.5 copy.116
  177.0 2.4 reshape_reshape.14
  180.1 14.7 %collective-permute-start.6 = (bf16[64,1,1280]{2,0,1:T(8,128)(2,1)}, bf16[64,1,1280]{2,0,1:T(8,128)(2,1)}, u32[]{:S(2)}, u32[]{:S(2)}) collective-permute-start(bf16[64,1,1280]{2,0,1:T(8,128)(2,1)} %get-tuple-element.48), channel_id=1, source_target_pairs={{0,1},{1,2},{2,3},{3,4},{4,5},{5,6},{6,7},{7,8},{8,9},{9,10},{10,1... | collective-permute-start | bytes 491528 | tf_op jit(solution)/shard_map/ppermute | solution.py:14
  194.8 2.1 collective-permute-start.7
  196.9 2.0 gather_fusion.2
  202.7 1.6 copy.122
  204.3 3.4 fusion
  212.6 1.7 copy.134
  214.4 467.6 %all-reduce.3.cloned.1.call-done = (bf16[256,256]{0,1:T(8,128)(2,1)}, bf16[256,256]{0,1:T(8,128)(2,1)}, bf16[256,256]{0,1:T(8,128)(2,1)}, bf16[256,256]{0,1:T(8,...) async-done(((bf16[256,256]{0,1:T(8,128)(2,1)}, bf16[256,256]{0,1:T(8,128)(2,1)}, ...) | async-done | bytes 1048592 | tf_op jit(solution)/shard_map/psum | solution.py:24
  (135 shorter events, 32.4 us)
Async XLA Ops:
  7.2 121.7 %copy-start = (f32[256,64]{0,1:T(8,128)S(1)}, f32[256,64]{0,1:T(8,128)}, u32[]{:S(2)}) copy-start(f32[256,64]{0,1:T(8,128)} %param.17) | copy-start | bytes 196612
  7.2 7.5 %copy-start.28 = (s32[4,256]{1,0:T(4,128)S(1)}, s32[4,256]{1,0:T(4,128)}, u32[]{:S(2)}) copy-start(s32[4,256]{1,0:T(4,128)} %param.18) | copy-start | bytes 12292
  7.2 7.6 %copy-start.26 = (s32[4]{0:T(128)S(1)}, s32[4]{0:T(128)}, u32[]{:S(2)}) copy-start(s32[4]{0:T(128)} %param.19) | copy-start | bytes 52
  7.2 10.1 %copy-start.20 = (bf16[1,4,256,256]{3,2,1,0:T(8,128)(2,1)S(1)}, bf16[1,4,256,256]{3,2,1,0:T(8,128)(2,1)}, u32[]{:S(2)}) copy-start(bf16[1,4,256,256]{3,2,1,0:T(8,128)(2,1)} %param.21) | copy-start | bytes 1572868
  7.2 103.0 %all-gather.2.cloned.1.call-start = ((), (), s32[]{:S(2)}) async-start(), calls=%async_computation | async-start | bytes 2228224 | tf_op jit(solution)/shard_map/all_gather | solution.py:69
  7.9 674.1 %all-reduce.3.cloned.1.call-start = ((), (), s32[]{:S(2)}) async-start(), calls=%async_computation.1 | async-start | bytes 2097152 | tf_op jit(solution)/shard_map/psum | solution.py:24
  9.1 12.4 %collective-permute-start = (bf16[64,1,1280]{2,0,1:T(8,128)(2,1)S(1)}, bf16[64,1,1280]{2,0,1:T(8,128)(2,1)S(1)}, u32[]{:S(2)}, u32[]{:S(2)}) collective-permute-start(bf16[64,1,1280]{2,0,1:T(8,128)(2,1)S(1)} %get-tuple-element.56), channel_id=1, source_target_pairs={{0,1},{1,2},{2,3},{3,4},{4,5},{5,6},{6,7},{7,8},{8,9},{9,10},{10,1... | collective-permute-start | bytes 491528 | tf_op jit(solution)/shard_map/ppermute | solution.py:14
  11.0 16.4 %collective-permute-start.1 = (bf16[64,1,1280]{2,0,1:T(8,128)(2,1)S(1)}, bf16[64,1,1280]{2,0,1:T(8,128)(2,1)S(1)}, u32[]{:S(2)}, u32[]{:S(2)}) collective-permute-start(bf16[64,1,1280]{2,0,1:T(8,128)(2,1)S(1)} %get-tuple-element.57), channel_id=1, source_target_pairs={{1,0},{2,1},{3,2},{4,3},{5,4},{6,5},{7,6},{8,7},{9,8},{10,9},{11,1... | collective-permute-start | bytes 491528 | tf_op jit(solution)/shard_map/ppermute | solution.py:17
  21.4 6.1 copy-start.4
  21.4 6.1 copy-start.7
  21.4 6.1 copy-start.16
  21.4 6.1 copy-start.25
  121.1 9.1 %collective-permute-start.2 = (bf16[64,1,1280]{2,0,1:T(8,128)(2,1)S(1)}, bf16[64,1,1280]{2,0,1:T(8,128)(2,1)S(1)}, u32[]{:S(2)}, u32[]{:S(2)}) collective-permute-start(bf16[64,1,1280]{2,0,1:T(8,128)(2,1)S(1)} %get-tuple-element.52), channel_id=1, source_target_pairs={{0,1},{1,2},{2,3},{3,4},{4,5},{5,6},{6,7},{7,8},{8,9},{9,10},{10,1... | collective-permute-start | bytes 491528 | tf_op jit(solution)/shard_map/ppermute | solution.py:14
  123.3 6.9 %collective-permute-start.3 = (bf16[64,1,1280]{2,0,1:T(8,128)(2,1)S(1)}, bf16[64,1,1280]{2,0,1:T(8,128)(2,1)S(1)}, u32[]{:S(2)}, u32[]{:S(2)}) collective-permute-start(bf16[64,1,1280]{2,0,1:T(8,128)(2,1)S(1)} %get-tuple-element.53), channel_id=1, source_target_pairs={{1,0},{2,1},{3,2},{4,3},{5,4},{6,5},{7,6},{8,7},{9,8},{10,9},{11,1... | collective-permute-start | bytes 491528 | tf_op jit(solution)/shard_map/ppermute | solution.py:17
  130.3 2.9 copy-start.1
  145.6 18.0 %collective-permute-start.4 = (bf16[64,1,1280]{2,0,1:T(8,128)(2,1)}, bf16[64,1,1280]{2,0,1:T(8,128)(2,1)}, u32[]{:S(2)}, u32[]{:S(2)}) collective-permute-start(bf16[64,1,1280]{2,0,1:T(8,128)(2,1)} %get-tuple-element.50), channel_id=1, source_target_pairs={{0,1},{1,2},{2,3},{3,4},{4,5},{5,6},{6,7},{7,8},{8,9},{9,10},{10,1... | collective-permute-start | bytes 491528 | tf_op jit(solution)/shard_map/ppermute | solution.py:14
  158.4 5.3 collective-permute-start.5
  162.3 2.4 copy-start.5
  162.4 2.4 copy-start.8
  162.4 2.4 copy-start.12
  162.4 2.4 copy-start.13
  180.1 20.1 %collective-permute-start.6 = (bf16[64,1,1280]{2,0,1:T(8,128)(2,1)}, bf16[64,1,1280]{2,0,1:T(8,128)(2,1)}, u32[]{:S(2)}, u32[]{:S(2)}) collective-permute-start(bf16[64,1,1280]{2,0,1:T(8,128)(2,1)} %get-tuple-element.48), channel_id=1, source_target_pairs={{0,1},{1,2},{2,3},{3,4},{4,5},{5,6},{6,7},{7,8},{8,9},{9,10},{10,1... | collective-permute-start | bytes 491528 | tf_op jit(solution)/shard_map/ppermute | solution.py:14
  194.8 5.5 collective-permute-start.7
  199.0 2.4 copy-start.6
  199.0 2.4 copy-start.9
  199.0 2.4 copy-start.14
  199.0 2.4 copy-start.15
  209.1 1.9 copy-start.27
  209.1 1.9 copy-start.3
  211.5 470.5 %copy-start.19 = (f32[256,256]{0,1:T(8,128)S(1)}, f32[256,256]{0,1:T(8,128)}, u32[]{:S(2)}) copy-start(f32[256,256]{0,1:T(8,128)} %get-tuple-element.77) | copy-start | bytes 786436
  212.6 470.7 %copy-start.17 = (f32[256,256]{0,1:T(8,128)S(1)}, f32[256,256]{0,1:T(8,128)}, u32[]{:S(2)}) copy-start(f32[256,256]{0,1:T(8,128)} %get-tuple-element.81) | copy-start | bytes 786436
  212.6 470.7 %copy-start.18 = (f32[256,256]{0,1:T(8,128)S(1)}, f32[256,256]{0,1:T(8,128)}, u32[]{:S(2)}) copy-start(f32[256,256]{0,1:T(8,128)} %get-tuple-element.79) | copy-start | bytes 786436
  (7 other events, 9.3 us)
Sparse Core Ops, SparseCore 0:
  11.4 98.7 all-gather.1
  211.0 470.9 all-reduce.2
where the time goes:
time: 694 us; the launch traced here: 693 us
  waiting for transfers between devices  556 us (80%)
  local copies, waits for them, and re-layouts  44.8 us (6%)
  starting transfers between devices  42.8 us (6%)
  matrix products  19.7 us (3%)
  between operations  17.4 us (3%)
  other arithmetic  12.3 us (2%)
    psum x1, waiting for transfers between devices, broadcast(): return lax.psum(kept, axis)  468 us
    all_gather x1, waiting for transfers between devices, local(): inverses_all = lax.all_gather(column_inverse, 'tile', axis=0, tiled=True)  81.5 us
    ppermute x4, starting transfers between devices, padded_2(): lax.ppermute(lax.slice_in_dim(block, block.shape[dim] - width, None, axis...  31.4 us
    dot_general x4, matrix products, vertical(): jnp.einsum('bkl,lybw->kybw', inverse, grouped, precision=lax.Precision.HI...  15.1 us
  transfers between devices with their start and end apart: 10, of which 3 were waited for; matrix products, arithmetic and copies ran while one was open for 3% of the time, Pallas kernels for 0%

commit v1 on v0

v1 whole, which is shorter than its diff:
```python
import functools

import jax
import jax.numpy as jnp
from jax import lax
from jax.experimental import pallas as pl
from jax.experimental.pallas import tpu as pltpu
from jax.sharding import PartitionSpec as P

F32 = jnp.float32
BF16 = jnp.bfloat16
SLOTS = 4
LEV = 64
NX = 1280
WIDE = 20
LANES = 128
TILES = NX // LANES
OBS = 256
CH = 256
VMEM = pl.BlockSpec(memory_space=pltpu.VMEM)
SMEM = pl.BlockSpec(memory_space=pltpu.SMEM)


def split(value):
    high = value.astype(BF16)
    return high, (value - high.astype(F32)).astype(BF16)


def stacked(value):
    high, low = split(value)
    return jnp.concatenate([high, high, low, low], axis=0)


def horizontal(centre, south, north, east_number, north_number, spread):
    west = pltpu.roll(centre, 1, 1)
    east = pltpu.roll(centre, NX - 1, 1)
    return (
        centre
        - east_number * (centre - west)
        - north_number * (centre - south)
        + spread * (east + west + north + south - 4.0 * centre)
    )


def vertical(matrices, high, low, rows, store):
    width = len(rows) * LANES
    lane = lax.broadcasted_iota(jnp.int32, (LEV, width), 1) % LANES
    for tile in range(TILES):
        cut = slice(tile * LANES, (tile + 1) * LANES)
        upper = jnp.concatenate([high[row, :, cut] for row in rows], axis=1)
        lower = jnp.concatenate([low[row, :, cut] for row in rows], axis=1)
        right = jnp.concatenate([upper, upper, lower, lower], axis=0)
        first = tile * LANES // WIDE
        last = (tile * LANES + LANES - 1) // WIDE
        left = matrices[first * LEV : (last + 1) * LEV, :]
        left = jnp.concatenate([left, left], axis=1)
        mixed = jnp.dot(left, right, preferred_element_type=F32)
        out = mixed[:LEV]
        for block in range(first + 1, last + 1):
            at = (block - first) * LEV
            out = jnp.where(lane >= block * WIDE - tile * LANES, mixed[at : at + LEV], out)
        for place, row in enumerate(rows):
            store(row, cut, out[:, place * LANES : (place + 1) * LANES])


def pick(read, cells, out_ref, at):
    total = jnp.zeros((2 * LEV, OBS), F32)
    steps = NX // 256
    for chunk in range(2 * steps):
        row, start = chunk // steps, (chunk % steps) * 256
        left = jnp.concatenate(split(read(row, slice(start, start + 256))), axis=0)
        cell = lax.broadcasted_iota(jnp.int32, (256, OBS), 0) + chunk * 256
        chosen = jnp.where(cell == cells, 1.0, 0.0).astype(BF16)
        total = total + jnp.dot(left, chosen, preferred_element_type=F32)
    value = total[:LEV] + total[LEV:]
    out_ref[at : at + LEV, :] = value[:, :LANES]
    out_ref[at + LEV : at + 2 * LEV, :] = value[:, LANES:]


def first_kernel(
    place, own, south, north, spread_ref, near, far, cells,
    state_out, halo_out, picked_out, matrices_out,
    state, high, low,
):
    here = place[0]
    for core in range(2):
        piece = near if core == 0 else far
        for y in range(4):
            for z in range(2):
                tile = jnp.bitwise_xor(here & 9, 8 * z + core) + 2 * y
                at = pl.multiple_of(tile * 256, 256)
                matrices_out[pl.ds(at, 256), :] = piece[y, z * 256 : (z + 1) * 256, :]
    spread = spread_ref[...]
    low_keep = jnp.where(here == 0, 0.0, 1.0)
    high_keep = jnp.where(here == 15, 0.0, 1.0)
    line = [south[0], south[1], own[2], own[3], north[2], north[3]]
    east_of = [south[2], own[0], own[4], north[0]]
    north_of = [south[3], own[1], own[5], north[1]]
    line = [value.astype(F32) for value in line]
    for row in range(4):
        value = horizontal(
            line[row + 1], line[row], line[row + 2],
            east_of[row].astype(F32), north_of[row].astype(F32), spread,
        )
        if row == 0:
            value = value * low_keep
        if row == 3:
            value = value * high_keep
        high[row], low[row] = split(value)

    def keep(row, cut, value):
        state[row, :, cut] = value

    vertical(matrices_out, high, low, range(4), keep)
    pick(lambda row, cut: state[row + 1, :, cut], cells[0:1, :], picked_out, 0)
    for row in range(2):
        value = horizontal(
            state[row + 1], state[row], state[row + 2],
            east_of[row + 1].astype(F32), north_of[row + 1].astype(F32), spread,
        )
        high[row], low[row] = split(value)

    def give(row, cut, value):
        state_out[row, :, cut] = value
        halo_out[row, :, cut] = value.astype(BF16)

    vertical(matrices_out, high, low, range(2), give)
    pick(lambda row, cut: state_out[row, :, cut], cells[1:2, :], picked_out, 2 * LEV)


def second_kernel(
    place, own, south_of, north_of_tile, mid, south, north, spread_ref, matrices, cells,
    final_out, picked_out,
    state, high, low,
):
    here = place[0]
    spread = spread_ref[...]
    low_keep = jnp.where(here == 0, 0.0, 1.0)
    high_keep = jnp.where(here == 15, 0.0, 1.0)
    line = [south[0].astype(F32), south[1].astype(F32), mid[0], mid[1], north[0].astype(F32), north[1].astype(F32)]
    east_of = [south_of[2], own[0], own[4], north_of_tile[0]]
    north_of = [south_of[3], own[1], own[5], north_of_tile[1]]
    for row in range(4):
        value = horizontal(
            line[row + 1], line[row], line[row + 2],
            east_of[row].astype(F32), north_of[row].astype(F32), spread,
        )
        if row == 0:
            value = value * low_keep
        if row == 3:
            value = value * high_keep
        high[row], low[row] = split(value)

    def keep(row, cut, value):
        state[row, :, cut] = value

    vertical(matrices, high, low, range(4), keep)
    pick(lambda row, cut: state[row + 1, :, cut], cells[2:3, :], picked_out, 0)
    for row in range(2):
        value = horizontal(
            state[row + 1], state[row], state[row + 2],
            east_of[row + 1].astype(F32), north_of[row + 1].astype(F32), spread,
        )
        high[row], low[row] = split(value)

    def give(row, cut, value):
        state[row, :, cut] = value
        final_out[row, :, cut] = value.astype(BF16)

    vertical(matrices, high, low, range(2), give)
    pick(lambda row, cut: state[row, :, cut], cells[3:4, :], picked_out, 2 * LEV)


def operator(jacobian_ref):
    high, low = split(jacobian_ref[...])
    return jnp.concatenate([high, low, high, low], axis=1)


def innovations_kernel(jacobian_ref, early, late, owned, mask, out_ref):
    left = operator(jacobian_ref)
    for slot in range(SLOTS):
        picked = early if slot < 2 else late
        at = (slot % 2) * 2 * LEV
        right = jnp.concatenate([picked[at : at + LEV, :], picked[at + LEV : at + 2 * LEV, :]], axis=1)
        modeled = jnp.dot(left, stacked(right), preferred_element_type=F32)
        used = mask[:, slot : slot + 1] == 1
        out_ref[slot] = jnp.where(used, owned[slot].astype(F32) - modeled, 0.0)


def perturbed_kernel(jacobian_ref, early, late, mean, out_ref):
    left = operator(jacobian_ref)
    for slot in range(SLOTS):
        picked = early if slot < 2 else late
        at = (slot % 2) * 2 * LEV
        whole = slot * 2 * LEV
        right = jnp.concatenate(
            [
                picked[at + half : at + half + LEV, :] - mean[whole + half : whole + half + LEV, :].astype(F32)
                for half in (0, LEV)
            ],
            axis=1,
        )
        out_ref[slot] = jnp.dot(left, stacked(right), preferred_element_type=F32).astype(BF16)


def call(kernel, out_shape, in_specs, scratch=(), flops=0, traffic=0):
    return pl.pallas_call(
        kernel,
        out_shape=out_shape,
        in_specs=in_specs,
        out_specs=jax.tree.map(lambda _: VMEM, out_shape),
        scratch_shapes=list(scratch),
        compiler_params=pltpu.CompilerParams(vmem_limit_bytes=40 * 1024 * 1024),
        cost_estimate=pl.CostEstimate(flops=flops, bytes_accessed=traffic, transcendentals=0),
    )


def shape(*sizes, dtype=F32):
    return jax.ShapeDtypeStruct(sizes, dtype)


def gathered_from(value, axis, groups):
    count = len(groups[0])
    copies = jnp.broadcast_to(value[None], (count, *value.shape))
    return lax.all_to_all(copies, axis, 0, 0, tiled=True, axis_index_groups=groups)


def local(
    increment,
    courant_x,
    courant_y,
    diffusivity,
    column_inverse,
    jacobian,
    obs_cells,
    owner,
    channel_mask,
    departures,
):
    here = lax.axis_index("tile")
    member = lax.axis_index("member")
    place = jnp.reshape(here, (1,)).astype(jnp.int32)

    inverse = column_inverse.reshape(4 * LEV, LEV)
    upper = lax.reduce_precision(inverse, exponent_bits=8, mantissa_bits=7)
    halves = jnp.concatenate([upper.astype(BF16), (inverse - upper).astype(BF16)], axis=1)
    mirrored = [
        ((z * 4 + x) * 16 + tile, ((7 - z) * 4 + x) * 16 + (tile ^ 8))
        for z in range(8)
        for x in range(4)
        for tile in range(16)
    ]
    other = lax.ppermute(halves, ("member", "tile"), mirrored)
    pair = jnp.concatenate([halves, other], axis=0)
    y_groups = [[8 * z + 2 * y + core for y in range(4)] for z in range(2) for core in range(2)]
    near = gathered_from(pair, "tile", y_groups).reshape(4, 512, LANES)
    far = lax.ppermute(near, "tile", [(i, i ^ 1) for i in range(16)])

    rows_in = jnp.swapaxes(increment[0], 0, 1)
    x_rows = jnp.swapaxes(courant_x, 0, 1)
    y_rows = jnp.swapaxes(courant_y, 0, 1)
    own = jnp.concatenate([x_rows[:1], y_rows[:1], rows_in, x_rows[1:], y_rows[1:]], axis=0)
    forward = [(i, i + 1) for i in range(15)]
    backward = [(i + 1, i) for i in range(15)]
    south = lax.ppermute(own[2:], "tile", forward)
    north = lax.ppermute(own[:4], "tile", backward)

    order = [[(p % 8) * 4 + p // 8 for p in range(32)]]
    pieces = lax.all_to_all(
        departures.reshape(32, 32, OBS), "member", 0, 0, tiled=True, axis_index_groups=order
    ).reshape(32, 32, OBS)
    slot_owner = lax.dynamic_index_in_dim(owner, member % 4, keepdims=False)
    source = (slot_owner % 4) * 8 + slot_owner // 4
    kept = lax.dynamic_index_in_dim(pieces, source, keepdims=False)
    owned = gathered_from(kept, "member", order).reshape(SLOTS, CH, OBS)

    cells = obs_cells - here * (2 * NX)
    spread = jnp.broadcast_to(diffusivity[:, None], (LEV, NX))
    window = [
        pltpu.VMEM((4, LEV, NX), F32),
        pltpu.VMEM((4, LEV, NX), BF16),
        pltpu.VMEM((4, LEV, NX), BF16),
    ]
    mid, halo, early, matrices = call(
        first_kernel,
        (
            shape(2, LEV, NX),
            shape(2, LEV, NX, dtype=BF16),
            shape(4 * LEV, LANES),
            shape(64 * LEV, LANES, dtype=BF16),
        ),
        [SMEM] + [VMEM] * 7,
        window,
        flops=2_000_000_000,
        traffic=8_000_000,
    )(place, own, south, north, spread, near, far, cells)
    south_mid = lax.ppermute(halo, "tile", forward)
    north_mid = lax.ppermute(halo, "tile", backward)
    final, late = call(
        second_kernel,
        (shape(2, LEV, NX, dtype=BF16), shape(4 * LEV, LANES)),
        [SMEM] + [VMEM] * 9,
        window,
        flops=2_000_000_000,
        traffic=8_000_000,
    )(place, own, south, north, mid, south_mid, north_mid, spread, matrices, cells)

    both = jnp.concatenate([early, late], axis=0).astype(BF16).reshape(32, 16, LANES)
    members = [list(range(32))]
    parts = lax.all_to_all(both, "member", 0, 0, tiled=True, axis_index_groups=members).reshape(32, 16, LANES)
    share = (jnp.sum(parts.astype(F32), axis=0) / 32.0).astype(BF16)
    mean = gathered_from(share, "member", members).reshape(8 * LEV, LANES)

    innovations = call(
        innovations_kernel, shape(SLOTS, CH, OBS), [VMEM] * 5, flops=130_000_000, traffic=2_000_000
    )(jacobian, early, late, owned, channel_mask.T)
    perturbed = call(
        perturbed_kernel, shape(SLOTS, CH, OBS, dtype=BF16), [VMEM] * 4, flops=130_000_000, traffic=1_000_000
    )(jacobian, early, late, mean)
    final_state = jnp.swapaxes(final, 0, 1)[None]
    return final_state, innovations[None], perturbed[None]


def solution(mesh):
    placed = (
        P("member", None, "tile", None),
        P(None, "tile", None),
        P(None, "tile", None),
        P(),
        P("tile", None, None),
        P(),
        P(None, "tile"),
        P(),
        P(),
        P("member", None, None, "tile"),
    )
    return jax.shard_map(
        local,
        mesh=mesh,
        in_specs=placed,
        out_specs=(
            P("member", None, "tile", None),
            P("member", None, None, "tile"),
            P("member", None, None, "tile"),
        ),
        check_vma=False,
    )
```

time: 694 us -> 216 us (0.31)
  the two profiles are of different devices: /device:TPU:24 before, /device:TPU:25 now
where the time goes in v1:
time: 216 us; the launch traced here: 215 us
  waiting for transfers between devices  102 us (47%)
  starting transfers between devices  61.8 us (29%)
  blocking collectives  25 us (12%)
  Pallas kernels  12.3 us (6%)
  local copies, waits for them, and re-layouts  8.68 us (4%)
  between operations  3.58 us (2%)
    ppermute x1, waiting for transfers between devices, local(): other = lax.ppermute(halves, ('member', 'tile'), mirrored)  30.9 us
    all_to_all x3, waiting for transfers between devices, gathered_from(): lax.all_to_all(copies, axis, 0, 0, tiled=True, axis_index_groups=groups)  30.2 us
    all_to_all x1, blocking collectives, local(): lax.all_to_all(both, 'member', 0, 0, tiled=True, axis_index_groups=members)  25 us
    all_to_all x1, waiting for transfers between devices, local(): lax.all_to_all(departures.reshape(32, 32, OBS), 'member', 0, 0, tiled=Tru...  22.4 us
    all_to_all x3, starting transfers between devices, gathered_from(): lax.all_to_all(copies, axis, 0, 0, tiled=True, axis_index_groups=groups)  15.9 us
    ppermute x1, starting transfers between devices, local(): south = lax.ppermute(own[2:], 'tile', forward)  15.6 us
    ppermute x1, waiting for transfers between devices, local(): north_mid = lax.ppermute(halo, 'tile', backward)  15.3 us
    ppermute x1, starting transfers between devices, local(): far = lax.ppermute(near, 'tile', [(i, i ^ 1) for i in range(16)])  11.5 us
  transfers between devices with their start and end apart: 10, of which 8 were waited for; matrix products, arithmetic and copies ran while one was open for 1% of the time, Pallas kernels for 1%

profile of v1, /device:TPU:25, one launch (start us, length us, event | category | flops | bytes accessed | tf_op | source)
XLA Modules:
  0.0 215.2 jit_solution(2781216053181056790)
XLA Ops:
  0.6 1.0 copy.27
  1.7 0.9 copy-done.1
  2.7 0.9 copy-done
  3.7 1.2 pad_maximum_fusion.1
  4.9 15.6 %collective-permute-start = (bf16[4,64,1280]{2,1,0:T(8,128)(2,1)}, bf16[4,64,1280]{2,1,0:T(8,128)(2,1)S(1)}, u32[]{:S(2)}, u32[]{:S(2)}) collective-permute-start(bf16[4,64,1280]{2,1,0:T(8,128)(2,1)} %get-tuple-element.19), channel_id=1, source_target_pairs={{0,1},{1,2},{2,3},{3,4},{4,5},{5,6},{6,7},{7,8},{8,9},{9,10},{10,1... | collective-permute-start | bytes 1966088 | tf_op jit(solution)/shard_map/ppermute | solution.py:265
  20.6 1.9 collective-permute-start.1
  22.6 1.9 collective-permute-start.2
  24.6 30.9 %collective-permute-done.2 = bf16[256,128]{1,0:T(8,128)(2,1)S(1)} collective-permute-done((bf16[256,128]{1,0:T(8,128)(2,1)S(1)}, bf16[256,128]{1,0:T(8,128)(2,1)S(1)}, u32[]{:S(2)}, u32[]{:S(2)}) %collective-permute-start.2) | collective-permute-done | bytes 65568 | tf_op jit(solution)/shard_map/ppermute | solution.py:253
  55.6 0.9 broadcast_in_dim.17
  56.5 3.9 %all-to-all-start = ((bf16[4,512,128]{2,1,0:T(8,128)(2,1)}), bf16[4,512,128]{2,1,0:T(8,128)(2,1)S(1)}, u32[]{:S(2)}, u32[]{:S(2)}) async-start(bf16[4,512,128]{2,1,0:T(8,128)(2,1)} %broadcast_in_dim.17), calls=%async_computation | async-start | bytes 1048576 | tf_op jit(solution)/shard_map/all_to_all | solution.py:225
  60.4 5.1 %all-to-all-done.near = bf16[4,512,128]{2,1,0:T(8,128)(2,1)S(1)} async-done(((bf16[4,512,128]{2,1,0:T(8,128)(2,1)}), bf16[4,512,128]{2,1,0:T(8,128)(2,1)S(1)}, u32[]{:S(2)}, u32[]{:S(2)}) %all-to-all-start) | async-done | bytes 524320 | tf_op jit(solution)/shard_map/all_to_all | solution.py:225
  65.6 11.5 %collective-permute-start.3 = (bf16[4,512,128]{2,1,0:T(8,128)(2,1)S(1)}, bf16[4,512,128]{2,1,0:T(8,128)(2,1)S(1)}, u32[]{:S(2)}, u32[]{:S(2)}) collective-permute-start(bf16[4,512,128]{2,1,0:T(8,128)(2,1)S(1)} %all-to-all-done.near), channel_id=1, source_target_pairs={{0,1},{1,0},{2,3},{3,2},{4,5},{5,4},{6,7},{7,6},{8,9},{9,8},{10,11... | collective-permute-start | bytes 1572872 | tf_op jit(solution)/shard_map/ppermute | solution.py:257
  77.1 1.4 collective-permute-done.3.far
  78.7 5.0 %shard_map.121 = (f32[2,64,1280]{2,1,0:T(8,128)S(1)}, bf16[2,64,1280]{2,1,0:T(8,128)(2,1)S(1)}, f32[256,128]{1,0:T(8,128)S(1)}, bf16[4096,128]{1,0:T(8,128)(2,1)S(1)}) custom-call(s32[1]{0:T(128)} %bitcast.place, bf16[6,64,1280]{2,1,0:T(8,128)(2,1)S(1)} %constant_dynamic-update-slice_fusion.own, ...), custom_call_target="tpu_custom_call" | custom-call | flops 2000000000 | bytes 8000000 | tf_op jit(solution)/shard_map/pallas_call | solution.py:284
  83.7 4.0 %collective-permute-start.4 = (bf16[2,64,1280]{2,1,0:T(8,128)(2,1)S(1)}, bf16[2,64,1280]{2,1,0:T(8,128)(2,1)S(1)}, u32[]{:S(2)}, u32[]{:S(2)}) collective-permute-start(bf16[2,64,1280]{2,1,0:T(8,128)(2,1)S(1)} %get-tuple-element.10), channel_id=1, source_target_pairs={{0,1},{1,2},{2,3},{3,4},{4,5},{5,6},{6,7},{7,8},{8,9},{9,10},{10,1... | collective-permute-start | bytes 983048 | tf_op jit(solution)/shard_map/ppermute | solution.py:297
  87.7 1.9 collective-permute-start.5
  89.7 2.1 collective-permute-done.4.south
  91.7 15.3 %collective-permute-done.5.north = bf16[2,64,1280]{2,1,0:T(8,128)(2,1)S(1)} collective-permute-done((bf16[2,64,1280]{2,1,0:T(8,128)(2,1)S(1)}, bf16[2,64,1280]{2,1,0:T(8,128)(2,1)S(1)}, u32[]{:S(2)}, u32[]{:S(2)}) %collective-permute-start.5) | collective-permute-done | bytes 327712 | tf_op jit(solution)/shard_map/ppermute | solution.py:298
  107.0 4.9 %shard_map.122 = (bf16[2,64,1280]{2,1,0:T(8,128)(2,1)S(1)}, f32[256,128]{1,0:T(8,128)S(1)}) custom-call(s32[1]{0:T(128)} %bitcast.place, bf16[6,64,1280]{2,1,0:T(8,128)(2,1)S(1)} %constant_dynamic-update-slice_fusion.own, bf16[4,64,1280]{2,1,0:T(8,128)(2,1)S(1)} %collective-permute-done.south.south_of, ...), custom_call_target="tpu_custom_call" | custom-call | flops 2000000000 | bytes 8000000 | tf_op jit(solution)/shard_map/pallas_call | solution.py:299
  111.9 25.0 %all_to_all.25 = bf16[32,16,128]{2,1,0:T(8,128)(2,1)S(1)} all-to-all(bf16[32,16,128]{2,1,0:T(8,128)(2,1)S(1)} %bitcast.41), channel_id=1, replica_groups={{0,16,32,48,64,80,96,112,128,144,160,176,192,208,224,240,256,272,288,30..., dimensions={0} | all-to-all | bytes 262144 | tf_op jit(solution)/shard_map/all_to_all | solution.py:310
  136.9 9.1 %all-to-all-start.1 = ((bf16[32,32,256]{2,1,0:T(8,128)(2,1)}), bf16[32,32,256]{2,1,0:T(8,128)(2,1)S(1)}, u32[]{:S(2)}, u32[]{:S(2)}) async-start(bf16[32,32,256]{2,1,0:T(8,128)(2,1)} %bitcast.9), calls=%async_computation.1 | async-start | bytes 1048576 | tf_op jit(solution)/shard_map/all_to_all | solution.py:269
  146.0 22.4 %all-to-all-done.1 = bf16[32,32,256]{2,1,0:T(8,128)(2,1)S(1)} async-done(((bf16[32,32,256]{2,1,0:T(8,128)(2,1)}), bf16[32,32,256]{2,1,0:T(8,128)(2,1)S(1)}, u32[]{:S(2)}, u32[]{:S(2)}) %all-to-all-start.1) | async-done | bytes 524320 | tf_op jit(solution)/shard_map/all_to_all | solution.py:269
  168.4 0.7 broadcast_in_dim.41
  169.1 4.3 %all-to-all-start.4 = ((bf16[32,16,128]{2,1,0:T(8,128)(2,1)}), bf16[32,16,128]{2,1,0:T(8,128)(2,1)S(1)}, u32[]{:S(2)}, u32[]{:S(2)}) async-start(bf16[32,16,128]{2,1,0:T(8,128)(2,1)} %broadcast_in_dim.41), calls=%async_computation.4 | async-start | bytes 262144 | tf_op jit(solution)/shard_map/all_to_all | solution.py:225
  173.5 0.6 copy-done.7
  177.4 8.2 %all-to-all-done.4 = bf16[32,16,128]{2,1,0:T(8,128)(2,1)S(1)} async-done(((bf16[32,16,128]{2,1,0:T(8,128)(2,1)}), bf16[32,16,128]{2,1,0:T(8,128)(2,1)S(1)}, u32[]{:S(2)}, u32[]{:S(2)}) %all-to-all-start.4) | async-done | bytes 131104 | tf_op jit(solution)/shard_map/all_to_all | solution.py:225
  185.6 0.9 broadcast_in_dim.39
  186.4 7.6 %all-to-all-start.2 = ((bf16[32,32,256]{2,1,0:T(8,128)(2,1)}), bf16[32,32,256]{2,1,0:T(8,128)(2,1)S(1)}, u32[]{:S(2)}, u32[]{:S(2)}) async-start(bf16[32,32,256]{2,1,0:T(8,128)(2,1)} %broadcast_in_dim.39), calls=%async_computation.2 | async-start | bytes 1048576 | tf_op jit(solution)/shard_map/all_to_all | solution.py:225
  194.9 1.1 copy.19
  195.9 1.1 shard_map.124
  197.1 16.8 %all-to-all-done.2 = bf16[32,32,256]{2,1,0:T(8,128)(2,1)S(1)} async-done(((bf16[32,32,256]{2,1,0:T(8,128)(2,1)}), bf16[32,32,256]{2,1,0:T(8,128)(2,1)S(1)}, u32[]{:S(2)}, u32[]{:S(2)}) %all-to-all-start.2) | async-done | bytes 524320 | tf_op jit(solution)/shard_map/all_to_all | solution.py:225
  213.9 1.3 shard_map.123
  (36 shorter events, 2.0 us)
Async XLA Ops:
  1.6 1.0 copy-start.1
  2.6 1.0 copy-start
  3.7 18.8 %copy-start.2 = (f32[4,64,64]{2,1,0:T(8,128)S(1)}, f32[4,64,64]{2,1,0:T(8,128)}, u32[]{:S(2)}) copy-start(f32[4,64,64]{2,1,0:T(8,128)} %param.14) | copy-start | bytes 196612
  4.9 72.2 %collective-permute-start = (bf16[4,64,1280]{2,1,0:T(8,128)(2,1)}, bf16[4,64,1280]{2,1,0:T(8,128)(2,1)S(1)}, u32[]{:S(2)}, u32[]{:S(2)}) collective-permute-start(bf16[4,64,1280]{2,1,0:T(8,128)(2,1)} %get-tuple-element.19), channel_id=1, source_target_pairs={{0,1},{1,2},{2,3},{3,4},{4,5},{5,6},{6,7},{7,8},{8,9},{9,10},{10,1... | collective-permute-start | bytes 1966088 | tf_op jit(solution)/shard_map/ppermute | solution.py:265
  20.6 56.6 %collective-permute-start.1 = (bf16[4,64,1280]{2,1,0:T(8,128)(2,1)}, bf16[4,64,1280]{2,1,0:T(8,128)(2,1)}, u32[]{:S(2)}, u32[]{:S(2)}) collective-permute-start(bf16[4,64,1280]{2,1,0:T(8,128)(2,1)} %get-tuple-element.18), channel_id=1, source_target_pairs={{1,0},{2,1},{3,2},{4,3},{5,4},{6,5},{7,6},{8,7},{9,8},{10,9},{11,1... | collective-permute-start | bytes 1966088 | tf_op jit(solution)/shard_map/ppermute | solution.py:266
  22.6 32.9 %collective-permute-start.2 = (bf16[256,128]{1,0:T(8,128)(2,1)S(1)}, bf16[256,128]{1,0:T(8,128)(2,1)S(1)}, u32[]{:S(2)}, u32[]{:S(2)}) collective-permute-start(bf16[256,128]{1,0:T(8,128)(2,1)S(1)} %pad_maximum_fusion.4), channel_id=1, source_target_pairs={{0,456},{1,457},{2,458},{3,459},{4,460},{5,461},{6,462},{7,463},{8... | collective-permute-start | bytes 196616 | tf_op jit(solution)/shard_map/ppermute | solution.py:253
  56.5 9.1 %all-to-all-start = ((bf16[4,512,128]{2,1,0:T(8,128)(2,1)}), bf16[4,512,128]{2,1,0:T(8,128)(2,1)S(1)}, u32[]{:S(2)}, u32[]{:S(2)}) async-start(bf16[4,512,128]{2,1,0:T(8,128)(2,1)} %broadcast_in_dim.17), calls=%async_computation | async-start | bytes 1048576 | tf_op jit(solution)/shard_map/all_to_all | solution.py:225
  60.4 16.7 %copy-start.5 = (s32[4,256]{1,0:T(4,128)S(1)}, s32[4,256]{1,0:T(4,128)}, u32[]{:S(2)}) copy-start(s32[4,256]{1,0:T(4,128)} %param.16) | copy-start | bytes 12292
  65.6 13.0 %collective-permute-start.3 = (bf16[4,512,128]{2,1,0:T(8,128)(2,1)S(1)}, bf16[4,512,128]{2,1,0:T(8,128)(2,1)S(1)}, u32[]{:S(2)}, u32[]{:S(2)}) collective-permute-start(bf16[4,512,128]{2,1,0:T(8,128)(2,1)S(1)} %all-to-all-done.near), channel_id=1, source_target_pairs={{0,1},{1,0},{2,3},{3,2},{4,5},{5,4},{6,7},{7,6},{8,9},{9,8},{10,11... | collective-permute-start | bytes 1572872 | tf_op jit(solution)/shard_map/ppermute | solution.py:257
  77.1 1.5 copy-start.6
  83.7 8.0 %collective-permute-start.4 = (bf16[2,64,1280]{2,1,0:T(8,128)(2,1)S(1)}, bf16[2,64,1280]{2,1,0:T(8,128)(2,1)S(1)}, u32[]{:S(2)}, u32[]{:S(2)}) collective-permute-start(bf16[2,64,1280]{2,1,0:T(8,128)(2,1)S(1)} %get-tuple-element.10), channel_id=1, source_target_pairs={{0,1},{1,2},{2,3},{3,4},{4,5},{5,6},{6,7},{7,8},{8,9},{9,10},{10,1... | collective-permute-start | bytes 983048 | tf_op jit(solution)/shard_map/ppermute | solution.py:297
  87.7 19.3 %collective-permute-start.5 = (bf16[2,64,1280]{2,1,0:T(8,128)(2,1)S(1)}, bf16[2,64,1280]{2,1,0:T(8,128)(2,1)S(1)}, u32[]{:S(2)}, u32[]{:S(2)}) collective-permute-start(bf16[2,64,1280]{2,1,0:T(8,128)(2,1)S(1)} %get-tuple-element.10), channel_id=1, source_target_pairs={{1,0},{2,1},{3,2},{4,3},{5,4},{6,5},{7,6},{8,7},{9,8},{10,9},{11,1... | collective-permute-start | bytes 983048 | tf_op jit(solution)/shard_map/ppermute | solution.py:298
  136.9 31.5 %all-to-all-start.1 = ((bf16[32,32,256]{2,1,0:T(8,128)(2,1)}), bf16[32,32,256]{2,1,0:T(8,128)(2,1)S(1)}, u32[]{:S(2)}, u32[]{:S(2)}) async-start(bf16[32,32,256]{2,1,0:T(8,128)(2,1)} %bitcast.9), calls=%async_computation.1 | async-start | bytes 1048576 | tf_op jit(solution)/shard_map/all_to_all | solution.py:269
  169.1 16.5 %all-to-all-start.4 = ((bf16[32,16,128]{2,1,0:T(8,128)(2,1)}), bf16[32,16,128]{2,1,0:T(8,128)(2,1)S(1)}, u32[]{:S(2)}, u32[]{:S(2)}) async-start(bf16[32,16,128]{2,1,0:T(8,128)(2,1)} %broadcast_in_dim.41), calls=%async_computation.4 | async-start | bytes 262144 | tf_op jit(solution)/shard_map/all_to_all | solution.py:225
  173.5 0.7 copy-start.7
  186.4 7.6 %copy-start.3 = (f32[256,64]{0,1:T(8,128)S(1)}, f32[256,64]{0,1:T(8,128)}, u32[]{:S(2)}) copy-start(f32[256,64]{0,1:T(8,128)} %param.15) | copy-start | bytes 196612
  186.4 27.4 %all-to-all-start.2 = ((bf16[32,32,256]{2,1,0:T(8,128)(2,1)}), bf16[32,32,256]{2,1,0:T(8,128)(2,1)S(1)}, u32[]{:S(2)}, u32[]{:S(2)}) async-start(bf16[32,32,256]{2,1,0:T(8,128)(2,1)} %broadcast_in_dim.39), calls=%async_computation.2 | async-start | bytes 1048576 | tf_op jit(solution)/shard_map/all_to_all | solution.py:225
  194.0 0.7 copy-start.4

commit v2 on v1

v2 whole, which is shorter than its diff:
```python
import jax
import jax.numpy as jnp
import numpy as np
from jax import lax
from jax.experimental import pallas as pl
from jax.experimental.pallas import tpu as pltpu
from jax.sharding import PartitionSpec as P

F32 = jnp.float32
BF16 = jnp.bfloat16
SLOTS = 4
LEV = 64
NX = 1280
WIDE = 20
LANES = 128
TILES = NX // LANES
OBS = 256
CH = 256
VMEM = pl.BlockSpec(memory_space=pltpu.VMEM)
SMEM = pl.BlockSpec(memory_space=pltpu.SMEM)
ANY = pl.BlockSpec(memory_space=pl.ANY)


def split(value):
    high = value.astype(BF16)
    return high, (value - high.astype(F32)).astype(BF16)


def stacked(value):
    high, low = split(value)
    return jnp.concatenate([high, high, low, low], axis=0)


def vertical(matrices, even, odd, rows, store):
    width = len(rows) * LANES
    lane = lax.broadcasted_iota(jnp.int32, (LEV, width), 1) % LANES
    for tile in range(TILES):
        cut = slice(tile * LANES, (tile + 1) * LANES)
        upper = jnp.concatenate([even[row, :, cut] for row in rows], axis=1)
        lower = jnp.concatenate([odd[row, :, cut] for row in rows], axis=1)
        right = jnp.concatenate([upper, upper, lower, lower], axis=0)
        first = tile * LANES // (2 * WIDE)
        last = (tile * LANES + LANES - 1) // (2 * WIDE)
        mixed = jnp.dot(
            matrices[first * LEV : (last + 1) * LEV, :], right, preferred_element_type=F32
        )
        out = mixed[:LEV]
        for pair in range(first + 1, last + 1):
            at = (pair - first) * LEV
            out = jnp.where(lane >= pair * 2 * WIDE - tile * LANES, mixed[at : at + LEV], out)
        for place, row in enumerate(rows):
            store(row, cut, out[:, place * LANES : (place + 1) * LANES])


def pick(read, cells, out_ref, at):
    total = jnp.zeros((2 * LEV, OBS), F32)
    steps = NX // 256
    for chunk in range(2 * steps):
        row, start = chunk // steps, (chunk % steps) * 256
        left = jnp.concatenate(split(read(row, slice(start, start + 256))), axis=0)
        cell = lax.broadcasted_iota(jnp.int32, (256, OBS), 0) + chunk * 256
        chosen = jnp.where(cell == cells, 1.0, 0.0).astype(BF16)
        total = total + jnp.dot(left, chosen, preferred_element_type=F32)
    value = total[:LEV] + total[LEV:]
    out_ref[at : at + LEV, :] = value[:, :LANES]
    out_ref[at + LEV : at + 2 * LEV, :] = value[:, LANES:]


def fetch(sem, target, source, far=None, over=None):
    if far is None:
        pltpu.make_async_copy(source, target, sem).start()
    else:

        @pl.when(jnp.logical_not(far))
        def _():
            pltpu.make_async_copy(source, target, sem).start()

        @pl.when(far)
        def _():
            pltpu.make_async_copy(over, target, sem).start()

    return pltpu.make_async_copy(source, target, sem)


def fetch_matrices(here, near, other_core, matrices, sems):
    blocks = []
    for core in range(2):
        piece = near if core == 0 else other_core
        for y in range(4):
            for z in range(2):
                tile = jnp.bitwise_xor(here & 9, 8 * z + core) + 2 * y
                at = pl.multiple_of(tile * LANES, LANES)
                blocks.append(
                    fetch(
                        sems.at[len(blocks)],
                        matrices.at[pl.ds(at, LANES), :],
                        piece.at[y, pl.ds(z * LANES, LANES), :],
                    )
                )
    return blocks


def fetch_numbers(here, numbers, own, south, north, beyond, sems):
    two = pl.ds(2, 2)
    first = pl.ds(0, 2)
    return [
        fetch(sems.at[0], numbers.at[0], south.at[two], here == 8, beyond.at[two]),
        fetch(sems.at[1], numbers.at[1], own.at[first]),
        fetch(sems.at[2], numbers.at[2], own.at[pl.ds(4, 2)]),
        fetch(sems.at[3], numbers.at[3], north.at[first], here == 7, beyond.at[first]),
    ]


def column_of(row_ref):
    diagonal = lax.broadcasted_iota(jnp.int32, (LEV, LEV), 0) == lax.broadcasted_iota(jnp.int32, (LEV, LEV), 1)
    return jnp.sum(jnp.where(diagonal, row_ref[...], 0.0), axis=1, keepdims=True)


def two_slots(here, line, numbers, spread, evens, matrices, blocks, parts, state, even, odd, stored, first_done):
    centre_part, east_part, north_part = parts
    for row in range(4):
        cross = numbers[row, 0].astype(F32) + spread
        along = numbers[row, 1].astype(F32) + spread
        east_part[row] = cross
        north_part[row] = along
        centre_part[row] = 1.0 - 2.0 * spread - cross - along
    for slot in range(2):
        count = 4 - 2 * slot
        for row in range(count):
            at = slot + row
            if slot == 0:
                low, mid, high = line(row), line(row + 1), line(row + 2)
            else:
                low, mid, high = state[row], state[row + 1], state[row + 2]
            west = pltpu.roll(mid, 1, 1)
            east = pltpu.roll(mid, NX - 1, 1)
            value = (
                centre_part[at] * mid
                + east_part[at] * west
                + north_part[at] * low
                + spread * (east + high)
            )
            if count == 4 and row == 0:
                value = value * jnp.where(here == 0, 0.0, 1.0)
            if count == 4 and row == 3:
                value = value * jnp.where(here == 15, 0.0, 1.0)
            value = value.astype(BF16)
            masked = value * evens
            even[row] = masked
            odd[row] = value - masked
        if slot == 0:
            for block in blocks:
                block.wait()

            def keep(row, cut, value):
                state[row, :, cut] = value

            vertical(matrices, even, odd, range(4), keep)
            first_done()
        else:
            vertical(matrices, even, odd, range(2), stored)


def first_kernel(
    place, own, south, north, beyond, near, far, spread_ref, evens,
    states_out, halo_out,
    rows, numbers, matrices, centre_part, east_part, north_part, state, later, even, odd, sems,
):
    here = place[0]
    two = pl.ds(2, 2)
    first = pl.ds(0, 2)
    loads = [
        fetch(sems.at[0], rows.at[first], south.at[first], here == 8, beyond.at[first]),
        fetch(sems.at[1], rows.at[two], own.at[two]),
        fetch(sems.at[2], rows.at[pl.ds(4, 2)], north.at[two], here == 7, beyond.at[two]),
    ]
    loads += fetch_numbers(here, numbers, own, south, north, beyond, sems.at[pl.ds(3, 4)])
    blocks = fetch_matrices(here, near, far, matrices, sems.at[pl.ds(7, 16)])
    for load in loads:
        load.wait()
    stores = [
        pltpu.make_async_copy(state.at[pl.ds(1, 2)], states_out.at[first], sems.at[0]),
        pltpu.make_async_copy(later, states_out.at[two], sems.at[1]),
    ]

    def stored(row, cut, value):
        later[row, :, cut] = value
        halo_out[row, :, cut] = value.astype(BF16)

    two_slots(
        here, lambda row: rows[row].astype(F32), numbers, column_of(spread_ref), jnp.concatenate([evens[...]] * 4, axis=0), matrices, blocks,
        (centre_part, east_part, north_part), state, even, odd, stored, stores[0].start,
    )
    stores[1].start()
    for store in stores:
        store.wait()


def second_kernel(
    place, own, south, north, beyond, near, far, spread_ref, evens,
    states, south_mid, north_mid, beyond_mid, cells,
    final_out, picked_out,
    mid, sides, numbers, matrices, centre_part, east_part, north_part, state, even, odd, sems,
):
    here = place[0]
    first = pl.ds(0, 2)
    loads = [
        fetch(sems.at[0], mid, states.at[pl.ds(2, 2)]),
        fetch(sems.at[1], sides.at[first], south_mid, here == 8, beyond_mid),
        fetch(sems.at[2], sides.at[pl.ds(2, 2)], north_mid, here == 7, beyond_mid),
    ]
    loads += fetch_numbers(here, numbers, own, south, north, beyond, sems.at[pl.ds(3, 4)])
    blocks = fetch_matrices(here, near, far, matrices, sems.at[pl.ds(7, 16)])
    for load in loads:
        load.wait()

    def line(row):
        if 2 <= row < 4:
            return mid[row - 2]
        return sides[row if row < 2 else row - 2].astype(F32)

    def first_done():
        pick(lambda row, cut: state[row + 1, :, cut], cells[2:3, :], picked_out, 0)

    def stored(row, cut, value):
        mid[row, :, cut] = value
        final_out[row, :, cut] = value.astype(BF16)

    two_slots(
        here, line, numbers, column_of(spread_ref), jnp.concatenate([evens[...]] * 4, axis=0), matrices, blocks,
        (centre_part, east_part, north_part), state, even, odd, stored, first_done,
    )
    pick(lambda row, cut: mid[row, :, cut], cells[3:4, :], picked_out, 2 * LEV)


def early_kernel(states, cells, picked_out):
    pick(lambda row, cut: states[row, :, cut], cells[0:1, :], picked_out, 0)
    pick(lambda row, cut: states[row + 2, :, cut], cells[1:2, :], picked_out, 2 * LEV)


def operator(jacobian_ref):
    high, low = split(jacobian_ref[...])
    return jnp.concatenate([high, low, high, low], axis=1)


def innovations_kernel(jacobian_ref, early, late, owned, mask, out_ref):
    left = operator(jacobian_ref)
    for slot in range(SLOTS):
        picked = early if slot < 2 else late
        at = slot % 2 * 2 * LEV
        right = jnp.concatenate([picked[at : at + LEV, :], picked[at + LEV : at + 2 * LEV, :]], axis=1)
        modeled = jnp.dot(left, stacked(right), preferred_element_type=F32)
        used = mask[:, slot : slot + 1] == 1
        out_ref[slot] = jnp.where(used, owned[slot].astype(F32) - modeled, 0.0)


def perturbed_kernel(jacobian_ref, early, late, mean, out_ref):
    left = operator(jacobian_ref)
    for slot in range(SLOTS):
        picked = early if slot < 2 else late
        at = slot % 2 * 2 * LEV
        whole = slot * 2 * LEV
        right = jnp.concatenate(
            [
                picked[at + half : at + half + LEV, :] - mean[whole + half : whole + half + LEV, :].astype(F32)
                for half in (0, LEV)
            ],
            axis=1,
        )
        out_ref[slot] = jnp.dot(left, stacked(right), preferred_element_type=F32).astype(BF16)


def call(kernel, out_shape, in_specs, scratch=(), flops=0, traffic=0, limit=16 * 1024 * 1024, out_specs=None):
    return pl.pallas_call(
        kernel,
        out_shape=out_shape,
        in_specs=in_specs,
        out_specs=jax.tree.map(lambda _: VMEM, out_shape) if out_specs is None else out_specs,
        scratch_shapes=list(scratch),
        compiler_params=pltpu.CompilerParams(vmem_limit_bytes=limit),
        cost_estimate=pl.CostEstimate(flops=flops, bytes_accessed=traffic, transcendentals=0),
    )


def shape(*sizes, dtype=F32):
    return jax.ShapeDtypeStruct(sizes, dtype)


def share_kernel(parts, out_ref):
    total = parts[0].astype(F32)
    for member in range(1, 32):
        total = total + parts[member].astype(F32)
    share = (total * (1.0 / 32.0)).astype(BF16)
    for member in range(32):
        out_ref[member] = share


def gathered_from(value, axis, groups):
    count = len(groups[0])
    copies = jnp.broadcast_to(value[None], (count, *value.shape))
    return lax.all_to_all(copies, axis, 0, 0, tiled=True, axis_index_groups=groups)


AXES = ("member", "tile")
Z_GROUPS = [[4 * z + x for z in range(8)] for x in range(4)]
X_GROUPS = [[4 * z + x for x in range(4)] for z in range(8)]


def device(z, x, y, core):
    return ((z % 8) * 4 + x) * 16 + (z // 8 % 2) * 8 + y * 2 + core


def over_the_gap():
    apart, across = [], []
    for z in range(8):
        for x in range(4):
            column, back = z % 4, 1 if z >= 4 else 0
            low, high = device(z, x, 3, 1), device(z + 8, x, 0, 0)
            up, down = device(z - back, x, column, 0), device(z + 8 - back, x, column, 1)
            apart += [(low, up), (high, down)]
            across += [(up, high), (down, low)]
    return apart, across


def local(
    increment,
    courant_x,
    courant_y,
    diffusivity,
    column_inverse,
    jacobian,
    obs_cells,
    owner,
    channel_mask,
    departures,
):
    here = lax.axis_index("tile")
    member = lax.axis_index("member")
    place = jnp.reshape(here, (1,)).astype(jnp.int32)

    inverse = column_inverse.reshape(2, 2, LEV, LEV)
    upper = lax.reduce_precision(inverse, exponent_bits=8, mantissa_bits=7)
    halves = jnp.concatenate([upper.astype(BF16), (inverse - upper).astype(BF16)], axis=3)
    halves = jnp.concatenate([halves[:, 0], halves[:, 1]], axis=2).reshape(2 * LEV, 4 * LEV)
    mirrored = [
        (device(z, x, y, core), device(15 - z, x, y, core))
        for z in range(16)
        for x in range(4)
        for y in range(4)
        for core in range(2)
    ]
    other = lax.ppermute(halves, AXES, mirrored)
    increment, courant_x, courant_y, _ = lax.optimization_barrier((increment, courant_x, courant_y, halves))
    rows_in = jnp.swapaxes(increment[0], 0, 1)
    x_rows = jnp.swapaxes(courant_x, 0, 1)
    y_rows = jnp.swapaxes(courant_y, 0, 1)
    own = jnp.concatenate([x_rows[:1], y_rows[:1], rows_in, x_rows[1:], y_rows[1:]], axis=0)
    apart, across = over_the_gap()
    halfway = lax.ppermute(lax.dynamic_slice_in_dim(own, jnp.where(here == 8, 0, 2), 4), AXES, apart)
    departures, _ = lax.optimization_barrier((departures, own))
    slot_owner = lax.dynamic_index_in_dim(owner, member % 4, keepdims=False)
    offered = lax.all_to_all(departures[0], "member", 0, 0, tiled=True, axis_index_groups=X_GROUPS)
    halfway, other, offered, own = lax.optimization_barrier((halfway, other, offered, own))

    beyond = lax.ppermute(halfway, AXES, across)
    pair = jnp.concatenate([halves, other], axis=0)
    y_groups = [[8 * z + 2 * y + core for y in range(4)] for z in range(2) for core in range(2)]
    near = gathered_from(pair, "tile", y_groups).reshape(4, 4 * LEV, 4 * LEV)
    chosen = lax.dynamic_index_in_dim(offered, slot_owner % 4, keepdims=False)
    chosen, _ = lax.optimization_barrier((chosen, near))
    pieces = lax.all_to_all(chosen.reshape(8, 32, OBS), "member", 0, 0, tiled=True, axis_index_groups=Z_GROUPS)
    forward = [(i, i + 1) for i in range(15) if i != 7]
    backward = [(i + 1, i) for i in range(15) if i != 7]
    south = lax.ppermute(own[2:], "tile", forward)
    north = lax.ppermute(own[:4], "tile", backward)
    far = lax.ppermute(near, "tile", [(i, i ^ 1) for i in range(16)])

    cells = obs_cells - here * (2 * NX)
    spread = diffusivity.reshape(1, LEV)
    evens = np.broadcast_to((np.arange(NX) // WIDE % 2 == 0), (16, NX)).astype(BF16)
    fields = [own, south, north, beyond, near, far]
    window = [
        pltpu.VMEM((4, 2, LEV, NX), BF16),
        pltpu.VMEM((32 * LEV, 4 * LEV), BF16),
        pltpu.VMEM((4, LEV, NX), F32),
        pltpu.VMEM((4, LEV, NX), F32),
        pltpu.VMEM((4, LEV, NX), F32),
        pltpu.VMEM((4, LEV, NX), F32),
    ]
    masks = [
        pltpu.VMEM((4, LEV, NX), BF16),
        pltpu.VMEM((4, LEV, NX), BF16),
        pltpu.SemaphoreType.DMA((23,)),
    ]
    states, halo = call(
        first_kernel,
        (shape(4, LEV, NX), shape(2, LEV, NX, dtype=BF16)),
        [SMEM] + [ANY] * 6 + [VMEM] * 2,
        [pltpu.VMEM((6, LEV, NX), BF16), *window, pltpu.VMEM((2, LEV, NX), F32), *masks],
        flops=2_000_000_000,
        limit=56 * 1024 * 1024,
        out_specs=(ANY, VMEM),
    )(place, *fields, spread, evens)

    halfway_mid = lax.ppermute(halo, AXES, apart)
    pieces, halfway_mid = lax.optimization_barrier((pieces, halfway_mid))
    kept = lax.dynamic_index_in_dim(pieces, slot_owner // 4, keepdims=False)
    south_mid = lax.ppermute(halo, "tile", forward)
    north_mid = lax.ppermute(halo, "tile", backward)
    beyond_mid = lax.ppermute(halfway_mid, AXES, across)
    early = call(early_kernel, shape(4 * LEV, LANES), [VMEM] * 2, flops=200_000_000, traffic=2_000_000)(states, cells)
    whole = gathered_from(kept, "member", Z_GROUPS).reshape(CH, OBS)
    whole, beyond_mid = lax.optimization_barrier((whole, beyond_mid))
    owned = gathered_from(whole, "member", X_GROUPS).reshape(SLOTS, CH, OBS)
    final, late = call(
        second_kernel,
        (shape(2, LEV, NX, dtype=BF16), shape(4 * LEV, LANES)),
        [SMEM] + [ANY] * 6 + [VMEM] * 2 + [ANY] * 4 + [VMEM],
        [pltpu.VMEM((2, LEV, NX), F32), pltpu.VMEM((4, LEV, NX), BF16), *window, *masks],
        flops=2_000_000_000,
        traffic=8_000_000,
        limit=56 * 1024 * 1024,
    )(place, *fields, spread, evens, states, south_mid, north_mid, beyond_mid, cells)

    both = jnp.concatenate([early, late], axis=0).astype(BF16).reshape(32, 16, LANES)
    both, owned = lax.optimization_barrier((both, owned))
    members = [list(range(32))]
    parts = lax.all_to_all(both, "member", 0, 0, tiled=True, axis_index_groups=members).reshape(32, 16, LANES)
    shares = call(share_kernel, shape(32, 16, LANES, dtype=BF16), [VMEM], flops=70_000, traffic=300_000)(parts)
    mean = lax.all_to_all(shares, "member", 0, 0, tiled=True, axis_index_groups=members).reshape(8 * LEV, LANES)
    innovations = call(
        innovations_kernel, shape(SLOTS, CH, OBS), [VMEM] * 5, flops=130_000_000, traffic=2_000_000
    )(jacobian, early, late, owned, channel_mask.T)
    perturbed = call(
        perturbed_kernel, shape(SLOTS, CH, OBS, dtype=BF16), [VMEM] * 4, flops=130_000_000, traffic=1_000_000
    )(jacobian, early, late, mean)
    final_state = jnp.swapaxes(final, 0, 1)[None]
    return final_state, innovations[None], perturbed[None]


def solution(mesh):
    placed = (
        P("member", None, "tile", None),
        P(None, "tile", None),
        P(None, "tile", None),
        P(),
        P("tile", None, None),
        P(),
        P(None, "tile"),
        P(),
        P(),
        P("member", None, None, "tile"),
    )
    return jax.shard_map(
        local,
        mesh=mesh,
        in_specs=placed,
        out_specs=(
            P("member", None, "tile", None),
            P("member", None, None, "tile"),
            P("member", None, None, "tile"),
        ),
        check_vma=False,
    )
```

time: 216 us -> 164 us (0.76)
  waiting for transfers between devices: 102 us -> 35.9 us
  starting transfers between devices: 61.8 us -> 71.4 us
  Pallas kernels: 12.3 us -> 17.3 us
    all_to_all x3, waiting for transfers between devices: 30.2 us -> 0.01 us  [gathered_from(): lax.all_to_all(copies, axis, 0, 0, tiled=True, axis_index_groups=groups)]
    ppermute x1, waiting for transfers between devices: 15.3 us -> 0.01 us  [local(): north_mid = lax.ppermute(halo, 'tile', backward)]
    ppermute x1 -> x5, starting transfers between devices: 1.92 us -> 17.2 us  [the longest x1 8.64 us: local(): lax.ppermute(lax.dynamic_slice_in_dim(own, jnp.where(here == 8, 0, 2), 4)...]
    ppermute x1, starting transfers between devices: 15.6 us -> 1.29 us  [local(): south = lax.ppermute(own[2:], 'tile', forward)]
    all_to_all x1 -> x3, starting transfers between devices: 9.05 us -> 19.4 us  [the longest x1 11.7 us: local(): lax.all_to_all(chosen.reshape(8, 32, OBS), 'member', 0, 0, tiled=True, ax...]
    all_to_all x1 -> x3, waiting for transfers between devices: 22.4 us -> 12.4 us  [the longest x1 9.45 us: local(): lax.all_to_all(shares, 'member', 0, 0, tiled=True, axis_index_groups=memb...]
    ppermute x1, starting transfers between devices: 11.5 us -> 3.03 us  [local(): far = lax.ppermute(near, 'tile', [(i, i ^ 1) for i in range(16)])]
    ppermute x1 -> x5, waiting for transfers between devices: 30.9 us -> 23.4 us  [the longest x1 13 us: local(): beyond_mid = lax.ppermute(halfway_mid, AXES, across)]
  transfers between devices with their start and end apart: 10 -> 16, of which waited for: 8 -> 6; matrix products, arithmetic and copies ran while one was open for 1% -> 3% of each run, Pallas kernels for 1% -> 9%
where the time goes in v2:
time: 164 us; the launch traced here: 163 us
  starting transfers between devices  71.4 us (44%)
  waiting for transfers between devices  35.9 us (22%)
  blocking collectives  24.9 us (15%)
  Pallas kernels  17.3 us (11%)
  local copies, waits for them, and re-layouts  7.76 us (5%)
  between operations  3.69 us (2%)
  other arithmetic  2.11 us (1%)
    all_to_all x1, blocking collectives, local(): lax.all_to_all(both, 'member', 0, 0, tiled=True, axis_index_groups=members)  24.9 us
    all_to_all x3, starting transfers between devices, gathered_from(): lax.all_to_all(copies, axis, 0, 0, tiled=True, axis_index_groups=groups)  20.5 us
    ppermute x1, waiting for transfers between devices, local(): beyond_mid = lax.ppermute(halfway_mid, AXES, across)  13 us
    all_to_all x1, starting transfers between devices, local(): lax.all_to_all(chosen.reshape(8, 32, OBS), 'member', 0, 0, tiled=True, ax...  11.7 us
    all_to_all x1, waiting for transfers between devices, local(): lax.all_to_all(shares, 'member', 0, 0, tiled=True, axis_index_groups=memb...  9.45 us
    ppermute x1, starting transfers between devices, local(): lax.ppermute(lax.dynamic_slice_in_dim(own, jnp.where(here == 8, 0, 2), 4)...  8.64 us
    pallas_call x1, Pallas kernels, local(): call(first_kernel, (shape(4, LEV, NX), shape(2, LEV, NX, dtype=BF16)), [S...  6.97 us
    ppermute x1, waiting for transfers between devices, local(): other = lax.ppermute(halves, AXES, mirrored)  6.61 us
  transfers between devices with their start and end apart: 16, of which 6 were waited for; matrix products, arithmetic and copies ran while one was open for 3% of the time, Pallas kernels for 9%

profile of v2, /device:TPU:25, one launch (start us, length us, event | category | flops | bytes accessed | tf_op | source)
XLA Modules:
  0.0 163.0 jit_solution(4793898700066978643)
XLA Ops:
  0.7 1.0 reduce-precision_convert_fusion
  1.8 1.0 copy.25
  3.0 8.6 %collective-permute-start = (bf16[4,64,1280]{2,1,0:T(8,128)(2,1)S(1)}, bf16[4,64,1280]{2,1,0:T(8,128)(2,1)}, u32[]{:S(2)}, u32[]{:S(2)}) collective-permute-start(bf16[4,64,1280]{2,1,0:T(8,128)(2,1)S(1)} %constant_dynamic-slice_fusion), channel_id=1, source_target_pairs={{7,0},{8,9},{23,16},{24,25},{39,32},{40,41},{55,48},{56,57},{71,66... | collective-permute-start | bytes 1966088 | tf_op jit(solution)/shard_map/ppermute | solution.py:359
  11.7 3.5 %all-to-all-start = ((bf16[4,256,256]{2,1,0:T(8,128)(2,1)}), bf16[4,256,256]{2,1,0:T(8,128)(2,1)S(1)}, u32[]{:S(2)}, u32[]{:S(2)}) async-start(bf16[4,256,256]{2,1,0:T(8,128)(2,1)} %bitcast.8), calls=%async_computation | async-start | bytes 1048576 | tf_op jit(solution)/shard_map/all_to_all | solution.py:362
  15.2 4.5 %collective-permute-start.1 = (bf16[128,256]{1,0:T(8,128)(2,1)S(1)}, bf16[128,256]{1,0:T(8,128)(2,1)S(1)}, u32[]{:S(2)}, u32[]{:S(2)}) collective-permute-start(bf16[128,256]{1,0:T(8,128)(2,1)S(1)} %pad_maximum_fusion.2), channel_id=1, source_target_pairs={{0,456},{1,457},{2,458},{3,459},{4,460},{5,461},{6,462},{7,463},{1... | collective-permute-start | bytes 196616 | tf_op jit(solution)/shard_map/ppermute | solution.py:352
  19.7 6.6 %collective-permute-done.1 = bf16[128,256]{1,0:T(8,128)(2,1)S(1)} collective-permute-done((bf16[128,256]{1,0:T(8,128)(2,1)S(1)}, bf16[128,256]{1,0:T(8,128)(2,1)S(1)}, u32[]{:S(2)}, u32[]{:S(2)}) %collective-permute-start.1) | collective-permute-done | bytes 65568 | tf_op jit(solution)/shard_map/ppermute | solution.py:352
  26.3 0.8 broadcast_in_dim.14
  27.2 3.9 %all-to-all-start.1 = ((bf16[4,256,256]{2,1,0:T(8,128)(2,1)}), bf16[4,256,256]{2,1,0:T(8,128)(2,1)S(1)}, u32[]{:S(2)}, u32[]{:S(2)}) async-start(bf16[4,256,256]{2,1,0:T(8,128)(2,1)} %broadcast_in_dim.14), calls=%async_computation.1 | async-start | bytes 1048576 | tf_op jit(solution)/shard_map/all_to_all | solution.py:301
  31.2 1.3 collective-permute-start.2
  32.5 5.6 %collective-permute-start.3 = (bf16[4,64,1280]{2,1,0:T(8,128)(2,1)S(1)}, bf16[4,64,1280]{2,1,0:T(8,128)(2,1)}, u32[]{:S(2)}, u32[]{:S(2)}) collective-permute-start(bf16[4,64,1280]{2,1,0:T(8,128)(2,1)S(1)} %get-tuple-element.44), channel_id=1, source_target_pairs={{1,0},{2,1},{3,2},{4,3},{5,4},{6,5},{7,6},{9,8},{10,9},{11,10},{12... | collective-permute-start | bytes 1966088 | tf_op jit(solution)/shard_map/ppermute | solution.py:375
  38.1 1.3 collective-permute-start.4
  39.5 3.0 %collective-permute-start.5 = (bf16[4,256,256]{2,1,0:T(8,128)(2,1)S(1)}, bf16[4,256,256]{2,1,0:T(8,128)(2,1)}, u32[]{:S(2)}, u32[]{:S(2)}) collective-permute-start(bf16[4,256,256]{2,1,0:T(8,128)(2,1)S(1)} %all-to-all-done.1.near), channel_id=1, source_target_pairs={{0,1},{1,0},{2,3},{3,2},{4,5},{5,4},{6,7},{7,6},{8,9},{9,8},{10,11... | collective-permute-start | bytes 1572872 | tf_op jit(solution)/shard_map/ppermute | solution.py:376
  45.7 11.7 %all-to-all-start.2 = ((bf16[8,32,256]{2,1,0:T(8,128)(2,1)}), bf16[8,32,256]{2,1,0:T(8,128)(2,1)S(1)}, u32[]{:S(2)}, u32[]{:S(2)}) async-start(bf16[8,32,256]{2,1,0:T(8,128)(2,1)} %bitcast.12), calls=%async_computation.2 | async-start | bytes 262144 | tf_op jit(solution)/shard_map/all_to_all | solution.py:371
  57.4 3.2 %collective-permute-done.4.beyond = bf16[4,64,1280]{2,1,0:T(8,128)(2,1)} collective-permute-done((bf16[4,64,1280]{2,1,0:T(8,128)(2,1)}, bf16[4,64,1280]{2,1,0:T(8,128)(2,1)}, u32[]{:S(2)}, u32[]{:S(2)}) %collective-permute-start.4) | collective-permute-done | bytes 655392 | tf_op jit(solution)/shard_map/ppermute | solution.py:365
  60.6 7.0 %shard_map.130 = (f32[4,64,1280]{2,1,0:T(8,128)}, bf16[2,64,1280]{2,1,0:T(8,128)(2,1)}) custom-call(s32[1]{0:T(128)} %bitcast.place, bf16[6,64,1280]{2,1,0:T(8,128)(2,1)} %copy-done.3, bf16[4,64,1280]{2,1,0:T(8,128)(2,1)} %copy-done.11, bf16[4,64,1280]{2,1,0:T(8,128)(2,1)} %collective-permute-done.3.north, ...), custom_call_target="tpu_custom_call" | custom-call | flops 2000000000 | tf_op jit(solution)/shard_map/pallas_call | solution.py:395
  67.6 1.4 collective-permute-start.8
  69.7 3.0 %all-to-all-done.2 = bf16[8,32,256]{2,1,0:T(8,128)(2,1)S(1)} async-done(((bf16[8,32,256]{2,1,0:T(8,128)(2,1)}), bf16[8,32,256]{2,1,0:T(8,128)(2,1)S(1)}, u32[]{:S(2)}, u32[]{:S(2)}) %all-to-all-start.2) | async-done | bytes 131104 | tf_op jit(solution)/shard_map/all_to_all | solution.py:371
  74.0 13.1 %all-to-all-start.3 = ((bf16[8,32,256]{2,1,0:T(8,128)(2,1)}), bf16[8,32,256]{2,1,0:T(8,128)(2,1)S(1)}, u32[]{:S(2)}, u32[]{:S(2)}) async-start(bf16[8,32,256]{2,1,0:T(8,128)(2,1)} %broadcast_in_dim.31), calls=%async_computation.3 | async-start | bytes 262144 | tf_op jit(solution)/shard_map/all_to_all | solution.py:301
  87.1 1.3 collective-permute-start.9
  88.4 1.3 collective-permute-start.6
  89.7 3.0 %collective-permute-start.7 = (bf16[2,64,1280]{2,1,0:T(8,128)(2,1)}, bf16[2,64,1280]{2,1,0:T(8,128)(2,1)S(1)}, u32[]{:S(2)}, u32[]{:S(2)}) collective-permute-start(bf16[2,64,1280]{2,1,0:T(8,128)(2,1)} %get-tuple-element.30), channel_id=1, source_target_pairs={{1,0},{2,1},{3,2},{4,3},{5,4},{6,5},{7,6},{9,8},{10,9},{11,10},{12... | collective-permute-start | bytes 983048 | tf_op jit(solution)/shard_map/ppermute | solution.py:409
  92.8 13.0 %collective-permute-done.9.beyond_mid = bf16[2,64,1280]{2,1,0:T(8,128)(2,1)S(1)} collective-permute-done((bf16[2,64,1280]{2,1,0:T(8,128)(2,1)S(1)}, bf16[2,64,1280]{2,1,0:T(8,128)(2,1)S(1)}, u32[]{:S(2)}, u32[]{:S(2)}) %collective-permute-start.9) | collective-permute-done | bytes 327712 | tf_op jit(solution)/shard_map/ppermute | solution.py:410
  105.8 0.9 broadcast_in_dim.33
  106.6 3.5 %all-to-all-start.4 = ((bf16[4,256,256]{2,1,0:T(8,128)(2,1)}), bf16[4,256,256]{2,1,0:T(8,128)(2,1)S(1)}, u32[]{:S(2)}, u32[]{:S(2)}) async-start(bf16[4,256,256]{2,1,0:T(8,128)(2,1)} %broadcast_in_dim.33), calls=%async_computation.4 | async-start | bytes 1048576 | tf_op jit(solution)/shard_map/all_to_all | solution.py:301
  112.2 6.6 %shard_map.131 = (bf16[2,64,1280]{2,1,0:T(8,128)(2,1)}, f32[256,128]{1,0:T(8,128)}) custom-call(s32[1]{0:T(128)} %bitcast.place, bf16[6,64,1280]{2,1,0:T(8,128)(2,1)} %copy-done.3, bf16[4,64,1280]{2,1,0:T(8,128)(2,1)} %copy-done.11, bf16[4,64,1280]{2,1,0:T(8,128)(2,1)} %collective-permute-done.3.north, bf16[4,64,1280]{2,1,0:T(8,128)(2,1)} %collective-permute-done.4.beyond, ...), custom_call_target="tpu_custom_call" | custom-call | flops 2000000000 | bytes 8000000 | tf_op jit(solution)/shard_map/pallas_call | solution.py:415
  118.9 1.0 convert.7
  119.9 24.9 %all_to_all.35.parts = bf16[32,16,128]{2,1,0:T(8,128)(2,1)S(1)} all-to-all(bf16[32,16,128]{2,1,0:T(8,128)(2,1)S(1)} %bitcast.40), channel_id=1, replica_groups={{0,16,32,48,64,80,96,112,128,144,160,176,192,208,224,240,256,272,288,30..., dimensions={0} | all-to-all | bytes 262144 | tf_op jit(solution)/shard_map/all_to_all | solution.py:428
  145.5 4.3 %all-to-all-start.6 = ((bf16[32,16,128]{2,1,0:T(8,128)(2,1)}), bf16[32,16,128]{2,1,0:T(8,128)(2,1)S(1)}, u32[]{:S(2)}, u32[]{:S(2)}) async-start(bf16[32,16,128]{2,1,0:T(8,128)(2,1)} %shard_map.134), calls=%async_computation.6 | async-start | bytes 262144 | tf_op jit(solution)/shard_map/all_to_all | solution.py:430
  150.1 1.1 copy.20
  151.1 1.3 shard_map.133
  152.5 9.5 %all-to-all-done.6 = bf16[32,16,128]{2,1,0:T(8,128)(2,1)S(1)} async-done(((bf16[32,16,128]{2,1,0:T(8,128)(2,1)}), bf16[32,16,128]{2,1,0:T(8,128)(2,1)S(1)}, u32[]{:S(2)}, u32[]{:S(2)}) %all-to-all-start.6) | async-done | bytes 131104 | tf_op jit(solution)/shard_map/all_to_all | solution.py:430
  161.9 1.1 shard_map.135
  (65 shorter events, 6.1 us)
Async XLA Ops:
  0.6 2.2 %copy-start.6 = (bf16[1,64,2,1280]{3,2,1,0:T(2,128)(2,1)S(1)}, bf16[1,64,2,1280]{3,2,1,0:T(2,128)(2,1)}, u32[]{:S(2)}) copy-start(bf16[1,64,2,1280]{3,2,1,0:T(2,128)(2,1)} %param.11) | copy-start | bytes 983044
  0.6 2.2 %copy-start.5 = (bf16[64,2,1280]{2,1,0:T(2,128)(2,1)S(1)}, bf16[64,2,1280]{2,1,0:T(2,128)(2,1)}, u32[]{:S(2)}) copy-start(bf16[64,2,1280]{2,1,0:T(2,128)(2,1)} %param.13) | copy-start | bytes 983044
  3.0 28.1 %copy-start.3 = (bf16[6,64,1280]{2,1,0:T(8,128)(2,1)}, bf16[6,64,1280]{2,1,0:T(8,128)(2,1)S(1)}, u32[]{:S(2)}) copy-start(bf16[6,64,1280]{2,1,0:T(8,128)(2,1)S(1)} %slice_dynamic-update-slice_fusion.own) | copy-start | bytes 2949124
  3.0 23.3 %collective-permute-start = (bf16[4,64,1280]{2,1,0:T(8,128)(2,1)S(1)}, bf16[4,64,1280]{2,1,0:T(8,128)(2,1)}, u32[]{:S(2)}, u32[]{:S(2)}) collective-permute-start(bf16[4,64,1280]{2,1,0:T(8,128)(2,1)S(1)} %constant_dynamic-slice_fusion), channel_id=1, source_target_pairs={{7,0},{8,9},{23,16},{24,25},{39,32},{40,41},{55,48},{56,57},{71,66... | collective-permute-start | bytes 1966088 | tf_op jit(solution)/shard_map/ppermute | solution.py:359
  11.7 14.6 %all-to-all-start = ((bf16[4,256,256]{2,1,0:T(8,128)(2,1)}), bf16[4,256,256]{2,1,0:T(8,128)(2,1)S(1)}, u32[]{:S(2)}, u32[]{:S(2)}) async-start(bf16[4,256,256]{2,1,0:T(8,128)(2,1)} %bitcast.8), calls=%async_computation | async-start | bytes 1048576 | tf_op jit(solution)/shard_map/all_to_all | solution.py:362
  15.2 11.1 %collective-permute-start.1 = (bf16[128,256]{1,0:T(8,128)(2,1)S(1)}, bf16[128,256]{1,0:T(8,128)(2,1)S(1)}, u32[]{:S(2)}, u32[]{:S(2)}) collective-permute-start(bf16[128,256]{1,0:T(8,128)(2,1)S(1)} %pad_maximum_fusion.2), channel_id=1, source_target_pairs={{0,456},{1,457},{2,458},{3,459},{4,460},{5,461},{6,462},{7,463},{1... | collective-permute-start | bytes 196616 | tf_op jit(solution)/shard_map/ppermute | solution.py:352
  27.2 12.3 %all-to-all-start.1 = ((bf16[4,256,256]{2,1,0:T(8,128)(2,1)}), bf16[4,256,256]{2,1,0:T(8,128)(2,1)S(1)}, u32[]{:S(2)}, u32[]{:S(2)}) async-start(bf16[4,256,256]{2,1,0:T(8,128)(2,1)} %broadcast_in_dim.14), calls=%async_computation.1 | async-start | bytes 1048576 | tf_op jit(solution)/shard_map/all_to_all | solution.py:301
  31.1 11.4 %copy-start.15 = (s32[4]{0:T(128)S(1)}, s32[4]{0:T(128)}, u32[]{:S(2)}) copy-start(s32[4]{0:T(128)} %param.18) | copy-start | bytes 52
  31.2 26.2 %collective-permute-start.2 = (bf16[4,64,1280]{2,1,0:T(8,128)(2,1)S(1)}, bf16[4,64,1280]{2,1,0:T(8,128)(2,1)S(1)}, u32[]{:S(2)}, u32[]{:S(2)}) collective-permute-start(bf16[4,64,1280]{2,1,0:T(8,128)(2,1)S(1)} %get-tuple-element.45), channel_id=1, source_target_pairs={{0,1},{1,2},{2,3},{3,4},{4,5},{5,6},{6,7},{8,9},{9,10},{10,11},{11... | collective-permute-start | bytes 1966088 | tf_op jit(solution)/shard_map/ppermute | solution.py:374
  32.5 24.9 %collective-permute-start.3 = (bf16[4,64,1280]{2,1,0:T(8,128)(2,1)S(1)}, bf16[4,64,1280]{2,1,0:T(8,128)(2,1)}, u32[]{:S(2)}, u32[]{:S(2)}) collective-permute-start(bf16[4,64,1280]{2,1,0:T(8,128)(2,1)S(1)} %get-tuple-element.44), channel_id=1, source_target_pairs={{1,0},{2,1},{3,2},{4,3},{5,4},{6,5},{7,6},{9,8},{10,9},{11,10},{12... | collective-permute-start | bytes 1966088 | tf_op jit(solution)/shard_map/ppermute | solution.py:375
  38.1 22.5 %collective-permute-start.4 = (bf16[4,64,1280]{2,1,0:T(8,128)(2,1)}, bf16[4,64,1280]{2,1,0:T(8,128)(2,1)}, u32[]{:S(2)}, u32[]{:S(2)}) collective-permute-start(bf16[4,64,1280]{2,1,0:T(8,128)(2,1)} %collective-permute-done), channel_id=1, source_target_pairs={{0,8},{9,7},{16,24},{25,23},{32,40},{41,39},{48,56},{57,55},{66,72... | collective-permute-start | bytes 1966088 | tf_op jit(solution)/shard_map/ppermute | solution.py:365
  39.4 21.2 %copy-start.4 = (bf16[4,256,256]{2,1,0:T(8,128)(2,1)}, bf16[4,256,256]{2,1,0:T(8,128)(2,1)S(1)}, u32[]{:S(2)}) copy-start(bf16[4,256,256]{2,1,0:T(8,128)(2,1)S(1)} %all-to-all-done.1.near) | copy-start | bytes 1572868
  39.5 21.2 %collective-permute-start.5 = (bf16[4,256,256]{2,1,0:T(8,128)(2,1)S(1)}, bf16[4,256,256]{2,1,0:T(8,128)(2,1)}, u32[]{:S(2)}, u32[]{:S(2)}) collective-permute-start(bf16[4,256,256]{2,1,0:T(8,128)(2,1)S(1)} %all-to-all-done.1.near), channel_id=1, source_target_pairs={{0,1},{1,0},{2,3},{3,2},{4,5},{5,4},{6,7},{7,6},{8,9},{9,8},{10,11... | collective-permute-start | bytes 1572872 | tf_op jit(solution)/shard_map/ppermute | solution.py:376
  45.7 27.0 %all-to-all-start.2 = ((bf16[8,32,256]{2,1,0:T(8,128)(2,1)}), bf16[8,32,256]{2,1,0:T(8,128)(2,1)S(1)}, u32[]{:S(2)}, u32[]{:S(2)}) async-start(bf16[8,32,256]{2,1,0:T(8,128)(2,1)} %bitcast.12), calls=%async_computation.2 | async-start | bytes 262144 | tf_op jit(solution)/shard_map/all_to_all | solution.py:371
  57.4 3.2 %copy-start.11 = (bf16[4,64,1280]{2,1,0:T(8,128)(2,1)}, bf16[4,64,1280]{2,1,0:T(8,128)(2,1)S(1)}, u32[]{:S(2)}) copy-start(bf16[4,64,1280]{2,1,0:T(8,128)(2,1)S(1)} %collective-permute-done.2.south) | copy-start | bytes 1966084
  67.6 42.5 %copy-start.10 = (s32[4,256]{1,0:T(4,128)S(1)}, s32[4,256]{1,0:T(4,128)}, u32[]{:S(2)}) copy-start(s32[4,256]{1,0:T(4,128)} %param.17) | copy-start | bytes 12292
  67.6 42.6 %copy-start = (f32[4,64,1280]{2,1,0:T(8,128)S(1)}, f32[4,64,1280]{2,1,0:T(8,128)}, u32[]{:S(2)}) copy-start(f32[4,64,1280]{2,1,0:T(8,128)} %get-tuple-element.29.states) | copy-start | bytes 3932164
  67.6 5.7 %collective-permute-start.8 = (bf16[2,64,1280]{2,1,0:T(8,128)(2,1)}, bf16[2,64,1280]{2,1,0:T(8,128)(2,1)S(1)}, u32[]{:S(2)}, u32[]{:S(2)}) collective-permute-start(bf16[2,64,1280]{2,1,0:T(8,128)(2,1)} %get-tuple-element.30), channel_id=1, source_target_pairs={{7,0},{8,9},{23,16},{24,25},{39,32},{40,41},{55,48},{56,57},{71,66... | collective-permute-start | bytes 983048 | tf_op jit(solution)/shard_map/ppermute | solution.py:405
  74.0 31.7 %all-to-all-start.3 = ((bf16[8,32,256]{2,1,0:T(8,128)(2,1)}), bf16[8,32,256]{2,1,0:T(8,128)(2,1)S(1)}, u32[]{:S(2)}, u32[]{:S(2)}) async-start(bf16[8,32,256]{2,1,0:T(8,128)(2,1)} %broadcast_in_dim.31), calls=%async_computation.3 | async-start | bytes 262144 | tf_op jit(solution)/shard_map/all_to_all | solution.py:301
  87.1 18.6 %collective-permute-start.9 = (bf16[2,64,1280]{2,1,0:T(8,128)(2,1)S(1)}, bf16[2,64,1280]{2,1,0:T(8,128)(2,1)S(1)}, u32[]{:S(2)}, u32[]{:S(2)}) collective-permute-start(bf16[2,64,1280]{2,1,0:T(8,128)(2,1)S(1)} %collective-permute-done.8), channel_id=1, source_target_pairs={{0,8},{9,7},{16,24},{25,23},{32,40},{41,39},{48,56},{57,55},{66,72... | collective-permute-start | bytes 983048 | tf_op jit(solution)/shard_map/ppermute | solution.py:410
  88.4 22.3 %collective-permute-start.6 = (bf16[2,64,1280]{2,1,0:T(8,128)(2,1)}, bf16[2,64,1280]{2,1,0:T(8,128)(2,1)S(1)}, u32[]{:S(2)}, u32[]{:S(2)}) collective-permute-start(bf16[2,64,1280]{2,1,0:T(8,128)(2,1)} %get-tuple-element.30), channel_id=1, source_target_pairs={{0,1},{1,2},{2,3},{3,4},{4,5},{5,6},{6,7},{8,9},{9,10},{10,11},{11... | collective-permute-start | bytes 983048 | tf_op jit(solution)/shard_map/ppermute | solution.py:408
  89.7 21.1 %collective-permute-start.7 = (bf16[2,64,1280]{2,1,0:T(8,128)(2,1)}, bf16[2,64,1280]{2,1,0:T(8,128)(2,1)S(1)}, u32[]{:S(2)}, u32[]{:S(2)}) collective-permute-start(bf16[2,64,1280]{2,1,0:T(8,128)(2,1)} %get-tuple-element.30), channel_id=1, source_target_pairs={{1,0},{2,1},{3,2},{4,3},{5,4},{6,5},{7,6},{9,8},{10,9},{11,10},{12... | collective-permute-start | bytes 983048 | tf_op jit(solution)/shard_map/ppermute | solution.py:409
  105.8 5.0 %copy-start.12 = (bf16[2,64,1280]{2,1,0:T(8,128)(2,1)}, bf16[2,64,1280]{2,1,0:T(8,128)(2,1)S(1)}, u32[]{:S(2)}) copy-start(bf16[2,64,1280]{2,1,0:T(8,128)(2,1)S(1)} %collective-permute-done.9.beyond_mid) | copy-start | bytes 983044
  106.6 13.2 %all-to-all-start.4 = ((bf16[4,256,256]{2,1,0:T(8,128)(2,1)}), bf16[4,256,256]{2,1,0:T(8,128)(2,1)S(1)}, u32[]{:S(2)}, u32[]{:S(2)}) async-start(bf16[4,256,256]{2,1,0:T(8,128)(2,1)} %broadcast_in_dim.33), calls=%async_computation.4 | async-start | bytes 1048576 | tf_op jit(solution)/shard_map/all_to_all | solution.py:301
  110.2 0.6 copy-start.2
  110.8 39.1 %copy-start.8 = (f32[256,64]{0,1:T(8,128)S(1)}, f32[256,64]{0,1:T(8,128)}, u32[]{:S(2)}) copy-start(f32[256,64]{0,1:T(8,128)} %param.16) | copy-start | bytes 196612
  110.8 0.7 copy-start.13
  111.5 0.7 copy-start.14
  118.8 31.1 %copy-start.9 = (s32[4,256]{1,0:T(4,128)S(1)}, s32[4,256]{1,0:T(4,128)}, u32[]{:S(2)}) copy-start(s32[4,256]{1,0:T(4,128)} %param.19) | copy-start | bytes 12292
  118.8 31.2 %copy-start.7 = (bf16[2,64,1280]{2,1,0:T(8,128)(2,1)S(1)}, bf16[2,64,1280]{2,1,0:T(8,128)(2,1)}, u32[]{:S(2)}) copy-start(bf16[2,64,1280]{2,1,0:T(8,128)(2,1)} %get-tuple-element.36) | copy-start | bytes 983044
  118.9 32.3 %copy-start.1 = (f32[256,128]{1,0:T(8,128)S(1)}, f32[256,128]{1,0:T(8,128)}, u32[]{:S(2)}) copy-start(f32[256,128]{1,0:T(8,128)} %get-tuple-element.37.late) | copy-start | bytes 393220
  145.5 16.4 %all-to-all-start.6 = ((bf16[32,16,128]{2,1,0:T(8,128)(2,1)}), bf16[32,16,128]{2,1,0:T(8,128)(2,1)S(1)}, u32[]{:S(2)}, u32[]{:S(2)}) async-start(bf16[32,16,128]{2,1,0:T(8,128)(2,1)} %shard_map.134), calls=%async_computation.6 | async-start | bytes 262144 | tf_op jit(solution)/shard_map/all_to_all | solution.py:430

commit v3 on v2

--- a/solution.py
+++ b/solution.py
@@ -302,7 +302,6 @@
 
 
 AXES = ("member", "tile")
-Z_GROUPS = [[4 * z + x for z in range(8)] for x in range(4)]
 X_GROUPS = [[4 * z + x for x in range(4)] for z in range(8)]
 
 
@@ -320,6 +319,11 @@
             apart += [(low, up), (high, down)]
             across += [(up, high), (down, low)]
     return apart, across
+
+
+def spread_along_z(value, offset, distance):
+    arrived = lax.ppermute(value, "member", [(i, i ^ (4 * distance)) for i in range(32)])
+    return jnp.where(offset & distance != 0, arrived, value)
 
 
 def local(
@@ -359,6 +363,7 @@
     halfway = lax.ppermute(lax.dynamic_slice_in_dim(own, jnp.where(here == 8, 0, 2), 4), AXES, apart)
     departures, _ = lax.optimization_barrier((departures, own))
     slot_owner = lax.dynamic_index_in_dim(owner, member % 4, keepdims=False)
+    offset = jnp.bitwise_xor(slot_owner // 4, member // 4)
     offered = lax.all_to_all(departures[0], "member", 0, 0, tiled=True, axis_index_groups=X_GROUPS)
     halfway, other, offered, own = lax.optimization_barrier((halfway, other, offered, own))
 
@@ -367,10 +372,13 @@
     y_groups = [[8 * z + 2 * y + core for y in range(4)] for z in range(2) for core in range(2)]
     near = gathered_from(pair, "tile", y_groups).reshape(4, 4 * LEV, 4 * LEV)
     chosen = lax.dynamic_index_in_dim(offered, slot_owner % 4, keepdims=False)
-    chosen, _ = lax.optimization_barrier((chosen, near))
-    pieces = lax.all_to_all(chosen.reshape(8, 32, OBS), "member", 0, 0, tiled=True, axis_index_groups=Z_GROUPS)
+    chosen = spread_along_z(chosen, offset, 1)
     forward = [(i, i + 1) for i in range(15) if i != 7]
     backward = [(i + 1, i) for i in range(15) if i != 7]
+    own, near, chosen = lax.optimization_barrier((own, near, chosen))
+    chosen = spread_along_z(chosen, offset, 2)
+    chosen, place = lax.optimization_barrier((chosen, place))
+    whole = spread_along_z(chosen, offset, 4)
     south = lax.ppermute(own[2:], "tile", forward)
     north = lax.ppermute(own[:4], "tile", backward)
     far = lax.ppermute(near, "tile", [(i, i ^ 1) for i in range(16)])
@@ -403,14 +411,10 @@
     )(place, *fields, spread, evens)
 
     halfway_mid = lax.ppermute(halo, AXES, apart)
-    pieces, halfway_mid = lax.optimization_barrier((pieces, halfway_mid))
-    kept = lax.dynamic_index_in_dim(pieces, slot_owner // 4, keepdims=False)
     south_mid = lax.ppermute(halo, "tile", forward)
     north_mid = lax.ppermute(halo, "tile", backward)
     beyond_mid = lax.ppermute(halfway_mid, AXES, across)
     early = call(early_kernel, shape(4 * LEV, LANES), [VMEM] * 2, flops=200_000_000, traffic=2_000_000)(states, cells)
-    whole = gathered_from(kept, "member", Z_GROUPS).reshape(CH, OBS)
-    whole, beyond_mid = lax.optimization_barrier((whole, beyond_mid))
     owned = gathered_from(whole, "member", X_GROUPS).reshape(SLOTS, CH, OBS)
     final, late = call(
         second_kernel,

time: 164 us -> 156 us (0.951)
  starting transfers between devices: 71.4 us -> 54.9 us
  waiting for transfers between devices: 35.9 us -> 48.1 us
  blocking collectives: 24.9 us -> 22.5 us
    ppermute x0 -> x3, waiting for transfers between devices: none -> 31.7 us  [spread_along_z(): lax.ppermute(value, 'member', [(i, i ^ 4 * distance) for i in range(32)])]
    all_to_all x3 -> x2, starting transfers between devices: 20.5 us -> 8.48 us  [gathered_from(): lax.all_to_all(copies, axis, 0, 0, tiled=True, axis_index_groups=groups)]
    all_to_all x1 -> x0, starting transfers between devices: 11.7 us -> none  [local(): lax.all_to_all(chosen.reshape(8, 32, OBS), 'member', 0, 0, tiled=True, ax...]
    ppermute x1, waiting for transfers between devices: 13 us -> 1.98 us  [local(): beyond_mid = lax.ppermute(halfway_mid, AXES, across)]
    ppermute x0 -> x3, starting transfers between devices: none -> 6.53 us  [spread_along_z(): lax.ppermute(value, 'member', [(i, i ^ 4 * distance) for i in range(32)])]
    ppermute x1, waiting for transfers between devices: 3.18 us -> 0.01 us  [local(): beyond = lax.ppermute(halfway, AXES, across)]
    all_to_all x1 -> x0, waiting for transfers between devices: 2.98 us -> none  [local(): lax.all_to_all(chosen.reshape(8, 32, OBS), 'member', 0, 0, tiled=True, ax...]
    ppermute x1, waiting for transfers between devices: 6.61 us -> 4.04 us  [local(): other = lax.ppermute(halves, AXES, mirrored)]
  transfers between devices with their start and end apart: 16 -> 17, of which waited for: 6 -> 6; matrix products, arithmetic and copies ran while one was open for 3% -> 2% of each run, Pallas kernels for 9% -> 5%
where the time goes in v3:
time: 156 us; the launch traced here: 155 us
  starting transfers between devices  54.9 us (35%)
  waiting for transfers between devices  48.1 us (31%)
  blocking collectives  22.5 us (14%)
  Pallas kernels  17.2 us (11%)
  local copies, waits for them, and re-layouts  6.44 us (4%)
  between operations  3.84 us (2%)
  other arithmetic  2.15 us (1%)
    ppermute x3, waiting for transfers between devices, spread_along_z(): lax.ppermute(value, 'member', [(i, i ^ 4 * distance) for i in range(32)])  31.7 us
    all_to_all x1, blocking collectives, local(): lax.all_to_all(both, 'member', 0, 0, tiled=True, axis_index_groups=members)  22.5 us
    all_to_all x1, waiting for transfers between devices, local(): lax.all_to_all(shares, 'member', 0, 0, tiled=True, axis_index_groups=memb...  10.4 us
    ppermute x1, starting transfers between devices, local(): lax.ppermute(lax.dynamic_slice_in_dim(own, jnp.where(here == 8, 0, 2), 4)...  8.64 us
    all_to_all x2, starting transfers between devices, gathered_from(): lax.all_to_all(copies, axis, 0, 0, tiled=True, axis_index_groups=groups)  8.48 us
    pallas_call x1, Pallas kernels, local(): call(first_kernel, (shape(4, LEV, NX), shape(2, LEV, NX, dtype=BF16)), [S...  6.95 us
    pallas_call x1, Pallas kernels, local(): call(second_kernel, (shape(2, LEV, NX, dtype=BF16), shape(4 * LEV, LANES)...  6.58 us
    ppermute x3, starting transfers between devices, spread_along_z(): lax.ppermute(value, 'member', [(i, i ^ 4 * distance) for i in range(32)])  6.53 us
  transfers between devices with their start and end apart: 17, of which 6 were waited for; matrix products, arithmetic and copies ran while one was open for 2% of the time, Pallas kernels for 5%

profile of v3, /device:TPU:25, one launch (start us, length us, event | category | flops | bytes accessed | tf_op | source)
XLA Modules:
  0.0 155.2 jit_solution(14806695314882406566)
XLA Ops:
  0.7 1.0 reduce-precision_convert_fusion
  1.8 1.0 copy.25
  3.1 8.6 %collective-permute-start = (bf16[4,64,1280]{2,1,0:T(8,128)(2,1)S(1)}, bf16[4,64,1280]{2,1,0:T(8,128)(2,1)}, u32[]{:S(2)}, u32[]{:S(2)}) collective-permute-start(bf16[4,64,1280]{2,1,0:T(8,128)(2,1)S(1)} %constant_dynamic-slice_fusion), channel_id=1, source_target_pairs={{7,0},{8,9},{23,16},{24,25},{39,32},{40,41},{55,48},{56,57},{71,66... | collective-permute-start | bytes 1966088 | tf_op jit(solution)/shard_map/ppermute | solution.py:363
  11.7 3.5 %all-to-all-start = ((bf16[4,256,256]{2,1,0:T(8,128)(2,1)}), bf16[4,256,256]{2,1,0:T(8,128)(2,1)S(1)}, u32[]{:S(2)}, u32[]{:S(2)}) async-start(bf16[4,256,256]{2,1,0:T(8,128)(2,1)} %bitcast.8), calls=%async_computation | async-start | bytes 1048576 | tf_op jit(solution)/shard_map/all_to_all | solution.py:367
  15.2 4.5 %collective-permute-start.1 = (bf16[128,256]{1,0:T(8,128)(2,1)S(1)}, bf16[128,256]{1,0:T(8,128)(2,1)S(1)}, u32[]{:S(2)}, u32[]{:S(2)}) collective-permute-start(bf16[128,256]{1,0:T(8,128)(2,1)S(1)} %pad_maximum_fusion.2), channel_id=1, source_target_pairs={{0,456},{1,457},{2,458},{3,459},{4,460},{5,461},{6,462},{7,463},{1... | collective-permute-start | bytes 196616 | tf_op jit(solution)/shard_map/ppermute | solution.py:356
  22.3 4.0 %collective-permute-done.1 = bf16[128,256]{1,0:T(8,128)(2,1)S(1)} collective-permute-done((bf16[128,256]{1,0:T(8,128)(2,1)S(1)}, bf16[128,256]{1,0:T(8,128)(2,1)S(1)}, u32[]{:S(2)}, u32[]{:S(2)}) %collective-permute-start.1) | collective-permute-done | bytes 65568 | tf_op jit(solution)/shard_map/ppermute | solution.py:356
  27.2 3.9 %all-to-all-start.1 = ((bf16[4,256,256]{2,1,0:T(8,128)(2,1)}), bf16[4,256,256]{2,1,0:T(8,128)(2,1)S(1)}, u32[]{:S(2)}, u32[]{:S(2)}) async-start(bf16[4,256,256]{2,1,0:T(8,128)(2,1)} %broadcast_in_dim.10), calls=%async_computation.1 | async-start | bytes 1048576 | tf_op jit(solution)/shard_map/all_to_all | solution.py:301
  31.1 2.3 %collective-permute-start.2 = (bf16[256,256]{1,0:T(8,128)(2,1)S(1)}, bf16[256,256]{1,0:T(8,128)(2,1)S(1)}, u32[]{:S(2)}, u32[]{:S(2)}) collective-permute-start(bf16[256,256]{1,0:T(8,128)(2,1)S(1)} %dynamic-slice_bitcast_fusion), channel_id=1, source_target_pairs={{0,64},{16,80},{32,96},{48,112},{64,0},{80,16},{96,32},{112,48},{1... | collective-permute-start | bytes 393224 | tf_op jit(solution)/shard_map/ppermute | solution.py:325
  34.1 1.3 collective-permute-start.6
  35.4 1.8 %collective-permute-done.2 = bf16[256,256]{1,0:T(8,128)(2,1)S(1)} collective-permute-done((bf16[256,256]{1,0:T(8,128)(2,1)S(1)}, bf16[256,256]{1,0:T(8,128)(2,1)S(1)}, u32[]{:S(2)}, u32[]{:S(2)}) %collective-permute-start.2) | collective-permute-done | bytes 131104 | tf_op jit(solution)/shard_map/ppermute | solution.py:325
  37.3 1.3 collective-permute-start.4
  38.6 6.5 %collective-permute-start.5 = (bf16[4,64,1280]{2,1,0:T(8,128)(2,1)S(1)}, bf16[4,64,1280]{2,1,0:T(8,128)(2,1)}, u32[]{:S(2)}, u32[]{:S(2)}) collective-permute-start(bf16[4,64,1280]{2,1,0:T(8,128)(2,1)S(1)} %get-tuple-element.44), channel_id=1, source_target_pairs={{1,0},{2,1},{3,2},{4,3},{5,4},{6,5},{7,6},{9,8},{10,9},{11,10},{12... | collective-permute-start | bytes 1966088 | tf_op jit(solution)/shard_map/ppermute | solution.py:383
  45.1 2.8 %collective-permute-start.7 = (bf16[4,256,256]{2,1,0:T(8,128)(2,1)S(1)}, bf16[4,256,256]{2,1,0:T(8,128)(2,1)}, u32[]{:S(2)}, u32[]{:S(2)}) collective-permute-start(bf16[4,256,256]{2,1,0:T(8,128)(2,1)S(1)} %all-to-all-done.1.near), channel_id=1, source_target_pairs={{0,1},{1,0},{2,3},{3,2},{4,5},{5,4},{6,7},{7,6},{8,9},{9,8},{10,11... | collective-permute-start | bytes 1572872 | tf_op jit(solution)/shard_map/ppermute | solution.py:384
  47.9 2.4 %collective-permute-start.3 = (bf16[256,256]{1,0:T(8,128)(2,1)S(1)}, bf16[256,256]{1,0:T(8,128)(2,1)S(1)}, u32[]{:S(2)}, u32[]{:S(2)}) collective-permute-start(bf16[256,256]{1,0:T(8,128)(2,1)S(1)} %broadcast_select_fusion.1), channel_id=1, source_target_pairs={{0,128},{16,144},{32,160},{48,176},{64,192},{80,208},{96,224},{112... | collective-permute-start | bytes 393224 | tf_op jit(solution)/shard_map/ppermute | solution.py:325
  50.3 20.6 %collective-permute-done.3 = bf16[256,256]{1,0:T(8,128)(2,1)S(1)} collective-permute-done((bf16[256,256]{1,0:T(8,128)(2,1)S(1)}, bf16[256,256]{1,0:T(8,128)(2,1)S(1)}, u32[]{:S(2)}, u32[]{:S(2)}) %collective-permute-start.3) | collective-permute-done | bytes 131104 | tf_op jit(solution)/shard_map/ppermute | solution.py:325
  71.8 6.9 %shard_map.130 = (f32[4,64,1280]{2,1,0:T(8,128)}, bf16[2,64,1280]{2,1,0:T(8,128)(2,1)}) custom-call(s32[1]{0:T(128)} %bitcast.10.place, bf16[6,64,1280]{2,1,0:T(8,128)(2,1)} %copy-done.3, bf16[4,64,1280]{2,1,0:T(8,128)(2,1)} %copy-done.11, bf16[4,64,1280]{2,1,0:T(8,128)(2,1)} %collective-permute-done.5.north, ...), custom_call_target="tpu_custom_call" | custom-call | flops 2000000000 | tf_op jit(solution)/shard_map/pallas_call | solution.py:403
  78.8 1.4 collective-permute-start.10
  80.2 1.9 %collective-permute-start.12 = (bf16[256,256]{1,0:T(8,128)(2,1)S(1)}, bf16[256,256]{1,0:T(8,128)(2,1)S(1)}, u32[]{:S(2)}, u32[]{:S(2)}) collective-permute-start(bf16[256,256]{1,0:T(8,128)(2,1)S(1)} %broadcast_select_fusion.2), channel_id=1, source_target_pairs={{0,256},{16,272},{32,288},{48,304},{64,320},{80,336},{96,352},{112... | collective-permute-start | bytes 393224 | tf_op jit(solution)/shard_map/ppermute | solution.py:325
  82.1 1.3 collective-permute-start.8
  83.4 3.0 %collective-permute-start.9 = (bf16[2,64,1280]{2,1,0:T(8,128)(2,1)}, bf16[2,64,1280]{2,1,0:T(8,128)(2,1)S(1)}, u32[]{:S(2)}, u32[]{:S(2)}) collective-permute-start(bf16[2,64,1280]{2,1,0:T(8,128)(2,1)} %get-tuple-element.35), channel_id=1, source_target_pairs={{1,0},{2,1},{3,2},{4,3},{5,4},{6,5},{7,6},{9,8},{10,9},{11,10},{12... | collective-permute-start | bytes 983048 | tf_op jit(solution)/shard_map/ppermute | solution.py:415
  86.5 1.3 collective-permute-start.11
  87.8 9.3 %collective-permute-done.12 = bf16[256,256]{1,0:T(8,128)(2,1)S(1)} collective-permute-done((bf16[256,256]{1,0:T(8,128)(2,1)S(1)}, bf16[256,256]{1,0:T(8,128)(2,1)S(1)}, u32[]{:S(2)}, u32[]{:S(2)}) %collective-permute-start.12) | collective-permute-done | bytes 131104 | tf_op jit(solution)/shard_map/ppermute | solution.py:325
  98.0 4.5 %all-to-all-start.2 = ((bf16[4,256,256]{2,1,0:T(8,128)(2,1)}), bf16[4,256,256]{2,1,0:T(8,128)(2,1)S(1)}, u32[]{:S(2)}, u32[]{:S(2)}) async-start(bf16[4,256,256]{2,1,0:T(8,128)(2,1)} %broadcast_in_dim.23), calls=%async_computation.2 | async-start | bytes 1048576 | tf_op jit(solution)/shard_map/all_to_all | solution.py:301
  103.2 2.0 %collective-permute-done.11.beyond_mid = bf16[2,64,1280]{2,1,0:T(8,128)(2,1)S(1)} collective-permute-done((bf16[2,64,1280]{2,1,0:T(8,128)(2,1)S(1)}, bf16[2,64,1280]{2,1,0:T(8,128)(2,1)S(1)}, u32[]{:S(2)}, u32[]{:S(2)}) %collective-permute-start.11) | collective-permute-done | bytes 327712 | tf_op jit(solution)/shard_map/ppermute | solution.py:416
  105.9 6.6 %shard_map.131 = (bf16[2,64,1280]{2,1,0:T(8,128)(2,1)}, f32[256,128]{1,0:T(8,128)}) custom-call(s32[1]{0:T(128)} %bitcast.10.place, bf16[6,64,1280]{2,1,0:T(8,128)(2,1)} %copy-done.3, bf16[4,64,1280]{2,1,0:T(8,128)(2,1)} %copy-done.11, bf16[4,64,1280]{2,1,0:T(8,128)(2,1)} %collective-permute-done.5.north, ...), custom_call_target="tpu_custom_call" | custom-call | flops 2000000000 | bytes 8000000 | tf_op jit(solution)/shard_map/pallas_call | solution.py:419
  112.5 1.0 convert.7
  113.5 22.5 %all_to_all.25.parts = bf16[32,16,128]{2,1,0:T(8,128)(2,1)S(1)} all-to-all(bf16[32,16,128]{2,1,0:T(8,128)(2,1)S(1)} %bitcast.37), channel_id=1, replica_groups={{0,16,32,48,64,80,96,112,128,144,160,176,192,208,224,240,256,272,288,30..., dimensions={0} | all-to-all | bytes 262144 | tf_op jit(solution)/shard_map/all_to_all | solution.py:432
  136.7 4.3 %all-to-all-start.4 = ((bf16[32,16,128]{2,1,0:T(8,128)(2,1)}), bf16[32,16,128]{2,1,0:T(8,128)(2,1)S(1)}, u32[]{:S(2)}, u32[]{:S(2)}) async-start(bf16[32,16,128]{2,1,0:T(8,128)(2,1)} %shard_map.134), calls=%async_computation.4 | async-start | bytes 262144 | tf_op jit(solution)/shard_map/all_to_all | solution.py:434
  141.3 1.1 copy.20
  142.3 1.3 shard_map.133
  143.7 10.4 %all-to-all-done.4 = bf16[32,16,128]{2,1,0:T(8,128)(2,1)S(1)} async-done(((bf16[32,16,128]{2,1,0:T(8,128)(2,1)}), bf16[32,16,128]{2,1,0:T(8,128)(2,1)S(1)}, u32[]{:S(2)}, u32[]{:S(2)}) %all-to-all-start.4) | async-done | bytes 131104 | tf_op jit(solution)/shard_map/all_to_all | solution.py:434
  154.0 1.1 shard_map.135
  (68 shorter events, 5.8 us)
Async XLA Ops:
  0.6 2.2 %copy-start.6 = (bf16[1,64,2,1280]{3,2,1,0:T(2,128)(2,1)S(1)}, bf16[1,64,2,1280]{3,2,1,0:T(2,128)(2,1)}, u32[]{:S(2)}) copy-start(bf16[1,64,2,1280]{3,2,1,0:T(2,128)(2,1)} %param.11) | copy-start | bytes 983044
  0.6 2.2 %copy-start.5 = (bf16[64,2,1280]{2,1,0:T(2,128)(2,1)S(1)}, bf16[64,2,1280]{2,1,0:T(2,128)(2,1)}, u32[]{:S(2)}) copy-start(bf16[64,2,1280]{2,1,0:T(2,128)(2,1)} %param.13) | copy-start | bytes 983044
  2.9 16.8 %copy-start.15 = (s32[4]{0:T(128)S(1)}, s32[4]{0:T(128)}, u32[]{:S(2)}) copy-start(s32[4]{0:T(128)} %param.18) | copy-start | bytes 52
  3.0 34.2 %copy-start.3 = (bf16[6,64,1280]{2,1,0:T(8,128)(2,1)}, bf16[6,64,1280]{2,1,0:T(8,128)(2,1)S(1)}, u32[]{:S(2)}) copy-start(bf16[6,64,1280]{2,1,0:T(8,128)(2,1)S(1)} %slice_dynamic-update-slice_fusion.own) | copy-start | bytes 2949124
  3.1 23.3 %collective-permute-start = (bf16[4,64,1280]{2,1,0:T(8,128)(2,1)S(1)}, bf16[4,64,1280]{2,1,0:T(8,128)(2,1)}, u32[]{:S(2)}, u32[]{:S(2)}) collective-permute-start(bf16[4,64,1280]{2,1,0:T(8,128)(2,1)S(1)} %constant_dynamic-slice_fusion), channel_id=1, source_target_pairs={{7,0},{8,9},{23,16},{24,25},{39,32},{40,41},{55,48},{56,57},{71,66... | collective-permute-start | bytes 1966088 | tf_op jit(solution)/shard_map/ppermute | solution.py:363
  11.7 14.6 %all-to-all-start = ((bf16[4,256,256]{2,1,0:T(8,128)(2,1)}), bf16[4,256,256]{2,1,0:T(8,128)(2,1)S(1)}, u32[]{:S(2)}, u32[]{:S(2)}) async-start(bf16[4,256,256]{2,1,0:T(8,128)(2,1)} %bitcast.8), calls=%async_computation | async-start | bytes 1048576 | tf_op jit(solution)/shard_map/all_to_all | solution.py:367
  15.2 11.1 %collective-permute-start.1 = (bf16[128,256]{1,0:T(8,128)(2,1)S(1)}, bf16[128,256]{1,0:T(8,128)(2,1)S(1)}, u32[]{:S(2)}, u32[]{:S(2)}) collective-permute-start(bf16[128,256]{1,0:T(8,128)(2,1)S(1)} %pad_maximum_fusion.2), channel_id=1, source_target_pairs={{0,456},{1,457},{2,458},{3,459},{4,460},{5,461},{6,462},{7,463},{1... | collective-permute-start | bytes 196616 | tf_op jit(solution)/shard_map/ppermute | solution.py:356
  27.2 10.0 %all-to-all-start.1 = ((bf16[4,256,256]{2,1,0:T(8,128)(2,1)}), bf16[4,256,256]{2,1,0:T(8,128)(2,1)S(1)}, u32[]{:S(2)}, u32[]{:S(2)}) async-start(bf16[4,256,256]{2,1,0:T(8,128)(2,1)} %broadcast_in_dim.10), calls=%async_computation.1 | async-start | bytes 1048576 | tf_op jit(solution)/shard_map/all_to_all | solution.py:301
  31.1 6.0 %collective-permute-start.2 = (bf16[256,256]{1,0:T(8,128)(2,1)S(1)}, bf16[256,256]{1,0:T(8,128)(2,1)S(1)}, u32[]{:S(2)}, u32[]{:S(2)}) collective-permute-start(bf16[256,256]{1,0:T(8,128)(2,1)S(1)} %dynamic-slice_bitcast_fusion), channel_id=1, source_target_pairs={{0,64},{16,80},{32,96},{48,112},{64,0},{80,16},{96,32},{112,48},{1... | collective-permute-start | bytes 393224 | tf_op jit(solution)/shard_map/ppermute | solution.py:325
  34.1 36.8 %collective-permute-start.6 = (bf16[4,64,1280]{2,1,0:T(8,128)(2,1)}, bf16[4,64,1280]{2,1,0:T(8,128)(2,1)}, u32[]{:S(2)}, u32[]{:S(2)}) collective-permute-start(bf16[4,64,1280]{2,1,0:T(8,128)(2,1)} %collective-permute-done), channel_id=1, source_target_pairs={{0,8},{9,7},{16,24},{25,23},{32,40},{41,39},{48,56},{57,55},{66,72... | collective-permute-start | bytes 1966088 | tf_op jit(solution)/shard_map/ppermute | solution.py:370
  37.2 7.9 %copy-start.4 = (bf16[4,256,256]{2,1,0:T(8,128)(2,1)}, bf16[4,256,256]{2,1,0:T(8,128)(2,1)S(1)}, u32[]{:S(2)}) copy-start(bf16[4,256,256]{2,1,0:T(8,128)(2,1)S(1)} %all-to-all-done.1.near) | copy-start | bytes 1572868
  37.3 33.6 %collective-permute-start.4 = (bf16[4,64,1280]{2,1,0:T(8,128)(2,1)S(1)}, bf16[4,64,1280]{2,1,0:T(8,128)(2,1)S(1)}, u32[]{:S(2)}, u32[]{:S(2)}) collective-permute-start(bf16[4,64,1280]{2,1,0:T(8,128)(2,1)S(1)} %get-tuple-element.45), channel_id=1, source_target_pairs={{0,1},{1,2},{2,3},{3,4},{4,5},{5,6},{6,7},{8,9},{9,10},{10,11},{11... | collective-permute-start | bytes 1966088 | tf_op jit(solution)/shard_map/ppermute | solution.py:382
  38.6 32.4 %collective-permute-start.5 = (bf16[4,64,1280]{2,1,0:T(8,128)(2,1)S(1)}, bf16[4,64,1280]{2,1,0:T(8,128)(2,1)}, u32[]{:S(2)}, u32[]{:S(2)}) collective-permute-start(bf16[4,64,1280]{2,1,0:T(8,128)(2,1)S(1)} %get-tuple-element.44), channel_id=1, source_target_pairs={{1,0},{2,1},{3,2},{4,3},{5,4},{6,5},{7,6},{9,8},{10,9},{11,10},{12... | collective-permute-start | bytes 1966088 | tf_op jit(solution)/shard_map/ppermute | solution.py:383
  45.1 25.8 %collective-permute-start.7 = (bf16[4,256,256]{2,1,0:T(8,128)(2,1)S(1)}, bf16[4,256,256]{2,1,0:T(8,128)(2,1)}, u32[]{:S(2)}, u32[]{:S(2)}) collective-permute-start(bf16[4,256,256]{2,1,0:T(8,128)(2,1)S(1)} %all-to-all-done.1.near), channel_id=1, source_target_pairs={{0,1},{1,0},{2,3},{3,2},{4,5},{5,4},{6,7},{7,6},{8,9},{9,8},{10,11... | collective-permute-start | bytes 1572872 | tf_op jit(solution)/shard_map/ppermute | solution.py:384
  47.9 23.0 %collective-permute-start.3 = (bf16[256,256]{1,0:T(8,128)(2,1)S(1)}, bf16[256,256]{1,0:T(8,128)(2,1)S(1)}, u32[]{:S(2)}, u32[]{:S(2)}) collective-permute-start(bf16[256,256]{1,0:T(8,128)(2,1)S(1)} %broadcast_select_fusion.1), channel_id=1, source_target_pairs={{0,128},{16,144},{32,160},{48,176},{64,192},{80,208},{96,224},{112... | collective-permute-start | bytes 393224 | tf_op jit(solution)/shard_map/ppermute | solution.py:325
  70.9 0.8 copy-start.11
  78.7 23.8 %copy-start.10 = (s32[4,256]{1,0:T(4,128)S(1)}, s32[4,256]{1,0:T(4,128)}, u32[]{:S(2)}) copy-start(s32[4,256]{1,0:T(4,128)} %param.17) | copy-start | bytes 12292
  78.7 23.8 %copy-start = (f32[4,64,1280]{2,1,0:T(8,128)S(1)}, f32[4,64,1280]{2,1,0:T(8,128)}, u32[]{:S(2)}) copy-start(f32[4,64,1280]{2,1,0:T(8,128)} %get-tuple-element.34.states) | copy-start | bytes 3932164
  78.8 7.7 %collective-permute-start.10 = (bf16[2,64,1280]{2,1,0:T(8,128)(2,1)}, bf16[2,64,1280]{2,1,0:T(8,128)(2,1)S(1)}, u32[]{:S(2)}, u32[]{:S(2)}) collective-permute-start(bf16[2,64,1280]{2,1,0:T(8,128)(2,1)} %get-tuple-element.35), channel_id=1, source_target_pairs={{7,0},{8,9},{23,16},{24,25},{39,32},{40,41},{55,48},{56,57},{71,66... | collective-permute-start | bytes 983048 | tf_op jit(solution)/shard_map/ppermute | solution.py:413
  80.2 16.9 %collective-permute-start.12 = (bf16[256,256]{1,0:T(8,128)(2,1)S(1)}, bf16[256,256]{1,0:T(8,128)(2,1)S(1)}, u32[]{:S(2)}, u32[]{:S(2)}) collective-permute-start(bf16[256,256]{1,0:T(8,128)(2,1)S(1)} %broadcast_select_fusion.2), channel_id=1, source_target_pairs={{0,256},{16,272},{32,288},{48,304},{64,320},{80,336},{96,352},{112... | collective-permute-start | bytes 393224 | tf_op jit(solution)/shard_map/ppermute | solution.py:325
  82.1 21.0 %collective-permute-start.8 = (bf16[2,64,1280]{2,1,0:T(8,128)(2,1)}, bf16[2,64,1280]{2,1,0:T(8,128)(2,1)S(1)}, u32[]{:S(2)}, u32[]{:S(2)}) collective-permute-start(bf16[2,64,1280]{2,1,0:T(8,128)(2,1)} %get-tuple-element.35), channel_id=1, source_target_pairs={{0,1},{1,2},{2,3},{3,4},{4,5},{5,6},{6,7},{8,9},{9,10},{10,11},{11... | collective-permute-start | bytes 983048 | tf_op jit(solution)/shard_map/ppermute | solution.py:414
  83.4 19.7 %collective-permute-start.9 = (bf16[2,64,1280]{2,1,0:T(8,128)(2,1)}, bf16[2,64,1280]{2,1,0:T(8,128)(2,1)S(1)}, u32[]{:S(2)}, u32[]{:S(2)}) collective-permute-start(bf16[2,64,1280]{2,1,0:T(8,128)(2,1)} %get-tuple-element.35), channel_id=1, source_target_pairs={{1,0},{2,1},{3,2},{4,3},{5,4},{6,5},{7,6},{9,8},{10,9},{11,10},{12... | collective-permute-start | bytes 983048 | tf_op jit(solution)/shard_map/ppermute | solution.py:415
  86.5 18.6 %collective-permute-start.11 = (bf16[2,64,1280]{2,1,0:T(8,128)(2,1)S(1)}, bf16[2,64,1280]{2,1,0:T(8,128)(2,1)S(1)}, u32[]{:S(2)}, u32[]{:S(2)}) collective-permute-start(bf16[2,64,1280]{2,1,0:T(8,128)(2,1)S(1)} %collective-permute-done.10), channel_id=1, source_target_pairs={{0,8},{9,7},{16,24},{25,23},{32,40},{41,39},{48,56},{57,55},{66,72... | collective-permute-start | bytes 983048 | tf_op jit(solution)/shard_map/ppermute | solution.py:416
  98.0 15.5 %all-to-all-start.2 = ((bf16[4,256,256]{2,1,0:T(8,128)(2,1)}), bf16[4,256,256]{2,1,0:T(8,128)(2,1)S(1)}, u32[]{:S(2)}, u32[]{:S(2)}) async-start(bf16[4,256,256]{2,1,0:T(8,128)(2,1)} %broadcast_in_dim.23), calls=%async_computation.2 | async-start | bytes 1048576 | tf_op jit(solution)/shard_map/all_to_all | solution.py:301
  102.5 2.6 %copy-start.2 = (s32[4,256]{1,0:T(4,128)}, s32[4,256]{1,0:T(4,128)S(1)}, u32[]{:S(2)}) copy-start(s32[4,256]{1,0:T(4,128)S(1)} %broadcast_subtract_fusion.cells) | copy-start | bytes 12292
  103.1 37.9 %copy-start.8 = (f32[256,64]{0,1:T(8,128)S(1)}, f32[256,64]{0,1:T(8,128)}, u32[]{:S(2)}) copy-start(f32[256,64]{0,1:T(8,128)} %param.16) | copy-start | bytes 196612
  103.1 2.0 %copy-start.12 = (bf16[2,64,1280]{2,1,0:T(8,128)(2,1)}, bf16[2,64,1280]{2,1,0:T(8,128)(2,1)S(1)}, u32[]{:S(2)}) copy-start(bf16[2,64,1280]{2,1,0:T(8,128)(2,1)S(1)} %collective-permute-done.8.south_mid) | copy-start | bytes 983044
  103.2 2.0 %copy-start.13 = (bf16[2,64,1280]{2,1,0:T(8,128)(2,1)}, bf16[2,64,1280]{2,1,0:T(8,128)(2,1)S(1)}, u32[]{:S(2)}) copy-start(bf16[2,64,1280]{2,1,0:T(8,128)(2,1)S(1)} %collective-permute-done.9.north_mid) | copy-start | bytes 983044
  112.5 28.6 %copy-start.9 = (s32[4,256]{1,0:T(4,128)S(1)}, s32[4,256]{1,0:T(4,128)}, u32[]{:S(2)}) copy-start(s32[4,256]{1,0:T(4,128)} %param.19) | copy-start | bytes 12292
  112.5 28.8 %copy-start.7 = (bf16[2,64,1280]{2,1,0:T(8,128)(2,1)S(1)}, bf16[2,64,1280]{2,1,0:T(8,128)(2,1)}, u32[]{:S(2)}) copy-start(bf16[2,64,1280]{2,1,0:T(8,128)(2,1)} %get-tuple-element.36) | copy-start | bytes 983044
  112.5 29.8 %copy-start.1 = (f32[256,128]{1,0:T(8,128)S(1)}, f32[256,128]{1,0:T(8,128)}, u32[]{:S(2)}) copy-start(f32[256,128]{1,0:T(8,128)} %get-tuple-element.37.late) | copy-start | bytes 393220
  136.7 17.3 %all-to-all-start.4 = ((bf16[32,16,128]{2,1,0:T(8,128)(2,1)}), bf16[32,16,128]{2,1,0:T(8,128)(2,1)S(1)}, u32[]{:S(2)}, u32[]{:S(2)}) async-start(bf16[32,16,128]{2,1,0:T(8,128)(2,1)} %shard_map.134), calls=%async_computation.4 | async-start | bytes 262144 | tf_op jit(solution)/shard_map/all_to_all | solution.py:434
  (1 other events, 0.7 us)

commit v4 on v3

--- a/solution.py
+++ b/solution.py
@@ -1,6 +1,5 @@
 import jax
 import jax.numpy as jnp
-import numpy as np
 from jax import lax
 from jax.experimental import pallas as pl
 from jax.experimental.pallas import tpu as pltpu
@@ -116,14 +115,26 @@
     return jnp.sum(jnp.where(diagonal, row_ref[...], 0.0), axis=1, keepdims=True)
 
 
-def two_slots(here, line, numbers, spread, evens, matrices, blocks, parts, state, even, odd, stored, first_done):
+def even_blocks():
+    lane = lax.broadcasted_iota(jnp.int32, (16, NX), 1)
+    block = (lane * 52429) >> 20
+    return jnp.concatenate([(1 - (block & 1)).astype(F32).astype(BF16)] * 4, axis=0)
+
+
+def two_slots(here, line, numbers, spread, evens, matrices, waits, parts, state, even, odd, stored, first_done):
     centre_part, east_part, north_part = parts
+    first_loads, loads, blocks, numbers_ready = waits
     for row in range(4):
+        if row < len(first_loads):
+            first_loads[row].wait()
         cross = numbers[row, 0].astype(F32) + spread
         along = numbers[row, 1].astype(F32) + spread
         east_part[row] = cross
         north_part[row] = along
         centre_part[row] = 1.0 - 2.0 * spread - cross - along
+    numbers_ready()
+    for load in loads:
+        load.wait()
     for slot in range(2):
         count = 4 - 2 * slot
         for row in range(count):
@@ -162,57 +173,57 @@
 
 
 def first_kernel(
-    place, own, south, north, beyond, near, far, spread_ref, evens,
-    states_out, halo_out,
-    rows, numbers, matrices, centre_part, east_part, north_part, state, later, even, odd, sems,
+    place, own, south, north, beyond, near, far, spread_ref,
+    states_out, numbers_out, halo_out,
+    rows, numbers, matrices, centre_part, east_part, north_part, state, later, halo, even, odd, sems,
 ):
     here = place[0]
     two = pl.ds(2, 2)
     first = pl.ds(0, 2)
+    first_loads = fetch_numbers(here, numbers, own, south, north, beyond, sems.at[pl.ds(3, 4)])
     loads = [
         fetch(sems.at[0], rows.at[first], south.at[first], here == 8, beyond.at[first]),
         fetch(sems.at[1], rows.at[two], own.at[two]),
         fetch(sems.at[2], rows.at[pl.ds(4, 2)], north.at[two], here == 7, beyond.at[two]),
     ]
-    loads += fetch_numbers(here, numbers, own, south, north, beyond, sems.at[pl.ds(3, 4)])
     blocks = fetch_matrices(here, near, far, matrices, sems.at[pl.ds(7, 16)])
-    for load in loads:
-        load.wait()
     stores = [
-        pltpu.make_async_copy(state.at[pl.ds(1, 2)], states_out.at[first], sems.at[0]),
-        pltpu.make_async_copy(later, states_out.at[two], sems.at[1]),
+        pltpu.make_async_copy(state.at[pl.ds(1, 2)], states_out.at[first], sems.at[23]),
+        pltpu.make_async_copy(later, states_out.at[two], sems.at[24]),
+        pltpu.make_async_copy(numbers, numbers_out, sems.at[25]),
+        pltpu.make_async_copy(halo, halo_out, sems.at[26]),
     ]
 
     def stored(row, cut, value):
         later[row, :, cut] = value
-        halo_out[row, :, cut] = value.astype(BF16)
+        halo[row, :, cut] = value.astype(BF16)
 
     two_slots(
-        here, lambda row: rows[row].astype(F32), numbers, column_of(spread_ref), jnp.concatenate([evens[...]] * 4, axis=0), matrices, blocks,
-        (centre_part, east_part, north_part), state, even, odd, stored, stores[0].start,
+        here, lambda row: rows[row].astype(F32), numbers, column_of(spread_ref), even_blocks(), matrices,
+        (first_loads, loads, blocks, stores[2].start), (centre_part, east_part, north_part), state, even, odd, stored,
+        stores[0].start,
     )
+    stores[3].start()
     stores[1].start()
     for store in stores:
         store.wait()
 
 
 def second_kernel(
-    place, own, south, north, beyond, near, far, spread_ref, evens,
-    states, south_mid, north_mid, beyond_mid, cells,
-    final_out, picked_out,
+    place, numbers_in, near, far, spread_ref,
+    states, south_mid, north_mid, beyond_mid, cells, early,
+    final_out, picked_out, both_out,
     mid, sides, numbers, matrices, centre_part, east_part, north_part, state, even, odd, sems,
 ):
     here = place[0]
     first = pl.ds(0, 2)
+    first_loads = [fetch(sems.at[3], numbers, numbers_in)]
     loads = [
         fetch(sems.at[0], mid, states.at[pl.ds(2, 2)]),
         fetch(sems.at[1], sides.at[first], south_mid, here == 8, beyond_mid),
         fetch(sems.at[2], sides.at[pl.ds(2, 2)], north_mid, here == 7, beyond_mid),
     ]
-    loads += fetch_numbers(here, numbers, own, south, north, beyond, sems.at[pl.ds(3, 4)])
     blocks = fetch_matrices(here, near, far, matrices, sems.at[pl.ds(7, 16)])
-    for load in loads:
-        load.wait()
 
     def line(row):
         if 2 <= row < 4:
@@ -227,10 +238,13 @@
         final_out[row, :, cut] = value.astype(BF16)
 
     two_slots(
-        here, line, numbers, column_of(spread_ref), jnp.concatenate([evens[...]] * 4, axis=0), matrices, blocks,
-        (centre_part, east_part, north_part), state, even, odd, stored, first_done,
+        here, line, numbers, column_of(spread_ref), even_blocks(), matrices,
+        (first_loads, loads, blocks, lambda: None), (centre_part, east_part, north_part), state, even, odd, stored,
+        first_done,
     )
     pick(lambda row, cut: mid[row, :, cut], cells[3:4, :], picked_out, 2 * LEV)
+    both_out[: 4 * LEV, :] = early[...].astype(BF16)
+    both_out[4 * LEV :, :] = picked_out[...].astype(BF16)
 
 
 def early_kernel(states, cells, picked_out):
@@ -385,7 +399,6 @@
 
     cells = obs_cells - here * (2 * NX)
     spread = diffusivity.reshape(1, LEV)
-    evens = np.broadcast_to((np.arange(NX) // WIDE % 2 == 0), (16, NX)).astype(BF16)
     fields = [own, south, north, beyond, near, far]
     window = [
         pltpu.VMEM((4, 2, LEV, NX), BF16),
@@ -398,17 +411,17 @@
     masks = [
         pltpu.VMEM((4, LEV, NX), BF16),
         pltpu.VMEM((4, LEV, NX), BF16),
-        pltpu.SemaphoreType.DMA((23,)),
-    ]
-    states, halo = call(
+        pltpu.SemaphoreType.DMA((27,)),
+    ]
+    states, numbers, halo = call(
         first_kernel,
-        (shape(4, LEV, NX), shape(2, LEV, NX, dtype=BF16)),
-        [SMEM] + [ANY] * 6 + [VMEM] * 2,
-        [pltpu.VMEM((6, LEV, NX), BF16), *window, pltpu.VMEM((2, LEV, NX), F32), *masks],
+        (shape(4, LEV, NX), shape(4, 2, LEV, NX, dtype=BF16), shape(2, LEV, NX, dtype=BF16)),
+        [SMEM] + [ANY] * 6 + [VMEM],
+        [pltpu.VMEM((6, LEV, NX), BF16), *window, pltpu.VMEM((2, LEV, NX), F32), pltpu.VMEM((2, LEV, NX), BF16), *masks],
         flops=2_000_000_000,
         limit=56 * 1024 * 1024,
-        out_specs=(ANY, VMEM),
-    )(place, *fields, spread, evens)
+        out_specs=(ANY, ANY, ANY),
+    )(place, *fields, spread)
 
     halfway_mid = lax.ppermute(halo, AXES, apart)
     south_mid = lax.ppermute(halo, "tile", forward)
@@ -416,17 +429,17 @@
     beyond_mid = lax.ppermute(halfway_mid, AXES, across)
     early = call(early_kernel, shape(4 * LEV, LANES), [VMEM] * 2, flops=200_000_000, traffic=2_000_000)(states, cells)
     owned = gathered_from(whole, "member", X_GROUPS).reshape(SLOTS, CH, OBS)
-    final, late = call(
+    final, late, both = call(
         second_kernel,
-        (shape(2, LEV, NX, dtype=BF16), shape(4 * LEV, LANES)),
-        [SMEM] + [ANY] * 6 + [VMEM] * 2 + [ANY] * 4 + [VMEM],
+        (shape(2, LEV, NX, dtype=BF16), shape(4 * LEV, LANES), shape(8 * LEV, LANES, dtype=BF16)),
+        [SMEM] + [ANY] * 3 + [VMEM] + [ANY] * 4 + [VMEM] * 2,
         [pltpu.VMEM((2, LEV, NX), F32), pltpu.VMEM((4, LEV, NX), BF16), *window, *masks],
         flops=2_000_000_000,
         traffic=8_000_000,
         limit=56 * 1024 * 1024,
-    )(place, *fields, spread, evens, states, south_mid, north_mid, beyond_mid, cells)
-
-    both = jnp.concatenate([early, late], axis=0).astype(BF16).reshape(32, 16, LANES)
+    )(place, numbers, near, far, spread, states, south_mid, north_mid, beyond_mid, cells, early)
+
+    both = both.reshape(32, 16, LANES)
     both, owned = lax.optimization_barrier((both, owned))
     members = [list(range(32))]
     parts = lax.all_to_all(both, "member", 0, 0, tiled=True, axis_index_groups=members).reshape(32, 16, LANES)

time: 156 us -> 154 us (0.987)
    unnamed x39 -> x45, local copies, waits for them, and re-layouts: 2.98 us -> 3.8 us
  transfers between devices with their start and end apart: 17 -> 17, of which waited for: 6 -> 6; matrix products, arithmetic and copies ran while one was open for 2% -> 2% of each run, Pallas kernels for 5% -> 6%
where the time goes in v4:
time: 154 us
  starting transfers between devices  54.9 us (36%)
  waiting for transfers between devices  47.6 us (31%)
  blocking collectives  22.5 us (15%)
  Pallas kernels  16.3 us (11%)
  local copies, waits for them, and re-layouts  7.25 us (5%)
  between operations  3.81 us (2%)
    ppermute x3, waiting for transfers between devices, spread_along_z(): lax.ppermute(value, 'member', [(i, i ^ 4 * distance) for i in range(32)])  31.7 us
    all_to_all x1, blocking collectives, local(): lax.all_to_all(both, 'member', 0, 0, tiled=True, axis_index_groups=members)  22.5 us
    all_to_all x1, waiting for transfers between devices, local(): lax.all_to_all(shares, 'member', 0, 0, tiled=True, axis_index_groups=memb...  10.5 us
    ppermute x1, starting transfers between devices, local(): lax.ppermute(lax.dynamic_slice_in_dim(own, jnp.where(here == 8, 0, 2), 4)...  8.63 us
    all_to_all x2, starting transfers between devices, gathered_from(): lax.all_to_all(copies, axis, 0, 0, tiled=True, axis_index_groups=groups)  8.48 us
    pallas_call x1, Pallas kernels, local(): call(second_kernel, (shape(2, LEV, NX, dtype=BF16), shape(4 * LEV, LANES)...  6.63 us
    ppermute x1, starting transfers between devices, local(): north = lax.ppermute(own[:4], 'tile', backward)  6.52 us
    ppermute x3, starting transfers between devices, spread_along_z(): lax.ppermute(value, 'member', [(i, i ^ 4 * distance) for i in range(32)])  6.51 us
  transfers between devices with their start and end apart: 17, of which 6 were waited for; matrix products, arithmetic and copies ran while one was open for 2% of the time, Pallas kernels for 6%

profile of v4, /device:TPU:25, one launch (start us, length us, event | category | flops | bytes accessed | tf_op | source)
XLA Modules:
  0.0 153.6 jit_solution(15840384787414454662)
XLA Ops:
  0.7 1.0 reduce-precision_convert_fusion
  1.8 1.0 copy.24
  3.1 8.6 %collective-permute-start = (bf16[4,64,1280]{2,1,0:T(8,128)(2,1)S(1)}, bf16[4,64,1280]{2,1,0:T(8,128)(2,1)}, u32[]{:S(2)}, u32[]{:S(2)}) collective-permute-start(bf16[4,64,1280]{2,1,0:T(8,128)(2,1)S(1)} %constant_dynamic-slice_fusion), channel_id=1, source_target_pairs={{7,0},{8,9},{23,16},{24,25},{39,32},{40,41},{55,48},{56,57},{71,66... | collective-permute-start | bytes 1966088 | tf_op jit(solution)/shard_map/ppermute | solution.py:377
  11.7 3.5 %all-to-all-start = ((bf16[4,256,256]{2,1,0:T(8,128)(2,1)}), bf16[4,256,256]{2,1,0:T(8,128)(2,1)S(1)}, u32[]{:S(2)}, u32[]{:S(2)}) async-start(bf16[4,256,256]{2,1,0:T(8,128)(2,1)} %bitcast.8), calls=%async_computation | async-start | bytes 1048576 | tf_op jit(solution)/shard_map/all_to_all | solution.py:381
  15.2 4.5 %collective-permute-start.1 = (bf16[128,256]{1,0:T(8,128)(2,1)S(1)}, bf16[128,256]{1,0:T(8,128)(2,1)S(1)}, u32[]{:S(2)}, u32[]{:S(2)}) collective-permute-start(bf16[128,256]{1,0:T(8,128)(2,1)S(1)} %pad_maximum_fusion.1), channel_id=1, source_target_pairs={{0,456},{1,457},{2,458},{3,459},{4,460},{5,461},{6,462},{7,463},{1... | collective-permute-start | bytes 196616 | tf_op jit(solution)/shard_map/ppermute | solution.py:370
  22.3 4.0 %collective-permute-done.1 = bf16[128,256]{1,0:T(8,128)(2,1)S(1)} collective-permute-done((bf16[128,256]{1,0:T(8,128)(2,1)S(1)}, bf16[128,256]{1,0:T(8,128)(2,1)S(1)}, u32[]{:S(2)}, u32[]{:S(2)}) %collective-permute-start.1) | collective-permute-done | bytes 65568 | tf_op jit(solution)/shard_map/ppermute | solution.py:370
  26.3 0.8 broadcast_in_dim.10
  27.1 3.9 %all-to-all-start.1 = ((bf16[4,256,256]{2,1,0:T(8,128)(2,1)}), bf16[4,256,256]{2,1,0:T(8,128)(2,1)S(1)}, u32[]{:S(2)}, u32[]{:S(2)}) async-start(bf16[4,256,256]{2,1,0:T(8,128)(2,1)} %broadcast_in_dim.10), calls=%async_computation.1 | async-start | bytes 1048576 | tf_op jit(solution)/shard_map/all_to_all | solution.py:315
  31.1 2.2 %collective-permute-start.2 = (bf16[256,256]{1,0:T(8,128)(2,1)S(1)}, bf16[256,256]{1,0:T(8,128)(2,1)S(1)}, u32[]{:S(2)}, u32[]{:S(2)}) collective-permute-start(bf16[256,256]{1,0:T(8,128)(2,1)S(1)} %dynamic-slice_bitcast_fusion), channel_id=1, source_target_pairs={{0,64},{16,80},{32,96},{48,112},{64,0},{80,16},{96,32},{112,48},{1... | collective-permute-start | bytes 393224 | tf_op jit(solution)/shard_map/ppermute | solution.py:339
  34.0 1.3 collective-permute-start.6
  35.3 1.8 %collective-permute-done.2 = bf16[256,256]{1,0:T(8,128)(2,1)S(1)} collective-permute-done((bf16[256,256]{1,0:T(8,128)(2,1)S(1)}, bf16[256,256]{1,0:T(8,128)(2,1)S(1)}, u32[]{:S(2)}, u32[]{:S(2)}) %collective-permute-start.2) | collective-permute-done | bytes 131104 | tf_op jit(solution)/shard_map/ppermute | solution.py:339
  37.3 1.3 collective-permute-start.4
  38.6 6.5 %collective-permute-start.5 = (bf16[4,64,1280]{2,1,0:T(8,128)(2,1)S(1)}, bf16[4,64,1280]{2,1,0:T(8,128)(2,1)}, u32[]{:S(2)}, u32[]{:S(2)}) collective-permute-start(bf16[4,64,1280]{2,1,0:T(8,128)(2,1)S(1)} %get-tuple-element.48), channel_id=1, source_target_pairs={{1,0},{2,1},{3,2},{4,3},{5,4},{6,5},{7,6},{9,8},{10,9},{11,10},{12... | collective-permute-start | bytes 1966088 | tf_op jit(solution)/shard_map/ppermute | solution.py:397
  45.1 2.8 %collective-permute-start.7 = (bf16[4,256,256]{2,1,0:T(8,128)(2,1)S(1)}, bf16[4,256,256]{2,1,0:T(8,128)(2,1)S(1)}, u32[]{:S(2)}, u32[]{:S(2)}) collective-permute-start(bf16[4,256,256]{2,1,0:T(8,128)(2,1)S(1)} %all-to-all-done.1.near), channel_id=1, source_target_pairs={{0,1},{1,0},{2,3},{3,2},{4,5},{5,4},{6,7},{7,6},{8,9},{9,8},{10,11... | collective-permute-start | bytes 1572872 | tf_op jit(solution)/shard_map/ppermute | solution.py:398
  47.9 2.4 %collective-permute-start.3 = (bf16[256,256]{1,0:T(8,128)(2,1)S(1)}, bf16[256,256]{1,0:T(8,128)(2,1)S(1)}, u32[]{:S(2)}, u32[]{:S(2)}) collective-permute-start(bf16[256,256]{1,0:T(8,128)(2,1)S(1)} %broadcast_select_fusion.1), channel_id=1, source_target_pairs={{0,128},{16,144},{32,160},{48,176},{64,192},{80,208},{96,224},{112... | collective-permute-start | bytes 393224 | tf_op jit(solution)/shard_map/ppermute | solution.py:339
  50.3 20.6 %collective-permute-done.3 = bf16[256,256]{1,0:T(8,128)(2,1)S(1)} collective-permute-done((bf16[256,256]{1,0:T(8,128)(2,1)S(1)}, bf16[256,256]{1,0:T(8,128)(2,1)S(1)}, u32[]{:S(2)}, u32[]{:S(2)}) %collective-permute-start.3) | collective-permute-done | bytes 131104 | tf_op jit(solution)/shard_map/ppermute | solution.py:339
  72.0 6.0 %shard_map.121 = (f32[4,64,1280]{2,1,0:T(8,128)}, bf16[4,2,64,1280]{3,2,1,0:T(8,128)(2,1)}, bf16[2,64,1280]{2,1,0:T(8,128)(2,1)}) custom-call(s32[1]{0:T(128)} %bitcast.10.place, bf16[6,64,1280]{2,1,0:T(8,128)(2,1)} %copy-done.5, bf16[4,64,1280]{2,1,0:T(8,128)(2,1)} %copy-done.13, bf16[4,64,1280]{2,1,0:T(8,128)(2,1)} %collective-permute-done.5.north, ...), custom_call_target="tpu_custom_call" | custom-call | flops 2000000000 | tf_op jit(solution)/shard_map/pallas_call | solution.py:416
  78.0 1.4 collective-permute-start.10
  79.4 1.9 %collective-permute-start.12 = (bf16[256,256]{1,0:T(8,128)(2,1)S(1)}, bf16[256,256]{1,0:T(8,128)(2,1)S(1)}, u32[]{:S(2)}, u32[]{:S(2)}) collective-permute-start(bf16[256,256]{1,0:T(8,128)(2,1)S(1)} %broadcast_select_fusion.2), channel_id=1, source_target_pairs={{0,256},{16,272},{32,288},{48,304},{64,320},{80,336},{96,352},{112... | collective-permute-start | bytes 393224 | tf_op jit(solution)/shard_map/ppermute | solution.py:339
  81.4 1.3 collective-permute-start.8
  82.7 3.0 %collective-permute-start.9 = (bf16[2,64,1280]{2,1,0:T(8,128)(2,1)}, bf16[2,64,1280]{2,1,0:T(8,128)(2,1)S(1)}, u32[]{:S(2)}, u32[]{:S(2)}) collective-permute-start(bf16[2,64,1280]{2,1,0:T(8,128)(2,1)} %get-tuple-element.38), channel_id=1, source_target_pairs={{1,0},{2,1},{3,2},{4,3},{5,4},{6,5},{7,6},{9,8},{10,9},{11,10},{12... | collective-permute-start | bytes 983048 | tf_op jit(solution)/shard_map/ppermute | solution.py:428
  85.7 1.3 collective-permute-start.11
  87.0 9.3 %collective-permute-done.12 = bf16[256,256]{1,0:T(8,128)(2,1)S(1)} collective-permute-done((bf16[256,256]{1,0:T(8,128)(2,1)S(1)}, bf16[256,256]{1,0:T(8,128)(2,1)S(1)}, u32[]{:S(2)}, u32[]{:S(2)}) %collective-permute-start.12) | collective-permute-done | bytes 131104 | tf_op jit(solution)/shard_map/ppermute | solution.py:339
  97.2 4.5 %all-to-all-start.2 = ((bf16[4,256,256]{2,1,0:T(8,128)(2,1)}), bf16[4,256,256]{2,1,0:T(8,128)(2,1)S(1)}, u32[]{:S(2)}, u32[]{:S(2)}) async-start(bf16[4,256,256]{2,1,0:T(8,128)(2,1)} %broadcast_in_dim.23), calls=%async_computation.2 | async-start | bytes 1048576 | tf_op jit(solution)/shard_map/all_to_all | solution.py:315
  103.0 1.4 collective-permute-done.11.beyond_mid
  105.1 6.6 %shard_map.123 = (bf16[2,64,1280]{2,1,0:T(8,128)(2,1)}, f32[256,128]{1,0:T(8,128)}, bf16[512,128]{1,0:T(8,128)(2,1)}) custom-call(s32[1]{0:T(128)} %bitcast.10.place, bf16[4,2,64,1280]{3,2,1,0:T(8,128)(2,1)} %get-tuple-element.36.numbers_in, bf16[4,256,256]{2,1,0:T(8,128)(2,1)} %copy-done.6, bf16[4,256,256]{2,1,0:T(8,128)(2,1)} %copy-done.14, ...), custom_call_target="tpu_custom_call" | custom-call | flops 2000000000 | bytes 8000000 | tf_op jit(solution)/shard_map/pallas_call | solution.py:432
  111.8 22.5 %all_to_all.25.parts = bf16[32,16,128]{2,1,0:T(8,128)(2,1)S(1)} all-to-all(bf16[32,16,128]{2,1,0:T(8,128)(2,1)} %bitcast.43), channel_id=1, replica_groups={{0,16,32,48,64,80,96,112,128,144,160,176,192,208,224,240,256,272,288,30..., dimensions={0} | all-to-all | bytes 262144 | tf_op jit(solution)/shard_map/all_to_all | solution.py:445
  135.0 4.3 %all-to-all-start.4 = ((bf16[32,16,128]{2,1,0:T(8,128)(2,1)}), bf16[32,16,128]{2,1,0:T(8,128)(2,1)S(1)}, u32[]{:S(2)}, u32[]{:S(2)}) async-start(bf16[32,16,128]{2,1,0:T(8,128)(2,1)} %shard_map.125), calls=%async_computation.4 | async-start | bytes 262144 | tf_op jit(solution)/shard_map/all_to_all | solution.py:447
  139.6 1.1 copy.19
  140.7 1.3 shard_map.124
  142.0 10.5 %all-to-all-done.4 = bf16[32,16,128]{2,1,0:T(8,128)(2,1)S(1)} async-done(((bf16[32,16,128]{2,1,0:T(8,128)(2,1)}), bf16[32,16,128]{2,1,0:T(8,128)(2,1)S(1)}, u32[]{:S(2)}, u32[]{:S(2)}) %all-to-all-start.4) | async-done | bytes 131104 | tf_op jit(solution)/shard_map/all_to_all | solution.py:447
  152.5 1.1 shard_map.126
  (71 shorter events, 5.8 us)
Async XLA Ops:
  0.6 2.2 %copy-start.8 = (bf16[1,64,2,1280]{3,2,1,0:T(2,128)(2,1)S(1)}, bf16[1,64,2,1280]{3,2,1,0:T(2,128)(2,1)}, u32[]{:S(2)}) copy-start(bf16[1,64,2,1280]{3,2,1,0:T(2,128)(2,1)} %param.10) | copy-start | bytes 983044
  0.6 2.2 %copy-start.7 = (bf16[64,2,1280]{2,1,0:T(2,128)(2,1)S(1)}, bf16[64,2,1280]{2,1,0:T(2,128)(2,1)}, u32[]{:S(2)}) copy-start(bf16[64,2,1280]{2,1,0:T(2,128)(2,1)} %param.12) | copy-start | bytes 983044
  2.9 16.8 %copy-start.18 = (s32[4]{0:T(128)S(1)}, s32[4]{0:T(128)}, u32[]{:S(2)}) copy-start(s32[4]{0:T(128)} %param.17) | copy-start | bytes 52
  3.0 34.2 %copy-start.5 = (bf16[6,64,1280]{2,1,0:T(8,128)(2,1)}, bf16[6,64,1280]{2,1,0:T(8,128)(2,1)S(1)}, u32[]{:S(2)}) copy-start(bf16[6,64,1280]{2,1,0:T(8,128)(2,1)S(1)} %slice_dynamic-update-slice_fusion.own) | copy-start | bytes 2949124
  3.1 23.2 %collective-permute-start = (bf16[4,64,1280]{2,1,0:T(8,128)(2,1)S(1)}, bf16[4,64,1280]{2,1,0:T(8,128)(2,1)}, u32[]{:S(2)}, u32[]{:S(2)}) collective-permute-start(bf16[4,64,1280]{2,1,0:T(8,128)(2,1)S(1)} %constant_dynamic-slice_fusion), channel_id=1, source_target_pairs={{7,0},{8,9},{23,16},{24,25},{39,32},{40,41},{55,48},{56,57},{71,66... | collective-permute-start | bytes 1966088 | tf_op jit(solution)/shard_map/ppermute | solution.py:377
  11.7 14.6 %all-to-all-start = ((bf16[4,256,256]{2,1,0:T(8,128)(2,1)}), bf16[4,256,256]{2,1,0:T(8,128)(2,1)S(1)}, u32[]{:S(2)}, u32[]{:S(2)}) async-start(bf16[4,256,256]{2,1,0:T(8,128)(2,1)} %bitcast.8), calls=%async_computation | async-start | bytes 1048576 | tf_op jit(solution)/shard_map/all_to_all | solution.py:381
  15.2 11.1 %collective-permute-start.1 = (bf16[128,256]{1,0:T(8,128)(2,1)S(1)}, bf16[128,256]{1,0:T(8,128)(2,1)S(1)}, u32[]{:S(2)}, u32[]{:S(2)}) collective-permute-start(bf16[128,256]{1,0:T(8,128)(2,1)S(1)} %pad_maximum_fusion.1), channel_id=1, source_target_pairs={{0,456},{1,457},{2,458},{3,459},{4,460},{5,461},{6,462},{7,463},{1... | collective-permute-start | bytes 196616 | tf_op jit(solution)/shard_map/ppermute | solution.py:370
  27.1 10.0 %all-to-all-start.1 = ((bf16[4,256,256]{2,1,0:T(8,128)(2,1)}), bf16[4,256,256]{2,1,0:T(8,128)(2,1)S(1)}, u32[]{:S(2)}, u32[]{:S(2)}) async-start(bf16[4,256,256]{2,1,0:T(8,128)(2,1)} %broadcast_in_dim.10), calls=%async_computation.1 | async-start | bytes 1048576 | tf_op jit(solution)/shard_map/all_to_all | solution.py:315
  31.1 6.0 %collective-permute-start.2 = (bf16[256,256]{1,0:T(8,128)(2,1)S(1)}, bf16[256,256]{1,0:T(8,128)(2,1)S(1)}, u32[]{:S(2)}, u32[]{:S(2)}) collective-permute-start(bf16[256,256]{1,0:T(8,128)(2,1)S(1)} %dynamic-slice_bitcast_fusion), channel_id=1, source_target_pairs={{0,64},{16,80},{32,96},{48,112},{64,0},{80,16},{96,32},{112,48},{1... | collective-permute-start | bytes 393224 | tf_op jit(solution)/shard_map/ppermute | solution.py:339
  34.0 36.9 %collective-permute-start.6 = (bf16[4,64,1280]{2,1,0:T(8,128)(2,1)}, bf16[4,64,1280]{2,1,0:T(8,128)(2,1)}, u32[]{:S(2)}, u32[]{:S(2)}) collective-permute-start(bf16[4,64,1280]{2,1,0:T(8,128)(2,1)} %collective-permute-done), channel_id=1, source_target_pairs={{0,8},{9,7},{16,24},{25,23},{32,40},{41,39},{48,56},{57,55},{66,72... | collective-permute-start | bytes 1966088 | tf_op jit(solution)/shard_map/ppermute | solution.py:384
  37.2 7.9 %copy-start.6 = (bf16[4,256,256]{2,1,0:T(8,128)(2,1)}, bf16[4,256,256]{2,1,0:T(8,128)(2,1)S(1)}, u32[]{:S(2)}) copy-start(bf16[4,256,256]{2,1,0:T(8,128)(2,1)S(1)} %all-to-all-done.1.near) | copy-start | bytes 1572868
  37.3 33.7 %collective-permute-start.4 = (bf16[4,64,1280]{2,1,0:T(8,128)(2,1)S(1)}, bf16[4,64,1280]{2,1,0:T(8,128)(2,1)S(1)}, u32[]{:S(2)}, u32[]{:S(2)}) collective-permute-start(bf16[4,64,1280]{2,1,0:T(8,128)(2,1)S(1)} %get-tuple-element.49), channel_id=1, source_target_pairs={{0,1},{1,2},{2,3},{3,4},{4,5},{5,6},{6,7},{8,9},{9,10},{10,11},{11... | collective-permute-start | bytes 1966088 | tf_op jit(solution)/shard_map/ppermute | solution.py:396
  38.6 32.4 %collective-permute-start.5 = (bf16[4,64,1280]{2,1,0:T(8,128)(2,1)S(1)}, bf16[4,64,1280]{2,1,0:T(8,128)(2,1)}, u32[]{:S(2)}, u32[]{:S(2)}) collective-permute-start(bf16[4,64,1280]{2,1,0:T(8,128)(2,1)S(1)} %get-tuple-element.48), channel_id=1, source_target_pairs={{1,0},{2,1},{3,2},{4,3},{5,4},{6,5},{7,6},{9,8},{10,9},{11,10},{12... | collective-permute-start | bytes 1966088 | tf_op jit(solution)/shard_map/ppermute | solution.py:397
  45.1 25.8 %collective-permute-start.7 = (bf16[4,256,256]{2,1,0:T(8,128)(2,1)S(1)}, bf16[4,256,256]{2,1,0:T(8,128)(2,1)S(1)}, u32[]{:S(2)}, u32[]{:S(2)}) collective-permute-start(bf16[4,256,256]{2,1,0:T(8,128)(2,1)S(1)} %all-to-all-done.1.near), channel_id=1, source_target_pairs={{0,1},{1,0},{2,3},{3,2},{4,5},{5,4},{6,7},{7,6},{8,9},{9,8},{10,11... | collective-permute-start | bytes 1572872 | tf_op jit(solution)/shard_map/ppermute | solution.py:398
  47.9 23.0 %collective-permute-start.3 = (bf16[256,256]{1,0:T(8,128)(2,1)S(1)}, bf16[256,256]{1,0:T(8,128)(2,1)S(1)}, u32[]{:S(2)}, u32[]{:S(2)}) collective-permute-start(bf16[256,256]{1,0:T(8,128)(2,1)S(1)} %broadcast_select_fusion.1), channel_id=1, source_target_pairs={{0,128},{16,144},{32,160},{48,176},{64,192},{80,208},{96,224},{112... | collective-permute-start | bytes 393224 | tf_op jit(solution)/shard_map/ppermute | solution.py:339
  78.0 23.8 %copy-start.12 = (s32[4,256]{1,0:T(4,128)S(1)}, s32[4,256]{1,0:T(4,128)}, u32[]{:S(2)}) copy-start(s32[4,256]{1,0:T(4,128)} %param.16) | copy-start | bytes 12292
  78.0 23.8 %copy-start = (f32[4,64,1280]{2,1,0:T(8,128)S(1)}, f32[4,64,1280]{2,1,0:T(8,128)}, u32[]{:S(2)}) copy-start(f32[4,64,1280]{2,1,0:T(8,128)} %get-tuple-element.37.states) | copy-start | bytes 3932164
  78.0 7.7 %collective-permute-start.10 = (bf16[2,64,1280]{2,1,0:T(8,128)(2,1)}, bf16[2,64,1280]{2,1,0:T(8,128)(2,1)S(1)}, u32[]{:S(2)}, u32[]{:S(2)}) collective-permute-start(bf16[2,64,1280]{2,1,0:T(8,128)(2,1)} %get-tuple-element.38), channel_id=1, source_target_pairs={{7,0},{8,9},{23,16},{24,25},{39,32},{40,41},{55,48},{56,57},{71,66... | collective-permute-start | bytes 983048 | tf_op jit(solution)/shard_map/ppermute | solution.py:426
  79.4 16.9 %collective-permute-start.12 = (bf16[256,256]{1,0:T(8,128)(2,1)S(1)}, bf16[256,256]{1,0:T(8,128)(2,1)S(1)}, u32[]{:S(2)}, u32[]{:S(2)}) collective-permute-start(bf16[256,256]{1,0:T(8,128)(2,1)S(1)} %broadcast_select_fusion.2), channel_id=1, source_target_pairs={{0,256},{16,272},{32,288},{48,304},{64,320},{80,336},{96,352},{112... | collective-permute-start | bytes 393224 | tf_op jit(solution)/shard_map/ppermute | solution.py:339
  81.4 21.6 %collective-permute-start.8 = (bf16[2,64,1280]{2,1,0:T(8,128)(2,1)}, bf16[2,64,1280]{2,1,0:T(8,128)(2,1)S(1)}, u32[]{:S(2)}, u32[]{:S(2)}) collective-permute-start(bf16[2,64,1280]{2,1,0:T(8,128)(2,1)} %get-tuple-element.38), channel_id=1, source_target_pairs={{0,1},{1,2},{2,3},{3,4},{4,5},{5,6},{6,7},{8,9},{9,10},{10,11},{11... | collective-permute-start | bytes 983048 | tf_op jit(solution)/shard_map/ppermute | solution.py:427
  82.7 20.3 %collective-permute-start.9 = (bf16[2,64,1280]{2,1,0:T(8,128)(2,1)}, bf16[2,64,1280]{2,1,0:T(8,128)(2,1)S(1)}, u32[]{:S(2)}, u32[]{:S(2)}) collective-permute-start(bf16[2,64,1280]{2,1,0:T(8,128)(2,1)} %get-tuple-element.38), channel_id=1, source_target_pairs={{1,0},{2,1},{3,2},{4,3},{5,4},{6,5},{7,6},{9,8},{10,9},{11,10},{12... | collective-permute-start | bytes 983048 | tf_op jit(solution)/shard_map/ppermute | solution.py:428
  85.7 18.6 %collective-permute-start.11 = (bf16[2,64,1280]{2,1,0:T(8,128)(2,1)S(1)}, bf16[2,64,1280]{2,1,0:T(8,128)(2,1)S(1)}, u32[]{:S(2)}, u32[]{:S(2)}) collective-permute-start(bf16[2,64,1280]{2,1,0:T(8,128)(2,1)S(1)} %collective-permute-done.10), channel_id=1, source_target_pairs={{0,8},{9,7},{16,24},{25,23},{32,40},{41,39},{48,56},{57,55},{66,72... | collective-permute-start | bytes 983048 | tf_op jit(solution)/shard_map/ppermute | solution.py:429
  97.2 14.6 %all-to-all-start.2 = ((bf16[4,256,256]{2,1,0:T(8,128)(2,1)}), bf16[4,256,256]{2,1,0:T(8,128)(2,1)S(1)}, u32[]{:S(2)}, u32[]{:S(2)}) async-start(bf16[4,256,256]{2,1,0:T(8,128)(2,1)} %broadcast_in_dim.23), calls=%async_computation.2 | async-start | bytes 1048576 | tf_op jit(solution)/shard_map/all_to_all | solution.py:315
  101.7 2.6 %copy-start.4 = (s32[4,256]{1,0:T(4,128)}, s32[4,256]{1,0:T(4,128)S(1)}, u32[]{:S(2)}) copy-start(s32[4,256]{1,0:T(4,128)S(1)} %broadcast_subtract_fusion.cells) | copy-start | bytes 12292
  103.0 1.4 copy-start.15
  103.0 1.4 copy-start.16
  105.1 34.2 %copy-start.10 = (f32[256,64]{0,1:T(8,128)S(1)}, f32[256,64]{0,1:T(8,128)}, u32[]{:S(2)}) copy-start(f32[256,64]{0,1:T(8,128)} %param.15) | copy-start | bytes 196612
  105.1 34.4 %copy-start.11 = (s32[4,256]{1,0:T(4,128)S(1)}, s32[4,256]{1,0:T(4,128)}, u32[]{:S(2)}) copy-start(s32[4,256]{1,0:T(4,128)} %param.18) | copy-start | bytes 12292
  111.7 27.9 %copy-start.9 = (bf16[2,64,1280]{2,1,0:T(8,128)(2,1)S(1)}, bf16[2,64,1280]{2,1,0:T(8,128)(2,1)}, u32[]{:S(2)}) copy-start(bf16[2,64,1280]{2,1,0:T(8,128)(2,1)} %get-tuple-element.39) | copy-start | bytes 983044
  111.7 28.9 %copy-start.2 = (f32[256,128]{1,0:T(8,128)S(1)}, f32[256,128]{1,0:T(8,128)}, u32[]{:S(2)}) copy-start(f32[256,128]{1,0:T(8,128)} %copy-done.1) | copy-start | bytes 393220
  111.8 28.9 %copy-start.3 = (f32[256,128]{1,0:T(8,128)S(1)}, f32[256,128]{1,0:T(8,128)}, u32[]{:S(2)}) copy-start(f32[256,128]{1,0:T(8,128)} %get-tuple-element.40.late) | copy-start | bytes 393220
  135.0 17.5 %all-to-all-start.4 = ((bf16[32,16,128]{2,1,0:T(8,128)(2,1)}), bf16[32,16,128]{2,1,0:T(8,128)(2,1)S(1)}, u32[]{:S(2)}, u32[]{:S(2)}) async-start(bf16[32,16,128]{2,1,0:T(8,128)(2,1)} %shard_map.125), calls=%async_computation.4 | async-start | bytes 262144 | tf_op jit(solution)/shard_map/all_to_all | solution.py:447
  (4 other events, 3.2 us)

commit v5 on v4

--- a/solution.py
+++ b/solution.py
@@ -1,3 +1,5 @@
+import functools
+
 import jax
 import jax.numpy as jnp
 from jax import lax
@@ -300,13 +302,13 @@
     return jax.ShapeDtypeStruct(sizes, dtype)
 
 
-def share_kernel(parts, out_ref):
+def share_kernel(scale, parts, out_ref):
     total = parts[0].astype(F32)
-    for member in range(1, 32):
-        total = total + parts[member].astype(F32)
-    share = (total * (1.0 / 32.0)).astype(BF16)
-    for member in range(32):
-        out_ref[member] = share
+    for part in range(1, parts.shape[0]):
+        total = total + parts[part].astype(F32)
+    share = (total * scale).astype(BF16)
+    for copy in range(out_ref.shape[0]):
+        out_ref[copy] = share
 
 
 def gathered_from(value, axis, groups):
@@ -439,12 +441,23 @@
         limit=56 * 1024 * 1024,
     )(place, numbers, near, far, spread, states, south_mid, north_mid, beyond_mid, cells, early)
 
-    both = both.reshape(32, 16, LANES)
+    eights = [list(range(8 * i, 8 * i + 8)) for i in range(4)]
+    fours = [[8 * i + j for i in range(4)] for j in range(8)]
     both, owned = lax.optimization_barrier((both, owned))
-    members = [list(range(32))]
-    parts = lax.all_to_all(both, "member", 0, 0, tiled=True, axis_index_groups=members).reshape(32, 16, LANES)
-    shares = call(share_kernel, shape(32, 16, LANES, dtype=BF16), [VMEM], flops=70_000, traffic=300_000)(parts)
-    mean = lax.all_to_all(shares, "member", 0, 0, tiled=True, axis_index_groups=members).reshape(8 * LEV, LANES)
+    parts = lax.all_to_all(both.reshape(8, LEV, LANES), "member", 0, 0, tiled=True, axis_index_groups=eights)
+    sums = call(
+        functools.partial(share_kernel, 1.0), shape(4, LEV, LANES, dtype=BF16), [VMEM], flops=70_000, traffic=300_000
+    )(parts)
+    sums = lax.all_to_all(sums, "member", 0, 0, tiled=True, axis_index_groups=fours)
+    shares = call(
+        functools.partial(share_kernel, 1.0 / 32.0),
+        shape(8, LEV, LANES, dtype=BF16),
+        [VMEM],
+        flops=70_000,
+        traffic=300_000,
+    )(sums)
+    mean = lax.all_to_all(shares, "member", 0, 0, tiled=True, axis_index_groups=eights).reshape(8 * LEV, LANES)
+
     innovations = call(
         innovations_kernel, shape(SLOTS, CH, OBS), [VMEM] * 5, flops=130_000_000, traffic=2_000_000
     )(jacobian, early, late, owned, channel_mask.T)

time: 154 us -> 149 us (0.968)
  waiting for transfers between devices: 47.6 us -> 40.3 us
  blocking collectives: 22.5 us -> 25.3 us
    all_to_all x1, waiting for transfers between devices: 10.5 us -> 3.14 us  [local(): lax.all_to_all(shares, 'member', 0, 0, tiled=True, axis_index_groups=eights)]
    all_to_all x1 -> x2, blocking collectives: 22.5 us -> 25.3 us  [the longest x1 13.3 us: local(): lax.all_to_all(both.reshape(8, LEV, LANES), 'member', 0, 0, tiled=True, a...]
where the time goes in v5:
time: 149 us; the launch traced here: 148 us
  starting transfers between devices  54 us (36%)
  waiting for transfers between devices  40.3 us (27%)
  blocking collectives  25.3 us (17%)
  Pallas kernels  16.3 us (11%)
  local copies, waits for them, and re-layouts  7.25 us (5%)
  between operations  3.82 us (3%)
    ppermute x3, waiting for transfers between devices, spread_along_z(): lax.ppermute(value, 'member', [(i, i ^ 4 * distance) for i in range(32)])  31.7 us
    all_to_all x1, blocking collectives, local(): lax.all_to_all(both.reshape(8, LEV, LANES), 'member', 0, 0, tiled=True, a...  13.3 us
    all_to_all x1, blocking collectives, local(): lax.all_to_all(sums, 'member', 0, 0, tiled=True, axis_index_groups=fours)  12 us
    ppermute x1, starting transfers between devices, local(): lax.ppermute(lax.dynamic_slice_in_dim(own, jnp.where(here == 8, 0, 2), 4)...  8.63 us
    all_to_all x2, starting transfers between devices, gathered_from(): lax.all_to_all(copies, axis, 0, 0, tiled=True, axis_index_groups=groups)  8.48 us
    pallas_call x1, Pallas kernels, local(): call(second_kernel, (shape(2, LEV, NX, dtype=BF16), shape(4 * LEV, LANES)...  6.63 us
    ppermute x1, starting transfers between devices, local(): north = lax.ppermute(own[:4], 'tile', backward)  6.52 us
    ppermute x3, starting transfers between devices, spread_along_z(): lax.ppermute(value, 'member', [(i, i ^ 4 * distance) for i in range(32)])  6.51 us
  transfers between devices with their start and end apart: 17, of which 6 were waited for; matrix products, arithmetic and copies ran while one was open for 2% of the time, Pallas kernels for 6%

profile of v5, /device:TPU:25, one launch (start us, length us, event | category | flops | bytes accessed | tf_op | source)
XLA Modules:
  0.0 148.1 jit_solution(1430863915213818558)
XLA Ops:
  0.7 1.0 reduce-precision_convert_fusion
  1.8 1.0 copy.24
  3.1 8.6 %collective-permute-start = (bf16[4,64,1280]{2,1,0:T(8,128)(2,1)S(1)}, bf16[4,64,1280]{2,1,0:T(8,128)(2,1)}, u32[]{:S(2)}, u32[]{:S(2)}) collective-permute-start(bf16[4,64,1280]{2,1,0:T(8,128)(2,1)S(1)} %constant_dynamic-slice_fusion), channel_id=1, source_target_pairs={{7,0},{8,9},{23,16},{24,25},{39,32},{40,41},{55,48},{56,57},{71,66... | collective-permute-start | bytes 1966088 | tf_op jit(solution)/shard_map/ppermute | solution.py:379
  11.7 3.5 %all-to-all-start = ((bf16[4,256,256]{2,1,0:T(8,128)(2,1)}), bf16[4,256,256]{2,1,0:T(8,128)(2,1)S(1)}, u32[]{:S(2)}, u32[]{:S(2)}) async-start(bf16[4,256,256]{2,1,0:T(8,128)(2,1)} %bitcast.8), calls=%async_computation | async-start | bytes 1048576 | tf_op jit(solution)/shard_map/all_to_all | solution.py:383
  15.2 4.5 %collective-permute-start.1 = (bf16[128,256]{1,0:T(8,128)(2,1)S(1)}, bf16[128,256]{1,0:T(8,128)(2,1)S(1)}, u32[]{:S(2)}, u32[]{:S(2)}) collective-permute-start(bf16[128,256]{1,0:T(8,128)(2,1)S(1)} %pad_maximum_fusion.1), channel_id=1, source_target_pairs={{0,456},{1,457},{2,458},{3,459},{4,460},{5,461},{6,462},{7,463},{1... | collective-permute-start | bytes 196616 | tf_op jit(solution)/shard_map/ppermute | solution.py:372
  22.3 4.0 %collective-permute-done.1 = bf16[128,256]{1,0:T(8,128)(2,1)S(1)} collective-permute-done((bf16[128,256]{1,0:T(8,128)(2,1)S(1)}, bf16[128,256]{1,0:T(8,128)(2,1)S(1)}, u32[]{:S(2)}, u32[]{:S(2)}) %collective-permute-start.1) | collective-permute-done | bytes 65568 | tf_op jit(solution)/shard_map/ppermute | solution.py:372
  27.1 3.9 %all-to-all-start.1 = ((bf16[4,256,256]{2,1,0:T(8,128)(2,1)}), bf16[4,256,256]{2,1,0:T(8,128)(2,1)S(1)}, u32[]{:S(2)}, u32[]{:S(2)}) async-start(bf16[4,256,256]{2,1,0:T(8,128)(2,1)} %broadcast_in_dim.10), calls=%async_computation.1 | async-start | bytes 1048576 | tf_op jit(solution)/shard_map/all_to_all | solution.py:317
  31.1 2.2 %collective-permute-start.2 = (bf16[256,256]{1,0:T(8,128)(2,1)S(1)}, bf16[256,256]{1,0:T(8,128)(2,1)S(1)}, u32[]{:S(2)}, u32[]{:S(2)}) collective-permute-start(bf16[256,256]{1,0:T(8,128)(2,1)S(1)} %dynamic-slice_bitcast_fusion), channel_id=1, source_target_pairs={{0,64},{16,80},{32,96},{48,112},{64,0},{80,16},{96,32},{112,48},{1... | collective-permute-start | bytes 393224 | tf_op jit(solution)/shard_map/ppermute | solution.py:341
  34.0 1.3 collective-permute-start.6
  35.3 1.8 %collective-permute-done.2 = bf16[256,256]{1,0:T(8,128)(2,1)S(1)} collective-permute-done((bf16[256,256]{1,0:T(8,128)(2,1)S(1)}, bf16[256,256]{1,0:T(8,128)(2,1)S(1)}, u32[]{:S(2)}, u32[]{:S(2)}) %collective-permute-start.2) | collective-permute-done | bytes 131104 | tf_op jit(solution)/shard_map/ppermute | solution.py:341
  37.3 1.3 collective-permute-start.4
  38.6 6.5 %collective-permute-start.5 = (bf16[4,64,1280]{2,1,0:T(8,128)(2,1)S(1)}, bf16[4,64,1280]{2,1,0:T(8,128)(2,1)}, u32[]{:S(2)}, u32[]{:S(2)}) collective-permute-start(bf16[4,64,1280]{2,1,0:T(8,128)(2,1)S(1)} %get-tuple-element.48), channel_id=1, source_target_pairs={{1,0},{2,1},{3,2},{4,3},{5,4},{6,5},{7,6},{9,8},{10,9},{11,10},{12... | collective-permute-start | bytes 1966088 | tf_op jit(solution)/shard_map/ppermute | solution.py:399
  45.1 2.8 %collective-permute-start.7 = (bf16[4,256,256]{2,1,0:T(8,128)(2,1)S(1)}, bf16[4,256,256]{2,1,0:T(8,128)(2,1)S(1)}, u32[]{:S(2)}, u32[]{:S(2)}) collective-permute-start(bf16[4,256,256]{2,1,0:T(8,128)(2,1)S(1)} %all-to-all-done.1.near), channel_id=1, source_target_pairs={{0,1},{1,0},{2,3},{3,2},{4,5},{5,4},{6,7},{7,6},{8,9},{9,8},{10,11... | collective-permute-start | bytes 1572872 | tf_op jit(solution)/shard_map/ppermute | solution.py:400
  47.9 2.4 %collective-permute-start.3 = (bf16[256,256]{1,0:T(8,128)(2,1)S(1)}, bf16[256,256]{1,0:T(8,128)(2,1)S(1)}, u32[]{:S(2)}, u32[]{:S(2)}) collective-permute-start(bf16[256,256]{1,0:T(8,128)(2,1)S(1)} %broadcast_select_fusion.1), channel_id=1, source_target_pairs={{0,128},{16,144},{32,160},{48,176},{64,192},{80,208},{96,224},{112... | collective-permute-start | bytes 393224 | tf_op jit(solution)/shard_map/ppermute | solution.py:341
  50.3 20.6 %collective-permute-done.3 = bf16[256,256]{1,0:T(8,128)(2,1)S(1)} collective-permute-done((bf16[256,256]{1,0:T(8,128)(2,1)S(1)}, bf16[256,256]{1,0:T(8,128)(2,1)S(1)}, u32[]{:S(2)}, u32[]{:S(2)}) %collective-permute-start.3) | collective-permute-done | bytes 131104 | tf_op jit(solution)/shard_map/ppermute | solution.py:341
  72.0 6.0 %shard_map.121 = (f32[4,64,1280]{2,1,0:T(8,128)}, bf16[4,2,64,1280]{3,2,1,0:T(8,128)(2,1)}, bf16[2,64,1280]{2,1,0:T(8,128)(2,1)}) custom-call(s32[1]{0:T(128)} %bitcast.10.place, bf16[6,64,1280]{2,1,0:T(8,128)(2,1)} %copy-done.5, bf16[4,64,1280]{2,1,0:T(8,128)(2,1)} %copy-done.13, bf16[4,64,1280]{2,1,0:T(8,128)(2,1)} %collective-permute-done.5.north, ...), custom_call_target="tpu_custom_call" | custom-call | flops 2000000000 | tf_op jit(solution)/shard_map/pallas_call | solution.py:418
  78.0 1.4 collective-permute-start.10
  79.4 1.9 %collective-permute-start.12 = (bf16[256,256]{1,0:T(8,128)(2,1)S(1)}, bf16[256,256]{1,0:T(8,128)(2,1)S(1)}, u32[]{:S(2)}, u32[]{:S(2)}) collective-permute-start(bf16[256,256]{1,0:T(8,128)(2,1)S(1)} %broadcast_select_fusion.2), channel_id=1, source_target_pairs={{0,256},{16,272},{32,288},{48,304},{64,320},{80,336},{96,352},{112... | collective-permute-start | bytes 393224 | tf_op jit(solution)/shard_map/ppermute | solution.py:341
  81.4 1.3 collective-permute-start.8
  82.7 3.0 %collective-permute-start.9 = (bf16[2,64,1280]{2,1,0:T(8,128)(2,1)}, bf16[2,64,1280]{2,1,0:T(8,128)(2,1)S(1)}, u32[]{:S(2)}, u32[]{:S(2)}) collective-permute-start(bf16[2,64,1280]{2,1,0:T(8,128)(2,1)} %get-tuple-element.38), channel_id=1, source_target_pairs={{1,0},{2,1},{3,2},{4,3},{5,4},{6,5},{7,6},{9,8},{10,9},{11,10},{12... | collective-permute-start | bytes 983048 | tf_op jit(solution)/shard_map/ppermute | solution.py:430
  85.7 1.3 collective-permute-start.11
  87.0 9.3 %collective-permute-done.12 = bf16[256,256]{1,0:T(8,128)(2,1)S(1)} collective-permute-done((bf16[256,256]{1,0:T(8,128)(2,1)S(1)}, bf16[256,256]{1,0:T(8,128)(2,1)S(1)}, u32[]{:S(2)}, u32[]{:S(2)}) %collective-permute-start.12) | collective-permute-done | bytes 131104 | tf_op jit(solution)/shard_map/ppermute | solution.py:341
  97.2 4.5 %all-to-all-start.2 = ((bf16[4,256,256]{2,1,0:T(8,128)(2,1)}), bf16[4,256,256]{2,1,0:T(8,128)(2,1)S(1)}, u32[]{:S(2)}, u32[]{:S(2)}) async-start(bf16[4,256,256]{2,1,0:T(8,128)(2,1)} %broadcast_in_dim.23), calls=%async_computation.2 | async-start | bytes 1048576 | tf_op jit(solution)/shard_map/all_to_all | solution.py:317
  103.0 1.4 collective-permute-done.11.beyond_mid
  105.1 6.6 %shard_map.123 = (bf16[2,64,1280]{2,1,0:T(8,128)(2,1)}, f32[256,128]{1,0:T(8,128)}, bf16[512,128]{1,0:T(8,128)(2,1)}) custom-call(s32[1]{0:T(128)} %bitcast.10.place, bf16[4,2,64,1280]{3,2,1,0:T(8,128)(2,1)} %get-tuple-element.36.numbers_in, bf16[4,256,256]{2,1,0:T(8,128)(2,1)} %copy-done.6, bf16[4,256,256]{2,1,0:T(8,128)(2,1)} %copy-done.14, ...), custom_call_target="tpu_custom_call" | custom-call | flops 2000000000 | bytes 8000000 | tf_op jit(solution)/shard_map/pallas_call | solution.py:434
  111.8 13.3 %all_to_all.30.parts = bf16[8,64,128]{2,1,0:T(8,128)(2,1)S(1)} all-to-all(bf16[8,64,128]{2,1,0:T(8,128)(2,1)} %bitcast.43), channel_id=1, replica_groups={{0,16,32,48,64,80,96,112},{128,144,160,176,192,208,224,240},{256,272,28..., dimensions={0} | all-to-all | bytes 262144 | tf_op jit(solution)/shard_map/all_to_all | solution.py:447
  125.1 12.0 %all_to_all.31.parts = bf16[4,64,128]{2,1,0:T(8,128)(2,1)S(1)} all-to-all(bf16[4,64,128]{2,1,0:T(8,128)(2,1)S(1)} %shard_map.125), channel_id=1, replica_groups={{0,128,256,384},{16,144,272,400},{32,160,288,416},{48,176,304,432},{64,..., dimensions={0} | all-to-all | bytes 131072 | tf_op jit(solution)/shard_map/all_to_all | solution.py:451
  137.8 3.4 %all-to-all-start.5 = ((bf16[8,64,128]{2,1,0:T(8,128)(2,1)}), bf16[8,64,128]{2,1,0:T(8,128)(2,1)S(1)}, u32[]{:S(2)}, u32[]{:S(2)}) async-start(bf16[8,64,128]{2,1,0:T(8,128)(2,1)} %shard_map.126), calls=%async_computation.5 | async-start | bytes 262144 | tf_op jit(solution)/shard_map/all_to_all | solution.py:459
  141.5 1.1 copy.19
  142.5 1.3 shard_map.124
  143.9 3.1 %all-to-all-done.5 = bf16[8,64,128]{2,1,0:T(8,128)(2,1)S(1)} async-done(((bf16[8,64,128]{2,1,0:T(8,128)(2,1)}), bf16[8,64,128]{2,1,0:T(8,128)(2,1)S(1)}, u32[]{:S(2)}, u32[]{:S(2)}) %all-to-all-start.5) | async-done | bytes 131104 | tf_op jit(solution)/shard_map/all_to_all | solution.py:459
  147.0 1.1 shard_map.127
  (73 shorter events, 6.6 us)
Async XLA Ops:
  0.6 2.2 %copy-start.8 = (bf16[1,64,2,1280]{3,2,1,0:T(2,128)(2,1)S(1)}, bf16[1,64,2,1280]{3,2,1,0:T(2,128)(2,1)}, u32[]{:S(2)}) copy-start(bf16[1,64,2,1280]{3,2,1,0:T(2,128)(2,1)} %param.10) | copy-start | bytes 983044
  0.6 2.2 %copy-start.7 = (bf16[64,2,1280]{2,1,0:T(2,128)(2,1)S(1)}, bf16[64,2,1280]{2,1,0:T(2,128)(2,1)}, u32[]{:S(2)}) copy-start(bf16[64,2,1280]{2,1,0:T(2,128)(2,1)} %param.12) | copy-start | bytes 983044
  2.9 16.8 %copy-start.18 = (s32[4]{0:T(128)S(1)}, s32[4]{0:T(128)}, u32[]{:S(2)}) copy-start(s32[4]{0:T(128)} %param.17) | copy-start | bytes 52
  3.0 34.2 %copy-start.5 = (bf16[6,64,1280]{2,1,0:T(8,128)(2,1)}, bf16[6,64,1280]{2,1,0:T(8,128)(2,1)S(1)}, u32[]{:S(2)}) copy-start(bf16[6,64,1280]{2,1,0:T(8,128)(2,1)S(1)} %slice_dynamic-update-slice_fusion.own) | copy-start | bytes 2949124
  3.1 23.2 %collective-permute-start = (bf16[4,64,1280]{2,1,0:T(8,128)(2,1)S(1)}, bf16[4,64,1280]{2,1,0:T(8,128)(2,1)}, u32[]{:S(2)}, u32[]{:S(2)}) collective-permute-start(bf16[4,64,1280]{2,1,0:T(8,128)(2,1)S(1)} %constant_dynamic-slice_fusion), channel_id=1, source_target_pairs={{7,0},{8,9},{23,16},{24,25},{39,32},{40,41},{55,48},{56,57},{71,66... | collective-permute-start | bytes 1966088 | tf_op jit(solution)/shard_map/ppermute | solution.py:379
  11.7 14.6 %all-to-all-start = ((bf16[4,256,256]{2,1,0:T(8,128)(2,1)}), bf16[4,256,256]{2,1,0:T(8,128)(2,1)S(1)}, u32[]{:S(2)}, u32[]{:S(2)}) async-start(bf16[4,256,256]{2,1,0:T(8,128)(2,1)} %bitcast.8), calls=%async_computation | async-start | bytes 1048576 | tf_op jit(solution)/shard_map/all_to_all | solution.py:383
  15.2 11.1 %collective-permute-start.1 = (bf16[128,256]{1,0:T(8,128)(2,1)S(1)}, bf16[128,256]{1,0:T(8,128)(2,1)S(1)}, u32[]{:S(2)}, u32[]{:S(2)}) collective-permute-start(bf16[128,256]{1,0:T(8,128)(2,1)S(1)} %pad_maximum_fusion.1), channel_id=1, source_target_pairs={{0,456},{1,457},{2,458},{3,459},{4,460},{5,461},{6,462},{7,463},{1... | collective-permute-start | bytes 196616 | tf_op jit(solution)/shard_map/ppermute | solution.py:372
  27.1 10.0 %all-to-all-start.1 = ((bf16[4,256,256]{2,1,0:T(8,128)(2,1)}), bf16[4,256,256]{2,1,0:T(8,128)(2,1)S(1)}, u32[]{:S(2)}, u32[]{:S(2)}) async-start(bf16[4,256,256]{2,1,0:T(8,128)(2,1)} %broadcast_in_dim.10), calls=%async_computation.1 | async-start | bytes 1048576 | tf_op jit(solution)/shard_map/all_to_all | solution.py:317
  31.1 6.0 %collective-permute-start.2 = (bf16[256,256]{1,0:T(8,128)(2,1)S(1)}, bf16[256,256]{1,0:T(8,128)(2,1)S(1)}, u32[]{:S(2)}, u32[]{:S(2)}) collective-permute-start(bf16[256,256]{1,0:T(8,128)(2,1)S(1)} %dynamic-slice_bitcast_fusion), channel_id=1, source_target_pairs={{0,64},{16,80},{32,96},{48,112},{64,0},{80,16},{96,32},{112,48},{1... | collective-permute-start | bytes 393224 | tf_op jit(solution)/shard_map/ppermute | solution.py:341
  34.0 36.9 %collective-permute-start.6 = (bf16[4,64,1280]{2,1,0:T(8,128)(2,1)}, bf16[4,64,1280]{2,1,0:T(8,128)(2,1)}, u32[]{:S(2)}, u32[]{:S(2)}) collective-permute-start(bf16[4,64,1280]{2,1,0:T(8,128)(2,1)} %collective-permute-done), channel_id=1, source_target_pairs={{0,8},{9,7},{16,24},{25,23},{32,40},{41,39},{48,56},{57,55},{66,72... | collective-permute-start | bytes 1966088 | tf_op jit(solution)/shard_map/ppermute | solution.py:386
  37.2 7.9 %copy-start.6 = (bf16[4,256,256]{2,1,0:T(8,128)(2,1)}, bf16[4,256,256]{2,1,0:T(8,128)(2,1)S(1)}, u32[]{:S(2)}) copy-start(bf16[4,256,256]{2,1,0:T(8,128)(2,1)S(1)} %all-to-all-done.1.near) | copy-start | bytes 1572868
  37.3 33.7 %collective-permute-start.4 = (bf16[4,64,1280]{2,1,0:T(8,128)(2,1)S(1)}, bf16[4,64,1280]{2,1,0:T(8,128)(2,1)S(1)}, u32[]{:S(2)}, u32[]{:S(2)}) collective-permute-start(bf16[4,64,1280]{2,1,0:T(8,128)(2,1)S(1)} %get-tuple-element.49), channel_id=1, source_target_pairs={{0,1},{1,2},{2,3},{3,4},{4,5},{5,6},{6,7},{8,9},{9,10},{10,11},{11... | collective-permute-start | bytes 1966088 | tf_op jit(solution)/shard_map/ppermute | solution.py:398
  38.6 32.4 %collective-permute-start.5 = (bf16[4,64,1280]{2,1,0:T(8,128)(2,1)S(1)}, bf16[4,64,1280]{2,1,0:T(8,128)(2,1)}, u32[]{:S(2)}, u32[]{:S(2)}) collective-permute-start(bf16[4,64,1280]{2,1,0:T(8,128)(2,1)S(1)} %get-tuple-element.48), channel_id=1, source_target_pairs={{1,0},{2,1},{3,2},{4,3},{5,4},{6,5},{7,6},{9,8},{10,9},{11,10},{12... | collective-permute-start | bytes 1966088 | tf_op jit(solution)/shard_map/ppermute | solution.py:399
  45.1 25.8 %collective-permute-start.7 = (bf16[4,256,256]{2,1,0:T(8,128)(2,1)S(1)}, bf16[4,256,256]{2,1,0:T(8,128)(2,1)S(1)}, u32[]{:S(2)}, u32[]{:S(2)}) collective-permute-start(bf16[4,256,256]{2,1,0:T(8,128)(2,1)S(1)} %all-to-all-done.1.near), channel_id=1, source_target_pairs={{0,1},{1,0},{2,3},{3,2},{4,5},{5,4},{6,7},{7,6},{8,9},{9,8},{10,11... | collective-permute-start | bytes 1572872 | tf_op jit(solution)/shard_map/ppermute | solution.py:400
  47.9 23.0 %collective-permute-start.3 = (bf16[256,256]{1,0:T(8,128)(2,1)S(1)}, bf16[256,256]{1,0:T(8,128)(2,1)S(1)}, u32[]{:S(2)}, u32[]{:S(2)}) collective-permute-start(bf16[256,256]{1,0:T(8,128)(2,1)S(1)} %broadcast_select_fusion.1), channel_id=1, source_target_pairs={{0,128},{16,144},{32,160},{48,176},{64,192},{80,208},{96,224},{112... | collective-permute-start | bytes 393224 | tf_op jit(solution)/shard_map/ppermute | solution.py:341
  78.0 23.8 %copy-start.12 = (s32[4,256]{1,0:T(4,128)S(1)}, s32[4,256]{1,0:T(4,128)}, u32[]{:S(2)}) copy-start(s32[4,256]{1,0:T(4,128)} %param.16) | copy-start | bytes 12292
  78.0 23.8 %copy-start = (f32[4,64,1280]{2,1,0:T(8,128)S(1)}, f32[4,64,1280]{2,1,0:T(8,128)}, u32[]{:S(2)}) copy-start(f32[4,64,1280]{2,1,0:T(8,128)} %get-tuple-element.37.states) | copy-start | bytes 3932164
  78.0 7.7 %collective-permute-start.10 = (bf16[2,64,1280]{2,1,0:T(8,128)(2,1)}, bf16[2,64,1280]{2,1,0:T(8,128)(2,1)S(1)}, u32[]{:S(2)}, u32[]{:S(2)}) collective-permute-start(bf16[2,64,1280]{2,1,0:T(8,128)(2,1)} %get-tuple-element.38), channel_id=1, source_target_pairs={{7,0},{8,9},{23,16},{24,25},{39,32},{40,41},{55,48},{56,57},{71,66... | collective-permute-start | bytes 983048 | tf_op jit(solution)/shard_map/ppermute | solution.py:428
  79.4 16.9 %collective-permute-start.12 = (bf16[256,256]{1,0:T(8,128)(2,1)S(1)}, bf16[256,256]{1,0:T(8,128)(2,1)S(1)}, u32[]{:S(2)}, u32[]{:S(2)}) collective-permute-start(bf16[256,256]{1,0:T(8,128)(2,1)S(1)} %broadcast_select_fusion.2), channel_id=1, source_target_pairs={{0,256},{16,272},{32,288},{48,304},{64,320},{80,336},{96,352},{112... | collective-permute-start | bytes 393224 | tf_op jit(solution)/shard_map/ppermute | solution.py:341
  81.4 21.6 %collective-permute-start.8 = (bf16[2,64,1280]{2,1,0:T(8,128)(2,1)}, bf16[2,64,1280]{2,1,0:T(8,128)(2,1)S(1)}, u32[]{:S(2)}, u32[]{:S(2)}) collective-permute-start(bf16[2,64,1280]{2,1,0:T(8,128)(2,1)} %get-tuple-element.38), channel_id=1, source_target_pairs={{0,1},{1,2},{2,3},{3,4},{4,5},{5,6},{6,7},{8,9},{9,10},{10,11},{11... | collective-permute-start | bytes 983048 | tf_op jit(solution)/shard_map/ppermute | solution.py:429
  82.7 20.3 %collective-permute-start.9 = (bf16[2,64,1280]{2,1,0:T(8,128)(2,1)}, bf16[2,64,1280]{2,1,0:T(8,128)(2,1)S(1)}, u32[]{:S(2)}, u32[]{:S(2)}) collective-permute-start(bf16[2,64,1280]{2,1,0:T(8,128)(2,1)} %get-tuple-element.38), channel_id=1, source_target_pairs={{1,0},{2,1},{3,2},{4,3},{5,4},{6,5},{7,6},{9,8},{10,9},{11,10},{12... | collective-permute-start | bytes 983048 | tf_op jit(solution)/shard_map/ppermute | solution.py:430
  85.7 18.6 %collective-permute-start.11 = (bf16[2,64,1280]{2,1,0:T(8,128)(2,1)S(1)}, bf16[2,64,1280]{2,1,0:T(8,128)(2,1)S(1)}, u32[]{:S(2)}, u32[]{:S(2)}) collective-permute-start(bf16[2,64,1280]{2,1,0:T(8,128)(2,1)S(1)} %collective-permute-done.10), channel_id=1, source_target_pairs={{0,8},{9,7},{16,24},{25,23},{32,40},{41,39},{48,56},{57,55},{66,72... | collective-permute-start | bytes 983048 | tf_op jit(solution)/shard_map/ppermute | solution.py:431
  97.2 14.6 %all-to-all-start.2 = ((bf16[4,256,256]{2,1,0:T(8,128)(2,1)}), bf16[4,256,256]{2,1,0:T(8,128)(2,1)S(1)}, u32[]{:S(2)}, u32[]{:S(2)}) async-start(bf16[4,256,256]{2,1,0:T(8,128)(2,1)} %broadcast_in_dim.23), calls=%async_computation.2 | async-start | bytes 1048576 | tf_op jit(solution)/shard_map/all_to_all | solution.py:317
  101.7 2.6 %copy-start.4 = (s32[4,256]{1,0:T(4,128)}, s32[4,256]{1,0:T(4,128)S(1)}, u32[]{:S(2)}) copy-start(s32[4,256]{1,0:T(4,128)S(1)} %broadcast_subtract_fusion.cells) | copy-start | bytes 12292
  103.0 1.4 copy-start.15
  103.0 1.4 copy-start.16
  105.1 36.1 %copy-start.10 = (f32[256,64]{0,1:T(8,128)S(1)}, f32[256,64]{0,1:T(8,128)}, u32[]{:S(2)}) copy-start(f32[256,64]{0,1:T(8,128)} %param.15) | copy-start | bytes 196612
  105.1 36.2 %copy-start.11 = (s32[4,256]{1,0:T(4,128)S(1)}, s32[4,256]{1,0:T(4,128)}, u32[]{:S(2)}) copy-start(s32[4,256]{1,0:T(4,128)} %param.18) | copy-start | bytes 12292
  111.7 29.7 %copy-start.9 = (bf16[2,64,1280]{2,1,0:T(8,128)(2,1)S(1)}, bf16[2,64,1280]{2,1,0:T(8,128)(2,1)}, u32[]{:S(2)}) copy-start(bf16[2,64,1280]{2,1,0:T(8,128)(2,1)} %get-tuple-element.39) | copy-start | bytes 983044
  111.7 30.8 %copy-start.2 = (f32[256,128]{1,0:T(8,128)S(1)}, f32[256,128]{1,0:T(8,128)}, u32[]{:S(2)}) copy-start(f32[256,128]{1,0:T(8,128)} %copy-done.1) | copy-start | bytes 393220
  111.8 30.8 %copy-start.3 = (f32[256,128]{1,0:T(8,128)S(1)}, f32[256,128]{1,0:T(8,128)}, u32[]{:S(2)}) copy-start(f32[256,128]{1,0:T(8,128)} %get-tuple-element.40.late) | copy-start | bytes 393220
  137.8 9.2 %all-to-all-start.5 = ((bf16[8,64,128]{2,1,0:T(8,128)(2,1)}), bf16[8,64,128]{2,1,0:T(8,128)(2,1)S(1)}, u32[]{:S(2)}, u32[]{:S(2)}) async-start(bf16[8,64,128]{2,1,0:T(8,128)(2,1)} %shard_map.126), calls=%async_computation.5 | async-start | bytes 262144 | tf_op jit(solution)/shard_map/all_to_all | solution.py:459
  (4 other events, 3.2 us)

commit v6 on v5

--- a/solution.py
+++ b/solution.py
@@ -421,7 +421,7 @@
         [SMEM] + [ANY] * 6 + [VMEM],
         [pltpu.VMEM((6, LEV, NX), BF16), *window, pltpu.VMEM((2, LEV, NX), F32), pltpu.VMEM((2, LEV, NX), BF16), *masks],
         flops=2_000_000_000,
-        limit=56 * 1024 * 1024,
+        limit=50 * 1024 * 1024,
         out_specs=(ANY, ANY, ANY),
     )(place, *fields, spread)
 
@@ -438,7 +438,7 @@
         [pltpu.VMEM((2, LEV, NX), F32), pltpu.VMEM((4, LEV, NX), BF16), *window, *masks],
         flops=2_000_000_000,
         traffic=8_000_000,
-        limit=56 * 1024 * 1024,
+        limit=50 * 1024 * 1024,
     )(place, numbers, near, far, spread, states, south_mid, north_mid, beyond_mid, cells, early)
 
     eights = [list(range(8 * i, 8 * i + 8)) for i in range(4)]

time: 149 us -> 149 us (level)
  starting transfers between devices: 54 us -> 60 us
  waiting for transfers between devices: 40.3 us -> 35.1 us
    all_to_all x2, starting transfers between devices: 8.48 us -> 13.1 us  [gathered_from(): lax.all_to_all(copies, axis, 0, 0, tiled=True, axis_index_groups=groups)]
    ppermute x1, waiting for transfers between devices: 4.02 us -> 0.01 us  [local(): other = lax.ppermute(halves, AXES, mirrored)]
    ppermute x3, waiting for transfers between devices: 31.7 us -> 29.3 us  [spread_along_z(): lax.ppermute(value, 'member', [(i, i ^ 4 * distance) for i in range(32)])]
    unnamed x45 -> x29, local copies, waits for them, and re-layouts: 3.8 us -> 1.49 us
  transfers between devices with their start and end apart: 17 -> 17, of which waited for: 6 -> 6; matrix products, arithmetic and copies ran while one was open for 2% -> 4% of each run, Pallas kernels for 6% -> 5%
where the time goes in v6:
time: 149 us; the launch traced here: 148 us
  starting transfers between devices  60 us (40%)
  waiting for transfers between devices  35.1 us (24%)
  blocking collectives  25.3 us (17%)
  Pallas kernels  15 us (10%)
  local copies, waits for them, and re-layouts  6.13 us (4%)
  between operations  3.73 us (3%)
  other arithmetic  2.48 us (2%)
    ppermute x3, waiting for transfers between devices, spread_along_z(): lax.ppermute(value, 'member', [(i, i ^ 4 * distance) for i in range(32)])  29.3 us
    all_to_all x1, blocking collectives, local(): lax.all_to_all(both.reshape(8, LEV, LANES), 'member', 0, 0, tiled=True, a...  14.4 us
    all_to_all x2, starting transfers between devices, gathered_from(): lax.all_to_all(copies, axis, 0, 0, tiled=True, axis_index_groups=groups)  13.1 us
    all_to_all x1, blocking collectives, local(): lax.all_to_all(sums, 'member', 0, 0, tiled=True, axis_index_groups=fours)  10.9 us
    ppermute x1, starting transfers between devices, local(): lax.ppermute(lax.dynamic_slice_in_dim(own, jnp.where(here == 8, 0, 2), 4)...  7.82 us
    ppermute x3, starting transfers between devices, spread_along_z(): lax.ppermute(value, 'member', [(i, i ^ 4 * distance) for i in range(32)])  7.2 us
    pallas_call x1, Pallas kernels, local(): call(first_kernel, (shape(4, LEV, NX), shape(4, 2, LEV, NX, dtype=BF16),...  6.04 us
    ppermute x1, starting transfers between devices, local(): north = lax.ppermute(own[:4], 'tile', backward)  5.84 us
  transfers between devices with their start and end apart: 17, of which 6 were waited for; matrix products, arithmetic and copies ran while one was open for 4% of the time, Pallas kernels for 5%

profile of v6, /device:TPU:25, one launch (start us, length us, event | category | flops | bytes accessed | tf_op | source)
XLA Modules:
  0.0 147.7 jit_solution(9195741606067398273)
XLA Ops:
  1.8 1.0 copy.24
  3.1 7.8 %collective-permute-start = (bf16[4,64,1280]{2,1,0:T(8,128)(2,1)S(1)}, bf16[4,64,1280]{2,1,0:T(8,128)(2,1)S(1)}, u32[]{:S(2)}, u32[]{:S(2)}) collective-permute-start(bf16[4,64,1280]{2,1,0:T(8,128)(2,1)S(1)} %constant_dynamic-slice_fusion), channel_id=1, source_target_pairs={{7,0},{8,9},{23,16},{24,25},{39,32},{40,41},{55,48},{56,57},{71,66... | collective-permute-start | bytes 1966088 | tf_op jit(solution)/shard_map/ppermute | solution.py:379
  10.9 3.5 %all-to-all-start = ((bf16[4,256,256]{2,1,0:T(8,128)(2,1)}), bf16[4,256,256]{2,1,0:T(8,128)(2,1)S(1)}, u32[]{:S(2)}, u32[]{:S(2)}) async-start(bf16[4,256,256]{2,1,0:T(8,128)(2,1)} %bitcast.8), calls=%async_computation | async-start | bytes 1048576 | tf_op jit(solution)/shard_map/all_to_all | solution.py:383
  14.4 4.5 %collective-permute-start.1 = (bf16[128,256]{1,0:T(8,128)(2,1)S(1)}, bf16[128,256]{1,0:T(8,128)(2,1)S(1)}, u32[]{:S(2)}, u32[]{:S(2)}) collective-permute-start(bf16[128,256]{1,0:T(8,128)(2,1)S(1)} %pad_maximum_fusion.1), channel_id=1, source_target_pairs={{0,456},{1,457},{2,458},{3,459},{4,460},{5,461},{6,462},{7,463},{1... | collective-permute-start | bytes 196616 | tf_op jit(solution)/shard_map/ppermute | solution.py:372
  22.6 7.8 %all-to-all-start.1 = ((bf16[4,256,256]{2,1,0:T(8,128)(2,1)}), bf16[4,256,256]{2,1,0:T(8,128)(2,1)S(1)}, u32[]{:S(2)}, u32[]{:S(2)}) async-start(bf16[4,256,256]{2,1,0:T(8,128)(2,1)} %broadcast_in_dim.10), calls=%async_computation.1 | async-start | bytes 1048576 | tf_op jit(solution)/shard_map/all_to_all | solution.py:317
  30.4 2.9 %collective-permute-start.2 = (bf16[256,256]{1,0:T(8,128)(2,1)S(1)}, bf16[256,256]{1,0:T(8,128)(2,1)S(1)}, u32[]{:S(2)}, u32[]{:S(2)}) collective-permute-start(bf16[256,256]{1,0:T(8,128)(2,1)S(1)} %dynamic-slice_bitcast_fusion), channel_id=1, source_target_pairs={{0,64},{16,80},{32,96},{48,112},{64,0},{80,16},{96,32},{112,48},{1... | collective-permute-start | bytes 393224 | tf_op jit(solution)/shard_map/ppermute | solution.py:341
  34.0 1.3 collective-permute-start.6
  35.3 1.1 collective-permute-done.2
  37.1 1.2 fusion.2
  38.3 1.3 collective-permute-start.4
  39.5 5.8 %collective-permute-start.5 = (bf16[4,64,1280]{2,1,0:T(8,128)(2,1)}, bf16[4,64,1280]{2,1,0:T(8,128)(2,1)S(1)}, u32[]{:S(2)}, u32[]{:S(2)}) collective-permute-start(bf16[4,64,1280]{2,1,0:T(8,128)(2,1)} %get-tuple-element.48), channel_id=1, source_target_pairs={{1,0},{2,1},{3,2},{4,3},{5,4},{6,5},{7,6},{9,8},{10,9},{11,10},{12... | collective-permute-start | bytes 1966088 | tf_op jit(solution)/shard_map/ppermute | solution.py:399
  45.4 3.6 %collective-permute-start.7 = (bf16[4,256,256]{2,1,0:T(8,128)(2,1)S(1)}, bf16[4,256,256]{2,1,0:T(8,128)(2,1)S(1)}, u32[]{:S(2)}, u32[]{:S(2)}) collective-permute-start(bf16[4,256,256]{2,1,0:T(8,128)(2,1)S(1)} %all-to-all-done.1.near), channel_id=1, source_target_pairs={{0,1},{1,0},{2,3},{3,2},{4,5},{5,4},{6,7},{7,6},{8,9},{9,8},{10,11... | collective-permute-start | bytes 1572872 | tf_op jit(solution)/shard_map/ppermute | solution.py:400
  49.0 2.3 %collective-permute-start.3 = (bf16[256,256]{1,0:T(8,128)(2,1)}, bf16[256,256]{1,0:T(8,128)(2,1)S(1)}, u32[]{:S(2)}, u32[]{:S(2)}) collective-permute-start(bf16[256,256]{1,0:T(8,128)(2,1)} %broadcast_select_fusion.1), channel_id=1, source_target_pairs={{0,128},{16,144},{32,160},{48,176},{64,192},{80,208},{96,224},{112... | collective-permute-start | bytes 393224 | tf_op jit(solution)/shard_map/ppermute | solution.py:341
  51.4 19.1 %collective-permute-done.3 = bf16[256,256]{1,0:T(8,128)(2,1)S(1)} collective-permute-done((bf16[256,256]{1,0:T(8,128)(2,1)}, bf16[256,256]{1,0:T(8,128)(2,1)S(1)}, u32[]{:S(2)}, u32[]{:S(2)}) %collective-permute-start.3) | collective-permute-done | bytes 131104 | tf_op jit(solution)/shard_map/ppermute | solution.py:341
  71.1 6.0 %shard_map.121 = (f32[4,64,1280]{2,1,0:T(8,128)}, bf16[4,2,64,1280]{3,2,1,0:T(8,128)(2,1)}, bf16[2,64,1280]{2,1,0:T(8,128)(2,1)S(1)}) custom-call(s32[1]{0:T(128)} %bitcast.10.place, bf16[6,64,1280]{2,1,0:T(8,128)(2,1)} %copy-done.3, bf16[4,64,1280]{2,1,0:T(8,128)(2,1)S(1)} %collective-permute-done.4.south, ...), custom_call_target="tpu_custom_call" | custom-call | flops 2000000000 | tf_op jit(solution)/shard_map/pallas_call | solution.py:418
  77.2 2.2 %collective-permute-start.10 = (bf16[2,64,1280]{2,1,0:T(8,128)(2,1)S(1)}, bf16[2,64,1280]{2,1,0:T(8,128)(2,1)}, u32[]{:S(2)}, u32[]{:S(2)}) collective-permute-start(bf16[2,64,1280]{2,1,0:T(8,128)(2,1)S(1)} %get-tuple-element.38), channel_id=1, source_target_pairs={{7,0},{8,9},{23,16},{24,25},{39,32},{40,41},{55,48},{56,57},{71,66... | collective-permute-start | bytes 983048 | tf_op jit(solution)/shard_map/ppermute | solution.py:428
  79.3 1.9 %collective-permute-start.12 = (bf16[256,256]{1,0:T(8,128)(2,1)}, bf16[256,256]{1,0:T(8,128)(2,1)S(1)}, u32[]{:S(2)}, u32[]{:S(2)}) collective-permute-start(bf16[256,256]{1,0:T(8,128)(2,1)} %broadcast_select_fusion.2), channel_id=1, source_target_pairs={{0,256},{16,272},{32,288},{48,304},{64,320},{80,336},{96,352},{112... | collective-permute-start | bytes 393224 | tf_op jit(solution)/shard_map/ppermute | solution.py:341
  81.3 1.3 collective-permute-start.8
  82.6 3.8 %collective-permute-start.9 = (bf16[2,64,1280]{2,1,0:T(8,128)(2,1)S(1)}, bf16[2,64,1280]{2,1,0:T(8,128)(2,1)}, u32[]{:S(2)}, u32[]{:S(2)}) collective-permute-start(bf16[2,64,1280]{2,1,0:T(8,128)(2,1)S(1)} %get-tuple-element.38), channel_id=1, source_target_pairs={{1,0},{2,1},{3,2},{4,3},{5,4},{6,5},{7,6},{9,8},{10,9},{11,10},{12... | collective-permute-start | bytes 983048 | tf_op jit(solution)/shard_map/ppermute | solution.py:430
  86.3 1.3 collective-permute-start.11
  87.6 9.2 %collective-permute-done.12 = bf16[256,256]{1,0:T(8,128)(2,1)S(1)} collective-permute-done((bf16[256,256]{1,0:T(8,128)(2,1)}, bf16[256,256]{1,0:T(8,128)(2,1)S(1)}, u32[]{:S(2)}, u32[]{:S(2)}) %collective-permute-start.12) | collective-permute-done | bytes 131104 | tf_op jit(solution)/shard_map/ppermute | solution.py:341
  97.7 5.3 %all-to-all-start.2 = ((bf16[4,256,256]{2,1,0:T(8,128)(2,1)}), bf16[4,256,256]{2,1,0:T(8,128)(2,1)S(1)}, u32[]{:S(2)}, u32[]{:S(2)}) async-start(bf16[4,256,256]{2,1,0:T(8,128)(2,1)} %broadcast_in_dim.23), calls=%async_computation.2 | async-start | bytes 1048576 | tf_op jit(solution)/shard_map/all_to_all | solution.py:317
  103.6 1.7 %collective-permute-done.11.beyond_mid = bf16[2,64,1280]{2,1,0:T(8,128)(2,1)} collective-permute-done((bf16[2,64,1280]{2,1,0:T(8,128)(2,1)}, bf16[2,64,1280]{2,1,0:T(8,128)(2,1)}, u32[]{:S(2)}, u32[]{:S(2)}) %collective-permute-start.11) | collective-permute-done | bytes 327712 | tf_op jit(solution)/shard_map/ppermute | solution.py:431
  105.3 5.2 %shard_map.123 = (bf16[2,64,1280]{2,1,0:T(8,128)(2,1)S(1)}, f32[256,128]{1,0:T(8,128)S(1)}, bf16[512,128]{1,0:T(8,128)(2,1)S(1)}) custom-call(s32[1]{0:T(128)} %bitcast.10.place, bf16[4,2,64,1280]{3,2,1,0:T(8,128)(2,1)S(1)} %copy-done.2, bf16[4,256,256]{2,1,0:T(8,128)(2,1)S(1)} %all-to-all-done.1.near, bf16[4,256,256]{2,1,0:T(8,128)(2,1)S(1)} %collective-permute-done.7.far, ...), custom_call_target="tpu_custom_call" | custom-call | flops 2000000000 | bytes 8000000 | tf_op jit(solution)/shard_map/pallas_call | solution.py:434
  110.5 1.3 all-to-all-done.2.owned
  111.8 14.4 %all_to_all.30.parts = bf16[8,64,128]{2,1,0:T(8,128)(2,1)S(1)} all-to-all(bf16[8,64,128]{2,1,0:T(8,128)(2,1)S(1)} %bitcast.32), channel_id=1, replica_groups={{0,16,32,48,64,80,96,112},{128,144,160,176,192,208,224,240},{256,272,28..., dimensions={0} | all-to-all | bytes 262144 | tf_op jit(solution)/shard_map/all_to_all | solution.py:447
  126.3 10.9 %all_to_all.31.parts = bf16[4,64,128]{2,1,0:T(8,128)(2,1)S(1)} all-to-all(bf16[4,64,128]{2,1,0:T(8,128)(2,1)S(1)} %shard_map.125), channel_id=1, replica_groups={{0,128,256,384},{16,144,272,400},{32,160,288,416},{48,176,304,432},{64,..., dimensions={0} | all-to-all | bytes 131072 | tf_op jit(solution)/shard_map/all_to_all | solution.py:451
  137.8 3.4 %all-to-all-start.5 = ((bf16[8,64,128]{2,1,0:T(8,128)(2,1)}), bf16[8,64,128]{2,1,0:T(8,128)(2,1)S(1)}, u32[]{:S(2)}, u32[]{:S(2)}) async-start(bf16[8,64,128]{2,1,0:T(8,128)(2,1)} %shard_map.126), calls=%async_computation.5 | async-start | bytes 262144 | tf_op jit(solution)/shard_map/all_to_all | solution.py:459
  141.5 1.1 copy.19
  142.5 1.3 shard_map.124
  143.9 2.7 %all-to-all-done.5 = bf16[8,64,128]{2,1,0:T(8,128)(2,1)S(1)} async-done(((bf16[8,64,128]{2,1,0:T(8,128)(2,1)}), bf16[8,64,128]{2,1,0:T(8,128)(2,1)S(1)}, u32[]{:S(2)}, u32[]{:S(2)}) %all-to-all-start.5) | async-done | bytes 131104 | tf_op jit(solution)/shard_map/all_to_all | solution.py:459
  146.6 1.1 shard_map.127
  (57 shorter events, 6.6 us)
Async XLA Ops:
  0.6 2.2 %copy-start.5 = (bf16[1,64,2,1280]{3,2,1,0:T(2,128)(2,1)S(1)}, bf16[1,64,2,1280]{3,2,1,0:T(2,128)(2,1)}, u32[]{:S(2)}) copy-start(bf16[1,64,2,1280]{3,2,1,0:T(2,128)(2,1)} %param.10) | copy-start | bytes 983044
  0.6 2.2 %copy-start.4 = (bf16[64,2,1280]{2,1,0:T(2,128)(2,1)S(1)}, bf16[64,2,1280]{2,1,0:T(2,128)(2,1)}, u32[]{:S(2)}) copy-start(bf16[64,2,1280]{2,1,0:T(2,128)(2,1)} %param.12) | copy-start | bytes 983044
  2.9 16.0 %copy-start.10 = (s32[4]{0:T(128)S(1)}, s32[4]{0:T(128)}, u32[]{:S(2)}) copy-start(s32[4]{0:T(128)} %param.17) | copy-start | bytes 52
  3.0 34.1 %copy-start.3 = (bf16[6,64,1280]{2,1,0:T(8,128)(2,1)}, bf16[6,64,1280]{2,1,0:T(8,128)(2,1)S(1)}, u32[]{:S(2)}) copy-start(bf16[6,64,1280]{2,1,0:T(8,128)(2,1)S(1)} %slice_dynamic-update-slice_fusion.own) | copy-start | bytes 2949124
  3.1 18.5 %collective-permute-start = (bf16[4,64,1280]{2,1,0:T(8,128)(2,1)S(1)}, bf16[4,64,1280]{2,1,0:T(8,128)(2,1)S(1)}, u32[]{:S(2)}, u32[]{:S(2)}) collective-permute-start(bf16[4,64,1280]{2,1,0:T(8,128)(2,1)S(1)} %constant_dynamic-slice_fusion), channel_id=1, source_target_pairs={{7,0},{8,9},{23,16},{24,25},{39,32},{40,41},{55,48},{56,57},{71,66... | collective-permute-start | bytes 1966088 | tf_op jit(solution)/shard_map/ppermute | solution.py:379
  10.9 10.6 %all-to-all-start = ((bf16[4,256,256]{2,1,0:T(8,128)(2,1)}), bf16[4,256,256]{2,1,0:T(8,128)(2,1)S(1)}, u32[]{:S(2)}, u32[]{:S(2)}) async-start(bf16[4,256,256]{2,1,0:T(8,128)(2,1)} %bitcast.8), calls=%async_computation | async-start | bytes 1048576 | tf_op jit(solution)/shard_map/all_to_all | solution.py:383
  14.4 7.1 %collective-permute-start.1 = (bf16[128,256]{1,0:T(8,128)(2,1)S(1)}, bf16[128,256]{1,0:T(8,128)(2,1)S(1)}, u32[]{:S(2)}, u32[]{:S(2)}) collective-permute-start(bf16[128,256]{1,0:T(8,128)(2,1)S(1)} %pad_maximum_fusion.1), channel_id=1, source_target_pairs={{0,456},{1,457},{2,458},{3,459},{4,460},{5,461},{6,462},{7,463},{1... | collective-permute-start | bytes 196616 | tf_op jit(solution)/shard_map/ppermute | solution.py:372
  21.5 1.0 copy-start.9
  22.6 14.5 %all-to-all-start.1 = ((bf16[4,256,256]{2,1,0:T(8,128)(2,1)}), bf16[4,256,256]{2,1,0:T(8,128)(2,1)S(1)}, u32[]{:S(2)}, u32[]{:S(2)}) async-start(bf16[4,256,256]{2,1,0:T(8,128)(2,1)} %broadcast_in_dim.10), calls=%async_computation.1 | async-start | bytes 1048576 | tf_op jit(solution)/shard_map/all_to_all | solution.py:317
  30.4 6.0 %collective-permute-start.2 = (bf16[256,256]{1,0:T(8,128)(2,1)S(1)}, bf16[256,256]{1,0:T(8,128)(2,1)S(1)}, u32[]{:S(2)}, u32[]{:S(2)}) collective-permute-start(bf16[256,256]{1,0:T(8,128)(2,1)S(1)} %dynamic-slice_bitcast_fusion), channel_id=1, source_target_pairs={{0,64},{16,80},{32,96},{48,112},{64,0},{80,16},{96,32},{112,48},{1... | collective-permute-start | bytes 393224 | tf_op jit(solution)/shard_map/ppermute | solution.py:341
  34.0 37.1 %collective-permute-start.6 = (bf16[4,64,1280]{2,1,0:T(8,128)(2,1)}, bf16[4,64,1280]{2,1,0:T(8,128)(2,1)S(1)}, u32[]{:S(2)}, u32[]{:S(2)}) collective-permute-start(bf16[4,64,1280]{2,1,0:T(8,128)(2,1)} %copy-done.9), channel_id=1, source_target_pairs={{0,8},{9,7},{16,24},{25,23},{32,40},{41,39},{48,56},{57,55},{66,72... | collective-permute-start | bytes 1966088 | tf_op jit(solution)/shard_map/ppermute | solution.py:386
  37.1 34.0 %copy-start.1 = (f32[64]{0:T(128)S(1)}, f32[64]{0:T(128)}, u32[]{:S(2)}) copy-start(f32[64]{0:T(128)} %param.13) | copy-start | bytes 772
  38.3 32.8 %collective-permute-start.4 = (bf16[4,64,1280]{2,1,0:T(8,128)(2,1)}, bf16[4,64,1280]{2,1,0:T(8,128)(2,1)S(1)}, u32[]{:S(2)}, u32[]{:S(2)}) collective-permute-start(bf16[4,64,1280]{2,1,0:T(8,128)(2,1)} %get-tuple-element.49), channel_id=1, source_target_pairs={{0,1},{1,2},{2,3},{3,4},{4,5},{5,6},{6,7},{8,9},{9,10},{10,11},{11... | collective-permute-start | bytes 1966088 | tf_op jit(solution)/shard_map/ppermute | solution.py:398
  39.5 31.6 %collective-permute-start.5 = (bf16[4,64,1280]{2,1,0:T(8,128)(2,1)}, bf16[4,64,1280]{2,1,0:T(8,128)(2,1)S(1)}, u32[]{:S(2)}, u32[]{:S(2)}) collective-permute-start(bf16[4,64,1280]{2,1,0:T(8,128)(2,1)} %get-tuple-element.48), channel_id=1, source_target_pairs={{1,0},{2,1},{3,2},{4,3},{5,4},{6,5},{7,6},{9,8},{10,9},{11,10},{12... | collective-permute-start | bytes 1966088 | tf_op jit(solution)/shard_map/ppermute | solution.py:399
  45.4 25.7 %collective-permute-start.7 = (bf16[4,256,256]{2,1,0:T(8,128)(2,1)S(1)}, bf16[4,256,256]{2,1,0:T(8,128)(2,1)S(1)}, u32[]{:S(2)}, u32[]{:S(2)}) collective-permute-start(bf16[4,256,256]{2,1,0:T(8,128)(2,1)S(1)} %all-to-all-done.1.near), channel_id=1, source_target_pairs={{0,1},{1,0},{2,3},{3,2},{4,5},{5,4},{6,7},{7,6},{8,9},{9,8},{10,11... | collective-permute-start | bytes 1572872 | tf_op jit(solution)/shard_map/ppermute | solution.py:400
  49.0 21.4 %collective-permute-start.3 = (bf16[256,256]{1,0:T(8,128)(2,1)}, bf16[256,256]{1,0:T(8,128)(2,1)S(1)}, u32[]{:S(2)}, u32[]{:S(2)}) collective-permute-start(bf16[256,256]{1,0:T(8,128)(2,1)} %broadcast_select_fusion.1), channel_id=1, source_target_pairs={{0,128},{16,144},{32,160},{48,176},{64,192},{80,208},{96,224},{112... | collective-permute-start | bytes 393224 | tf_op jit(solution)/shard_map/ppermute | solution.py:341
  77.2 25.8 %copy-start.8 = (s32[4,256]{1,0:T(4,128)S(1)}, s32[4,256]{1,0:T(4,128)}, u32[]{:S(2)}) copy-start(s32[4,256]{1,0:T(4,128)} %param.16) | copy-start | bytes 12292
  77.2 25.8 %copy-start = (f32[4,64,1280]{2,1,0:T(8,128)S(1)}, f32[4,64,1280]{2,1,0:T(8,128)}, u32[]{:S(2)}) copy-start(f32[4,64,1280]{2,1,0:T(8,128)} %get-tuple-element.37.states) | copy-start | bytes 3932164
  77.2 9.2 %collective-permute-start.10 = (bf16[2,64,1280]{2,1,0:T(8,128)(2,1)S(1)}, bf16[2,64,1280]{2,1,0:T(8,128)(2,1)}, u32[]{:S(2)}, u32[]{:S(2)}) collective-permute-start(bf16[2,64,1280]{2,1,0:T(8,128)(2,1)S(1)} %get-tuple-element.38), channel_id=1, source_target_pairs={{7,0},{8,9},{23,16},{24,25},{39,32},{40,41},{55,48},{56,57},{71,66... | collective-permute-start | bytes 983048 | tf_op jit(solution)/shard_map/ppermute | solution.py:428
  79.3 17.5 %collective-permute-start.12 = (bf16[256,256]{1,0:T(8,128)(2,1)}, bf16[256,256]{1,0:T(8,128)(2,1)S(1)}, u32[]{:S(2)}, u32[]{:S(2)}) collective-permute-start(bf16[256,256]{1,0:T(8,128)(2,1)} %broadcast_select_fusion.2), channel_id=1, source_target_pairs={{0,256},{16,272},{32,288},{48,304},{64,320},{80,336},{96,352},{112... | collective-permute-start | bytes 393224 | tf_op jit(solution)/shard_map/ppermute | solution.py:341
  81.3 22.3 %collective-permute-start.8 = (bf16[2,64,1280]{2,1,0:T(8,128)(2,1)S(1)}, bf16[2,64,1280]{2,1,0:T(8,128)(2,1)}, u32[]{:S(2)}, u32[]{:S(2)}) collective-permute-start(bf16[2,64,1280]{2,1,0:T(8,128)(2,1)S(1)} %get-tuple-element.38), channel_id=1, source_target_pairs={{0,1},{1,2},{2,3},{3,4},{4,5},{5,6},{6,7},{8,9},{9,10},{10,11},{11... | collective-permute-start | bytes 983048 | tf_op jit(solution)/shard_map/ppermute | solution.py:429
  82.6 21.0 %collective-permute-start.9 = (bf16[2,64,1280]{2,1,0:T(8,128)(2,1)S(1)}, bf16[2,64,1280]{2,1,0:T(8,128)(2,1)}, u32[]{:S(2)}, u32[]{:S(2)}) collective-permute-start(bf16[2,64,1280]{2,1,0:T(8,128)(2,1)S(1)} %get-tuple-element.38), channel_id=1, source_target_pairs={{1,0},{2,1},{3,2},{4,3},{5,4},{6,5},{7,6},{9,8},{10,9},{11,10},{12... | collective-permute-start | bytes 983048 | tf_op jit(solution)/shard_map/ppermute | solution.py:430
  86.3 18.9 %collective-permute-start.11 = (bf16[2,64,1280]{2,1,0:T(8,128)(2,1)}, bf16[2,64,1280]{2,1,0:T(8,128)(2,1)}, u32[]{:S(2)}, u32[]{:S(2)}) collective-permute-start(bf16[2,64,1280]{2,1,0:T(8,128)(2,1)} %collective-permute-done.10), channel_id=1, source_target_pairs={{0,8},{9,7},{16,24},{25,23},{32,40},{41,39},{48,56},{57,55},{66,72... | collective-permute-start | bytes 983048 | tf_op jit(solution)/shard_map/ppermute | solution.py:431
  97.7 14.2 %all-to-all-start.2 = ((bf16[4,256,256]{2,1,0:T(8,128)(2,1)}), bf16[4,256,256]{2,1,0:T(8,128)(2,1)S(1)}, u32[]{:S(2)}, u32[]{:S(2)}) async-start(bf16[4,256,256]{2,1,0:T(8,128)(2,1)} %broadcast_in_dim.23), calls=%async_computation.2 | async-start | bytes 1048576 | tf_op jit(solution)/shard_map/all_to_all | solution.py:317
  103.0 2.3 %copy-start.2 = (bf16[4,2,64,1280]{3,2,1,0:T(8,128)(2,1)S(1)}, bf16[4,2,64,1280]{3,2,1,0:T(8,128)(2,1)}, u32[]{:S(2)}) copy-start(bf16[4,2,64,1280]{3,2,1,0:T(8,128)(2,1)} %get-tuple-element.36.numbers_in) | copy-start | bytes 3932164
  105.3 35.9 %copy-start.6 = (f32[256,64]{0,1:T(8,128)S(1)}, f32[256,64]{0,1:T(8,128)}, u32[]{:S(2)}) copy-start(f32[256,64]{0,1:T(8,128)} %param.15) | copy-start | bytes 196612
  105.3 36.0 %copy-start.7 = (s32[4,256]{1,0:T(4,128)S(1)}, s32[4,256]{1,0:T(4,128)}, u32[]{:S(2)}) copy-start(s32[4,256]{1,0:T(4,128)} %param.18) | copy-start | bytes 12292
  137.8 8.7 %all-to-all-start.5 = ((bf16[8,64,128]{2,1,0:T(8,128)(2,1)}), bf16[8,64,128]{2,1,0:T(8,128)(2,1)S(1)}, u32[]{:S(2)}, u32[]{:S(2)}) async-start(bf16[8,64,128]{2,1,0:T(8,128)(2,1)} %shard_map.126), calls=%async_computation.5 | async-start | bytes 262144 | tf_op jit(solution)/shard_map/all_to_all | solution.py:459
